TPU v7x, 32 devices: a whole 2x2x4 slice. The times are simulated.
32 devices in a mesh: groups: 1, dp: 32 (over z, y, x, core).
Axes of the slice: x: 2, y: 2, z: 4, core: 2. Of those that a mesh axis runs over, the one named last changes fastest.
Arguments:
- learn_hidden: bfloat16 [4096, 1536], P(('groups', 'dp')), may hold values from -6 to 6
- learn_cotangent: bfloat16 [4096, 2048], P(('groups', 'dp')), may hold values from -0.1875 to 0.1875
- master: float32 [192, 128, 128], P('dp'), may hold values from -0.15625 to 0.15625
- moment_first: float32 [192, 128, 128], P('dp'), may hold values from -0.18 to 0.18
- moment_second: float32 [192, 128, 128], P('dp'), may hold values from 0.01 to 0.2
- resident_weight: bfloat16 [24576, 2048], P('dp'), may hold values from -440 to 440
- resident_scale: float32 [192, 16], P('dp'), may hold values from 0.0001 to 0.0006
- placement: int32 [16], replicated, may hold values from 0 to 15, each once
- decode_hidden: bfloat16 [4, 256, 8, 1536], P(None, ('groups', 'dp')), may hold values from -6 to 6
- routing: int32 [4, 256, 8], P(None, ('groups', 'dp')), may hold values from 0 to 15, all different within a row; in each aligned block of 8 rows (0 to 7, 8 to 15, ..., all dimensions but the last counted through in order) at most 6 rows name the same one
- gate_weight: float32 [4, 256, 8], P(None, ('groups', 'dp')), may hold values from 0.05 to 1
Outputs:
- decoded: bfloat16 [4, 256, 2048], P(None, ('groups', 'dp'))
- new_master: float32 [192, 128, 128], P(('groups', 'dp'))
Inputs may be any that keep to these rules, and one draw needn't show every extreme that they name: `routing`: in every decode step, the 8 rows of one device name each expert at most 6 times, a bound that some block reaches; a row names 8 different experts. `placement`: each owner pair serves exactly one expert.
All inputs are finite; a program needn't handle non-finite values.
Results may differ from a plain program's by a relative error of at most 0.009.
Values may be sent and summed in bfloat16 or wider, within the bound.
No kernel may reach another device: no remote copies, remote signals or barrier semaphores. Data moves between devices by JAX's collectives and lax.ppermute only.
A program may use at most 128 MiB of HBM per device.

v0:
```python
from functools import partial

import jax
import jax.numpy as jnp
from jax import lax
from jax.sharding import PartitionSpec as P

learn_rate = 0.05
beta_first = 0.9
beta_second = 0.95
correct_first = 1.0 - 0.9**10
correct_second = 1.0 - 0.95**10
decay_rate = 0.1
adam_epsilon = 1e-08
quant_range = 448.0


def optimizer(gradient, master, moment_first, moment_second):
    first_moment = beta_first * moment_first + (1.0 - beta_first) * gradient
    second_moment = beta_second * moment_second + (1.0 - beta_second) * gradient * gradient
    update = (
        first_moment / correct_first / (jnp.sqrt(second_moment / correct_second) + adam_epsilon)
    )
    return master - learn_rate * (update + decay_rate * master)


def quantize(weights):
    largest = jnp.max(jnp.abs(weights), axis=(1, 2))
    scales = (largest + 1e-06) / quant_range
    quantized = (weights / scales[:, None, None]).astype(jnp.bfloat16)
    return (quantized, scales)


def scaled_partial(input_rows, weights, scales, block_side):
    row_count = input_rows.shape[0]
    columns = weights.shape[1]
    summed = jnp.zeros((row_count, columns // block_side, block_side), jnp.float32)
    for row_block in range(weights.shape[0] // block_side):
        product = jnp.dot(
            input_rows[:, row_block * block_side : (row_block + 1) * block_side],
            weights[row_block * block_side : (row_block + 1) * block_side],
            preferred_element_type=jnp.float32,
        )
        summed = (
            summed
            + product.reshape(row_count, columns // block_side, block_side)
            * scales[row_block][:, None]
        )
    return summed.reshape(row_count, columns).astype(jnp.bfloat16)


def pack_rows(hidden, routed, placement, experts, capacity):
    entries = routed.reshape(-1)
    entry_count = entries.shape[0]
    owner_pair = jnp.sum(
        jnp.where(
            entries[:, None] == jnp.arange(experts, dtype=jnp.int32)[None, :], placement[None, :], 0
        ),
        axis=1,
    )
    same_pair = owner_pair[:, None] == owner_pair[None, :]
    earlier = jnp.arange(entry_count)[None, :] < jnp.arange(entry_count)[:, None]
    position = jnp.sum((same_pair & earlier).astype(jnp.int32), axis=1)
    slot_index = owner_pair * capacity + position
    onehot = (
        jnp.arange(experts * capacity, dtype=jnp.int32)[:, None] == slot_index[None, :]
    ).astype(jnp.bfloat16)
    packed = jnp.dot(
        onehot, hidden.reshape(entry_count, -1), preferred_element_type=jnp.float32
    ).astype(jnp.bfloat16)
    packed = (
        packed.reshape(experts, capacity, 2, -1)
        .transpose(0, 2, 1, 3)
        .reshape(2 * experts, capacity, -1)
    )
    return (packed, slot_index)


def local(
    learn_hidden,
    learn_cotangent,
    master,
    moment_first,
    moment_second,
    resident_weight,
    resident_scale,
    placement,
    decode_hidden,
    routing,
    gate_weight,
):
    block_side = master.shape[1]
    hidden_width = learn_hidden.shape[1]
    columns = learn_cotangent.shape[1]
    row_blocks = hidden_width // block_side
    column_blocks = columns // block_side
    full_gradient = jnp.dot(learn_hidden.T, learn_cotangent, preferred_element_type=jnp.float32)
    full_gradient = (
        full_gradient.reshape(row_blocks, block_side, column_blocks, block_side)
        .transpose(0, 2, 1, 3)
        .reshape(-1, block_side, block_side)
    )
    gradient = lax.psum_scatter(full_gradient, "dp", scatter_dimension=0, tiled=True)
    new_master = optimizer(gradient, master, moment_first, moment_second)
    quantized, scales = quantize(new_master)
    all_blocks, all_scales = (
        lax.all_gather(quantized, "dp", axis=0, tiled=True),
        lax.all_gather(scales.astype(jnp.bfloat16), "dp", axis=0, tiled=True).astype(scales.dtype),
    )
    device = lax.axis_index("dp")
    owner_half = device % 2
    half_blocks = all_blocks.shape[0] // 2
    fresh_piece = lax.dynamic_slice_in_dim(all_blocks, owner_half * half_blocks, half_blocks, 0)
    fresh_piece = (
        fresh_piece.reshape(row_blocks // 2, column_blocks, block_side, block_side)
        .transpose(0, 2, 1, 3)
        .reshape(hidden_width // 2, columns)
    )
    fresh_scale = lax.dynamic_slice_in_dim(
        all_scales, owner_half * half_blocks, half_blocks, 0
    ).reshape(row_blocks // 2, column_blocks)
    is_trained = placement[0] == device // 2
    weights = jnp.where(is_trained, fresh_piece, resident_weight)
    scale_table = jnp.where(is_trained, fresh_scale, resident_scale)
    experts = lax.axis_size("dp") // 2
    step_rows = decode_hidden.shape[1]
    topk_count = decode_hidden.shape[2]
    capacity = min(step_rows, step_rows * topk_count // experts + 2)
    packer = jax.vmap(partial(pack_rows, placement=placement, experts=experts, capacity=capacity))

    def expert_partials(received):
        received_shape = received.shape
        flat_rows = received.reshape(-1, received_shape[3])
        partial_out = scaled_partial(flat_rows, weights, scale_table, block_side)
        return partial_out.reshape(received_shape[0], received_shape[1], received_shape[2], columns)

    def expert_work(received):
        partial_out = expert_partials(received)
        return lax.all_to_all(partial_out, "dp", split_axis=1, concat_axis=1, tiled=True)

    def decode(hidden, routed, gate_values):
        packed, slot_index = packer(hidden, routed)
        returned = expert_work(
            lax.all_to_all(packed, "dp", split_axis=1, concat_axis=1, tiled=True)
        )
        step_count = returned.shape[0]
        returned = returned.reshape(step_count, experts, 2, capacity, columns).astype(jnp.float32)
        combined = (returned[:, :, 0] + returned[:, :, 1]).astype(jnp.bfloat16)
        combined = lax.optimization_barrier(combined)
        combined = combined.reshape(step_count, experts * capacity, columns).astype(jnp.float32)
        picked = jax.vmap(partial(jnp.take, axis=0))(combined, slot_index)
        weighted = (
            picked.reshape(step_count, step_rows, topk_count, columns) * gate_values[..., None]
        )
        return jnp.sum(weighted, axis=2).astype(jnp.bfloat16)

    decoded = jnp.concatenate(
        [
            decode(
                decode_hidden[step_index : step_index + 1],
                routing[step_index : step_index + 1],
                gate_weight[step_index : step_index + 1],
            )
            for step_index in range(decode_hidden.shape[0])
        ],
        axis=0,
    )
    return (decoded, new_master)


def solution(mesh):
    return jax.shard_map(
        local,
        mesh=mesh,
        in_specs=(
            P(("groups", "dp"), None),
            P(("groups", "dp"), None),
            P("dp", None, None),
            P("dp", None, None),
            P("dp", None, None),
            P("dp", None),
            P("dp", None),
            P(),
            P(None, ("groups", "dp"), None, None),
            P(None, ("groups", "dp"), None),
            P(None, ("groups", "dp"), None),
        ),
        out_specs=(P(None, ("groups", "dp"), None), P(("groups", "dp"), None, None)),
        check_vma=False,
    )
```

profile of v0, /device:TPU:0, one launch (start us, length us, event | category | flops | bytes accessed | tf_op | source)
XLA Modules:
  0.0 513.5 jit_solution(5902203654378722062)
XLA Ops:
  8.2 7.3 %convolution_bitcast_fusion = f32[192,8,16,128]{3,1,2,0:T(8,128)} fusion(bf16[128,1536]{1,0:T(8,128)(2,1)} %param.13, bf16[128,2048]{1,0:T(8,128)(2,1)S(1)} %copy-done), kind=kOutput, calls=%fused_computation.5 | convolution fusion | flops 805306368 | bytes 13500416 | tf_op jit(solution)/shard_map/dot_general | solution.py:97
  15.5 12.2 %copy.185 = f32[192,8,16,128]{3,2,1,0:T(8,128)} copy(f32[192,8,16,128]{3,1,2,0:T(8,128)} %convolution_bitcast_fusion) | data formatting | bytes 25165824
  27.7 9.9 %bitcast_bitcast_fusion = f32[12,16,128,128]{3,1,2,0:T(8,128)} fusion(f32[12,128,16,128]{3,2,1,0:T(8,128)} %bitcast.225), kind=kLoop, calls=%fused_computation.4 | loop fusion | bytes 25165824 | tf_op jit(solution)/shard_map/transpose | solution.py:100
  37.6 12.9 %copy.145 = f32[12,16,128,128]{3,2,1,0:T(8,128)} copy(f32[12,16,128,128]{3,1,2,0:T(8,128)} %bitcast_bitcast_fusion) | data formatting | bytes 25165824 | tf_op jit(solution)/shard_map/transpose | solution.py:100
  50.6 158.5 %reduce-scatter.2.cloned.1.call-done = f32[6,128,128]{2,1,0:T(8,128)} async-done(((f32[192,128,128]{2,1,0:T(8,128)}), f32[6,128,128]{2,1,0:T(8,128)}) %reduce-scatter.2.cloned.1.call-update) | async-done | bytes 393232 | tf_op jit(solution)/shard_map/reduce_scatter | solution.py:103
  214.0 4.0 all-to-all-start.6
  220.2 14.7 %all-to-all-done.6 = bf16[1,32,6,768]{3,2,0,1:T(8,128)(2,1)S(1)} async-done(((bf16[1,32,6,768]{3,2,0,1:T(8,128)(2,1)}), bf16[1,32,6,768]{3,2,0,1:T(8,128)(2,1)S(1)}, u32[]{:S(2)}, u32[]{:S(2)}) %all-to-all-start.6) | async-done | bytes 294944 | tf_op jit(solution)/shard_map/all_to_all | solution.py:144
  239.5 18.5 %all-to-all-done.4 = bf16[1,32,6,768]{3,2,0,1:T(8,128)(2,1)S(1)} async-done(((bf16[1,32,6,768]{3,2,0,1:T(8,128)(2,1)}), bf16[1,32,6,768]{3,2,0,1:T(8,128)(2,1)S(1)}, u32[]{:S(2)}, u32[]{:S(2)}) %all-to-all-start.4) | async-done | bytes 294944 | tf_op jit(solution)/shard_map/all_to_all | solution.py:144
  262.9 19.4 %all-to-all-done.2 = bf16[1,32,6,768]{3,2,0,1:T(8,128)(2,1)S(1)} async-done(((bf16[1,32,6,768]{3,2,0,1:T(8,128)(2,1)}), bf16[1,32,6,768]{3,2,0,1:T(8,128)(2,1)S(1)}, u32[]{:S(2)}, u32[]{:S(2)}) %all-to-all-start.2) | async-done | bytes 294944 | tf_op jit(solution)/shard_map/all_to_all | solution.py:144
  282.3 4.8 all-to-all-start
  289.7 10.6 %all-to-all-done = bf16[1,32,6,768]{3,2,0,1:T(8,128)(2,1)S(1)} async-done(((bf16[1,32,6,768]{3,2,0,1:T(8,128)(2,1)}), bf16[1,32,6,768]{3,2,0,1:T(8,128)(2,1)S(1)}, u32[]{:S(2)}, u32[]{:S(2)}) %all-to-all-start) | async-done | bytes 294944 | tf_op jit(solution)/shard_map/all_to_all | solution.py:144
  300.7 38.7 %all-reduce = bf16[192]{0:T(256)(128)(2,1)S(1)} all-reduce(bf16[192]{0:T(256)(128)(2,1)S(1)} %dynamic-update-slice), channel_id=1, replica_groups=mesh['groups'=1,'dp'=32] {'dp'}, use_global_device_ids=true, to_apply=%add | all-reduce | flops 192 | bytes 768
  358.9 13.2 %all-to-all-start.7 = ((bf16[1,32,6,2048]{3,2,0,1:T(8,128)(2,1)}), bf16[1,32,6,2048]{3,2,0,1:T(8,128)(2,1)}, u32[]{:S(2)}, u32[]{:S(2)}) async-start(bf16[1,32,6,2048]{3,2,0,1:T(8,128)(2,1)} %bitcast.230), calls=%async_computation.8 | async-start | bytes 2097152 | tf_op jit(solution)/shard_map/all_to_all | solution.py:139
  372.1 4.8 fusion.21
  387.6 10.6 %all-to-all-done.7 = bf16[1,32,6,2048]{3,2,0,1:T(8,128)(2,1)} async-done(((bf16[1,32,6,2048]{3,2,0,1:T(8,128)(2,1)}), bf16[1,32,6,2048]{3,2,0,1:T(8,128)(2,1)}, u32[]{:S(2)}, u32[]{:S(2)}) %all-to-all-start.7) | async-done | bytes 786464 | tf_op jit(solution)/shard_map/all_to_all | solution.py:139
  398.1 3.8 all-to-all-start.5
  401.9 4.8 fusion.22
  414.9 13.2 %all-to-all-done.5 = bf16[1,32,6,2048]{3,2,0,1:T(8,128)(2,1)} async-done(((bf16[1,32,6,2048]{3,2,0,1:T(8,128)(2,1)}), bf16[1,32,6,2048]{3,2,0,1:T(8,128)(2,1)}, u32[]{:S(2)}, u32[]{:S(2)}) %all-to-all-start.5) | async-done | bytes 786464 | tf_op jit(solution)/shard_map/all_to_all | solution.py:139
  428.1 3.7 all-to-all-start.3
  433.3 4.0 fusion.23
  449.3 8.8 %all-to-all-done.3 = bf16[1,32,6,2048]{3,2,0,1:T(8,128)(2,1)} async-done(((bf16[1,32,6,2048]{3,2,0,1:T(8,128)(2,1)}), bf16[1,32,6,2048]{3,2,0,1:T(8,128)(2,1)}, u32[]{:S(2)}, u32[]{:S(2)}) %all-to-all-start.3) | async-done | bytes 786464 | tf_op jit(solution)/shard_map/all_to_all | solution.py:139
  458.1 4.0 all-to-all-start.1
  472.2 16.0 %all-to-all-done.1 = bf16[1,32,6,2048]{3,2,0,1:T(8,128)(2,1)} async-done(((bf16[1,32,6,2048]{3,2,0,1:T(8,128)(2,1)}), bf16[1,32,6,2048]{3,2,0,1:T(8,128)(2,1)}, u32[]{:S(2)}, u32[]{:S(2)}) %all-to-all-start.1) | async-done | bytes 786464 | tf_op jit(solution)/shard_map/all_to_all | solution.py:139
  488.2 4.3 reshape.1460
  (160 shorter events, 95.9 us)
Async XLA Ops:
  7.2 201.9 %reduce-scatter.2.cloned.1.call-start = ((), (), s32[]{:S(2)}) async-start(), calls=%async_computation.9 | async-start | bytes 12976128 | tf_op jit(solution)/shard_map/reduce_scatter | solution.py:103
  50.4 158.6 %copy-start.12 = (f32[6,128,128]{2,1,0:T(8,128)S(1)}, f32[6,128,128]{2,1,0:T(8,128)}, u32[]{:S(2)}) copy-start(f32[6,128,128]{2,1,0:T(8,128)} %param.15) | copy-start | bytes 1179652
  50.4 158.6 %copy-start.13 = (f32[6,128,128]{2,1,0:T(8,128)S(1)}, f32[6,128,128]{2,1,0:T(8,128)}, u32[]{:S(2)}) copy-start(f32[6,128,128]{2,1,0:T(8,128)} %param.17) | copy-start | bytes 1179652
  50.4 158.6 %copy-start.14 = (f32[6,128,128]{2,1,0:T(8,128)S(1)}, f32[6,128,128]{2,1,0:T(8,128)}, u32[]{:S(2)}) copy-start(f32[6,128,128]{2,1,0:T(8,128)} %param.16) | copy-start | bytes 1179652
  50.5 160.9 %copy-start.15 = (s32[4,8,8]{2,1,0:T(8,128)S(1)}, s32[4,8,8]{2,1,0:T(8,128)}, u32[]{:S(2)}) copy-start(s32[4,8,8]{2,1,0:T(8,128)} %param.22) | copy-start | bytes 3076
  50.5 161.2 %copy-start.19 = (s32[16]{0:T(128)S(1)}, s32[16]{0:T(128)}, u32[]{:S(2)}) copy-start(s32[16]{0:T(128)} %param.20) | copy-start | bytes 196
  50.5 162.0 %copy-start.11 = (bf16[4,8,8,1536]{3,2,1,0:T(8,128)(2,1)S(1)}, bf16[4,8,8,1536]{3,2,1,0:T(8,128)(2,1)}, u32[]{:S(2)}) copy-start(bf16[4,8,8,1536]{3,2,1,0:T(8,128)(2,1)} %param.21) | copy-start | bytes 2359300
  50.5 289.3 %all-gather.2.cloned.1.call-start = ((), (), s32[]{:S(2)}) async-start(), calls=%async_computation.10 | async-start | bytes 6488064 | tf_op jit(solution)/shard_map/all_gather | solution.py:107
  210.5 3.6 copy-start.7
  214.0 20.8 %all-to-all-start.6 = ((bf16[1,32,6,768]{3,2,0,1:T(8,128)(2,1)}), bf16[1,32,6,768]{3,2,0,1:T(8,128)(2,1)S(1)}, u32[]{:S(2)}, u32[]{:S(2)}) async-start(bf16[1,32,6,768]{3,2,0,1:T(8,128)(2,1)} %bitcast.70), calls=%async_computation.7 | async-start | bytes 786432 | tf_op jit(solution)/shard_map/all_to_all | solution.py:144
  234.9 23.0 %all-to-all-start.4 = ((bf16[1,32,6,768]{3,2,0,1:T(8,128)(2,1)}), bf16[1,32,6,768]{3,2,0,1:T(8,128)(2,1)S(1)}, u32[]{:S(2)}, u32[]{:S(2)}) async-start(bf16[1,32,6,768]{3,2,0,1:T(8,128)(2,1)} %bitcast.54), calls=%async_computation.5 | async-start | bytes 786432 | tf_op jit(solution)/shard_map/all_to_all | solution.py:144
  257.9 29.3 %copy-start.16 = (f32[4,8,8]{2,1,0:T(8,128)S(1)}, f32[4,8,8]{2,1,0:T(8,128)}, u32[]{:S(2)}) copy-start(f32[4,8,8]{2,1,0:T(8,128)} %param.23) | copy-start | bytes 3076
  257.9 24.4 %all-to-all-start.2 = ((bf16[1,32,6,768]{3,2,0,1:T(8,128)(2,1)}), bf16[1,32,6,768]{3,2,0,1:T(8,128)(2,1)S(1)}, u32[]{:S(2)}, u32[]{:S(2)}) async-start(bf16[1,32,6,768]{3,2,0,1:T(8,128)(2,1)} %bitcast.38), calls=%async_computation.3 | async-start | bytes 786432 | tf_op jit(solution)/shard_map/all_to_all | solution.py:144
  282.3 18.0 %all-to-all-start = ((bf16[1,32,6,768]{3,2,0,1:T(8,128)(2,1)}), bf16[1,32,6,768]{3,2,0,1:T(8,128)(2,1)S(1)}, u32[]{:S(2)}, u32[]{:S(2)}) async-start(bf16[1,32,6,768]{3,2,0,1:T(8,128)(2,1)} %bitcast.5), calls=%async_computation | async-start | bytes 786432 | tf_op jit(solution)/shard_map/all_to_all | solution.py:144
  287.1 52.4 %copy-start.17 = (f32[6,16]{1,0:T(8,128)S(1)}, f32[6,16]{1,0:T(8,128)}, u32[]{:S(2)}) copy-start(f32[6,16]{1,0:T(8,128)} %param.19) | copy-start | bytes 1156
  358.9 39.2 %all-to-all-start.7 = ((bf16[1,32,6,2048]{3,2,0,1:T(8,128)(2,1)}), bf16[1,32,6,2048]{3,2,0,1:T(8,128)(2,1)}, u32[]{:S(2)}, u32[]{:S(2)}) async-start(bf16[1,32,6,2048]{3,2,0,1:T(8,128)(2,1)} %bitcast.230), calls=%async_computation.8 | async-start | bytes 2097152 | tf_op jit(solution)/shard_map/all_to_all | solution.py:139
  379.1 2.4 copy-start.8
  398.1 30.0 %all-to-all-start.5 = ((bf16[1,32,6,2048]{3,2,0,1:T(8,128)(2,1)}), bf16[1,32,6,2048]{3,2,0,1:T(8,128)(2,1)}, u32[]{:S(2)}, u32[]{:S(2)}) async-start(bf16[1,32,6,2048]{3,2,0,1:T(8,128)(2,1)} %bitcast.229), calls=%async_computation.6 | async-start | bytes 2097152 | tf_op jit(solution)/shard_map/all_to_all | solution.py:139
  428.1 30.0 %all-to-all-start.3 = ((bf16[1,32,6,2048]{3,2,0,1:T(8,128)(2,1)}), bf16[1,32,6,2048]{3,2,0,1:T(8,128)(2,1)}, u32[]{:S(2)}, u32[]{:S(2)}) async-start(bf16[1,32,6,2048]{3,2,0,1:T(8,128)(2,1)} %bitcast.228), calls=%async_computation.4 | async-start | bytes 2097152 | tf_op jit(solution)/shard_map/all_to_all | solution.py:139
  449.3 12.8 %copy-start.4 = (f32[1,16,1,6,2048]{4,0,3,2,1:T(1,128)S(1)}, f32[1,16,1,6,2048]{4,0,3,2,1:T(1,128)}, u32[]{:S(2)}) copy-start(f32[1,16,1,6,2048]{4,0,3,2,1:T(1,128)} %get-tuple-element.23) | copy-start | bytes 2359300
  449.3 12.8 %copy-start.5 = (f32[1,16,1,6,2048]{4,0,3,2,1:T(1,128)S(1)}, f32[1,16,1,6,2048]{4,0,3,2,1:T(1,128)}, u32[]{:S(2)}) copy-start(f32[1,16,1,6,2048]{4,0,3,2,1:T(1,128)} %get-tuple-element.24) | copy-start | bytes 2359300
  458.1 30.2 %all-to-all-start.1 = ((bf16[1,32,6,2048]{3,2,0,1:T(8,128)(2,1)}), bf16[1,32,6,2048]{3,2,0,1:T(8,128)(2,1)}, u32[]{:S(2)}, u32[]{:S(2)}) async-start(bf16[1,32,6,2048]{3,2,0,1:T(8,128)(2,1)} %bitcast.23), calls=%async_computation.2 | async-start | bytes 2097152 | tf_op jit(solution)/shard_map/all_to_all | solution.py:139
  501.8 2.6 copy-start.6
  501.8 4.4 copy-start.1
  (6 other events, 7.6 us)
Sparse Core Ops, SparseCore 0:
  50.6 158.4 reduce-scatter.1
  212.3 80.3 all-gather.1
where the time goes:
time: 523 us; the launch traced here: 513 us
  waiting for transfers between devices  270 us (52%)
  local copies, waits for them, and re-layouts  90.4 us (17%)
  matrix products  48 us (9%)
  starting transfers between devices  40.2 us (8%)
  blocking collectives  38.7 us (7%)
  between operations  15.2 us (3%)
  other arithmetic  10.6 us (2%)
    reduce_scatter x1, waiting for transfers between devices, local(): lax.psum_scatter(full_gradient, 'dp', scatter_dimension=0, tiled=True)  158 us
    all_to_all x4, waiting for transfers between devices, decode(): lax.all_to_all(packed, 'dp', split_axis=1, concat_axis=1, tiled=True)  63.2 us
    all_to_all x4, waiting for transfers between devices, expert_work(): lax.all_to_all(partial_out, 'dp', split_axis=1, concat_axis=1, tiled=True)  48.5 us
    dot_general x24, matrix products, scaled_partial(): jnp.dot(input_rows[:, row_block * block_side:(row_block + 1) * block_side...  39.4 us
    unnamed x1, blocking collectives  38.7 us
    all_to_all x4, starting transfers between devices, expert_work(): lax.all_to_all(partial_out, 'dp', split_axis=1, concat_axis=1, tiled=True)  24.7 us
    transpose x2, local copies, waits for them, and re-layouts, local(): full_gradient = full_gradient.reshape(row_blocks, block_side, column_bloc...  22.7 us
    all_to_all x4, starting transfers between devices, decode(): lax.all_to_all(packed, 'dp', split_axis=1, concat_axis=1, tiled=True)  15.4 us
  transfers between devices with their start and end apart: 10, of which 9 were waited for; matrix products, arithmetic and copies ran while one was open for 13% of the time, Pallas kernels for 0%

commit v1 on v0

v1 whole, which is shorter than its diff:
```python
import jax
import jax.numpy as jnp
from jax import lax
from jax.experimental import pallas as pl
from jax.experimental.pallas import tpu as pltpu
from jax.sharding import PartitionSpec as P

learn_rate = 0.05
beta_first = 0.9
beta_second = 0.95
correct_first = 1.0 - 0.9**10
correct_second = 1.0 - 0.95**10
decay_rate = 0.1
adam_epsilon = 1e-08
quant_range = 448.0

F32 = jnp.float32
BF16 = jnp.bfloat16
PARAMS = pltpu.CompilerParams(vmem_limit_bytes=40 * 2**20)


def optimizer(gradient, master, moment_first, moment_second):
    first_moment = beta_first * moment_first + (1.0 - beta_first) * gradient
    second_moment = beta_second * moment_second + (1.0 - beta_second) * gradient * gradient
    update = (
        first_moment / correct_first / (jnp.sqrt(second_moment / correct_second) + adam_epsilon)
    )
    return master - learn_rate * (update + decay_rate * master)


def quantize(weights):
    largest = jnp.max(jnp.abs(weights), axis=(1, 2))
    scales = (largest + 1e-06) / quant_range
    quantized = (weights / scales[:, None, None]).astype(BF16)
    return (quantized, scales)


def vmem(count):
    return [pl.BlockSpec(memory_space=pltpu.VMEM)] * count


def pack_kernel(
    steps,
    experts,
    capacity,
    placement,
    route_row,
    route_column,
    gate_row,
    hidden,
    packed,
    gates,
    gates_trained,
):
    entries = route_row.shape[1]
    step_entries = entries // steps
    topk = step_entries // (gates.shape[0] // 2 // steps)
    rows = gates.shape[0] // 2
    routed = route_row[...]
    lane = lax.broadcasted_iota(jnp.int32, (entries, entries), 1)
    line = lax.broadcasted_iota(jnp.int32, (entries, entries), 0)
    earlier = (lane // step_entries == line // step_entries) & (line // topk < lane // topk)
    same = (route_column[...] == routed) & earlier
    place = jnp.sum(jnp.where(same, 1.0, 0.0), axis=0, keepdims=True).astype(jnp.int32)
    pair = jnp.zeros_like(routed)
    for expert in range(experts):
        pair = jnp.where(routed == expert, placement[expert], pair)
    entry = lax.broadcasted_iota(jnp.int32, (1, entries), 1)
    step_slot = entry // step_entries * capacity + place
    slot = pair * (steps * capacity) + step_slot
    slots = gates.shape[1]
    onehot = jnp.where(
        lax.broadcasted_iota(jnp.int32, (slots, entries), 0) == slot, 1.0, 0.0
    ).astype(BF16)
    half = packed.shape[2]
    for side in range(2):
        packed[side] = jnp.dot(
            onehot, hidden[:, side * half : (side + 1) * half], preferred_element_type=F32
        ).astype(BF16)
    row = lax.broadcasted_iota(jnp.int32, (rows, entries), 0)
    mine = lax.broadcasted_iota(jnp.int32, (rows, entries), 1) // topk == row
    trained = routed == 0
    onehot_trained = jnp.where(
        (lax.broadcasted_iota(jnp.int32, (steps * capacity, entries), 0) == step_slot) & trained,
        1.0,
        0.0,
    ).astype(BF16)
    weight = jnp.where(mine, gate_row[...], 0.0)
    high = weight.astype(BF16)
    rest = (weight - high.astype(F32)).astype(BF16)
    plain = jnp.where(trained, 0.0, 1.0).astype(BF16)
    over_entries = (((1,), (1,)), ((), ()))
    for index, part in enumerate((high, rest)):
        at = slice(index * rows, (index + 1) * rows)
        gates[at] = lax.dot_general(
            part * plain, onehot, over_entries, preferred_element_type=F32
        ).astype(BF16)
        gates_trained[at] = lax.dot_general(
            part, onehot_trained, over_entries, preferred_element_type=F32
        ).astype(BF16)


def gradient_kernel(
    device_ref,
    hidden_own,
    hidden_other,
    cotangent_own,
    cotangent_other,
    first_sent,
    first_kept,
    second_sent,
    second_kept,
    hidden_across,
    cotangent,
):
    device = device_ref[0]
    tokens = hidden_own.shape[0]
    hidden_across[:, :tokens] = hidden_own[...].T
    hidden_across[:, tokens:] = hidden_other[...].T
    cotangent[:tokens] = cotangent_own[...]
    cotangent[tokens:] = cotangent_other[...]
    highs, _, blocks, side, _ = first_sent.shape
    column_blocks = cotangent.shape[1] // side
    wide = 2 if blocks % 2 == 0 else 1
    core = device % 2
    bit_x = device // 2 % 2
    bit_y = device // 4 % 2

    def fill(out, dest_of):
        def body(index, carry):
            high, free = index // 2, index % 2
            dest = dest_of(high, free)
            for at in range(0, blocks, wide):
                block = dest * blocks + at
                row = pl.multiple_of(block // column_blocks * side, side)
                column = pl.multiple_of(block % column_blocks * side, side)
                product = jnp.dot(
                    hidden_across[pl.ds(row, side), :],
                    cotangent[:, pl.ds(column, wide * side)],
                    preferred_element_type=F32,
                ).astype(out.dtype)
                for part in range(wide):
                    out[high, free, at + part] = product[:, part * side : (part + 1) * side]
            return carry

        lax.fori_loop(0, 2 * highs, body, 0)

    def number(high, y, x):
        return ((high * 2 + y) * 2 + x) * 2 + core

    fill(first_sent, lambda high, free: number(high, free, 1 - bit_x))
    fill(second_sent, lambda high, free: number(high + highs, 1 - bit_y, free))
    fill(first_kept, lambda high, free: number(high, free, bit_x))
    fill(second_kept, lambda high, free: number(high + highs, bit_y, free))


def trained_kernel(device_ref, plane, flips, rows, weights, out):
    device = device_ref[0]
    depth, blocks, side, _ = weights.shape
    inner = device % plane
    floor = device // plane
    column_blocks = plane * blocks
    for at in range(blocks):
        total = jnp.zeros((rows.shape[1], side), F32)
        for slot in range(depth):
            block = ((floor ^ flips[slot]) * plane + inner) * blocks + at
            row_block = block // out_columns(rows, plane, blocks, depth)
            total = total + jnp.dot(rows[row_block], weights[slot, at], preferred_element_type=F32)
        out[:, at * side : (at + 1) * side] = total.astype(out.dtype)


def out_columns(rows, plane, blocks, depth):
    return plane * blocks * depth // rows.shape[0]


def combine_kernel(returned, trained, gates, gates_trained, out):
    peers, _, width = trained.shape
    columns = out.shape[1]
    side = 128
    per_peer = width // side
    count = out.shape[0]
    for column in range(columns // side):
        at = slice(column * side, (column + 1) * side)
        fresh = None
        for number in range(column, peers * per_peer, columns // side):
            peer, block = divmod(number, per_peer)
            part = trained[peer, :, block * side : (block + 1) * side].astype(F32)
            fresh = part if fresh is None else fresh + part
        both = jnp.dot(gates[...], returned[:, at], preferred_element_type=F32) + jnp.dot(
            gates_trained[...], fresh.astype(BF16), preferred_element_type=F32
        )
        out[:, at] = (both[:count] + both[count:]).astype(out.dtype)


def local(
    learn_hidden,
    learn_cotangent,
    master,
    moment_first,
    moment_second,
    resident_weight,
    resident_scale,
    placement,
    decode_hidden,
    routing,
    gate_weight,
):
    devices = lax.axis_size("dp")
    device = lax.axis_index("dp")
    device_ref = device.astype(jnp.int32).reshape(1)
    blocks, side = master.shape[:2]
    hidden_width = learn_hidden.shape[1]
    columns = learn_cotangent.shape[1]
    row_blocks = hidden_width // side
    column_blocks = columns // side
    tokens = learn_hidden.shape[0]
    steps, step_rows, topk = routing.shape
    experts = placement.shape[0]
    capacity = min(step_rows, step_rows * topk // experts + 2)
    entries = steps * step_rows * topk
    pair_slots = steps * capacity
    slots = experts * pair_slots
    half = hidden_width // 2

    def flip(array, mask):
        return lax.ppermute(array, "dp", [(i, i ^ mask) for i in range(devices)])

    def bit(number):
        return device // 2**number % 2

    def pick(array, index, axis):
        return lax.dynamic_index_in_dim(array, index, axis, keepdims=False)

    routed = routing.reshape(1, entries)
    packed, gates, gates_trained = pl.pallas_call(
        lambda *refs: pack_kernel(steps, experts, capacity, *refs),
        out_shape=(
            jax.ShapeDtypeStruct((2, slots, half), BF16),
            jax.ShapeDtypeStruct((2 * steps * step_rows, slots), BF16),
            jax.ShapeDtypeStruct((2 * steps * step_rows, pair_slots), BF16),
        ),
        in_specs=[pl.BlockSpec(memory_space=pltpu.SMEM)] + vmem(4),
        out_specs=tuple(vmem(3)),
        compiler_params=PARAMS,
    )(
        placement,
        routed,
        routed.reshape(entries, 1),
        gate_weight.reshape(1, entries),
        decode_hidden.reshape(entries, hidden_width),
    )
    by_core = [list(range(0, devices, 2)) + list(range(1, devices, 2))]
    received = lax.all_to_all(
        packed.reshape(devices, pair_slots, half),
        "dp",
        split_axis=0,
        concat_axis=0,
        tiled=True,
        axis_index_groups=by_core,
    ).reshape(2, slots, half)

    highs = devices // 16
    part = jax.ShapeDtypeStruct((highs, 2, blocks, side, side), BF16)
    first_sent, first_kept, second_sent, second_kept = pl.pallas_call(
        gradient_kernel,
        out_shape=(part,) * 4,
        in_specs=[pl.BlockSpec(memory_space=pltpu.SMEM)] + vmem(4),
        out_specs=tuple(vmem(4)),
        scratch_shapes=[
            pltpu.VMEM((hidden_width, 2 * tokens), BF16),
            pltpu.VMEM((2 * tokens, columns), BF16),
        ],
        compiler_params=PARAMS,
    )(
        device_ref,
        learn_hidden,
        flip(learn_hidden, 1),
        learn_cotangent,
        flip(learn_cotangent, 1),
    )

    def halve(kept, arrived, number):
        total = kept.astype(F32) + arrived.astype(F32)
        return pick(total, 1 - bit(number), 1).astype(BF16), pick(total, bit(number), 1)

    first_sent, first_kept = halve(first_kept, flip(first_sent, 2), 2)
    second_sent, second_kept = halve(second_kept, flip(second_sent, 4), 1)
    first = first_kept + flip(first_sent, 4).astype(F32)
    second = second_kept + flip(second_sent, 2).astype(F32)
    gradient = jnp.concatenate([first, second], axis=0)
    number = 3
    while gradient.shape[0] > 1:
        split = gradient.reshape((-1, 2) + gradient.shape[1:])
        sent = pick(split, 1 - bit(number), 1).astype(BF16)
        gradient = pick(split, bit(number), 1) + flip(sent, 2**number).astype(F32)
        number += 1
    new_master = optimizer(gradient[0], master, moment_first, moment_second)
    quantized, scales = quantize(new_master)
    fresh = (quantized.astype(F32) * scales[:, None, None]).astype(BF16)

    scale_rows = jnp.repeat(resident_scale, side, axis=1)[:, None, :]
    weights = (
        (resident_weight.reshape(row_blocks // 2, side, columns).astype(F32) * scale_rows)
        .astype(BF16)
        .reshape(half, columns)
    )
    core = bit(0)
    sent = jnp.dot(pick(received, 1 - core, 0), weights, preferred_element_type=F32).astype(BF16)
    kept = jnp.dot(pick(received, core, 0), weights, preferred_element_type=F32).astype(BF16)
    expert_out = (kept.astype(F32) + flip(sent, 1).astype(F32)).astype(BF16)
    same_core = [list(range(0, devices, 2)), list(range(1, devices, 2))]
    returned = lax.all_to_all(
        expert_out.reshape(experts, pair_slots, columns),
        "dp",
        split_axis=0,
        concat_axis=0,
        tiled=True,
        axis_index_groups=same_core,
    ).reshape(slots, columns)

    plane = 1
    while plane * blocks % column_blocks:
        plane *= 2
    depth = devices // plane
    gathered = pick(packed.reshape(2, experts, pair_slots, half), placement[0], 1)[None]
    mask = 1
    while mask < plane:
        other = flip(gathered, mask)
        upper = device // mask % 2 == 1
        gathered = jnp.concatenate(
            [jnp.where(upper, other, gathered), jnp.where(upper, gathered, other)], axis=0
        )
        mask *= 2
    rows = (
        gathered.reshape(plane, 2, pair_slots, row_blocks // 2, side)
        .transpose(1, 3, 0, 2, 4)
        .reshape(row_blocks, plane * pair_slots, side)
    )
    held, flips = fresh[None], [0]
    mask = devices // 2
    while mask >= plane:
        held = jnp.concatenate([held, flip(held, mask)], axis=0)
        flips = flips + [f ^ (mask // plane) for f in flips]
        mask //= 2
    trained = pl.pallas_call(
        lambda device_ref, *refs: trained_kernel(device_ref, plane, flips, *refs),
        out_shape=jax.ShapeDtypeStruct((plane * pair_slots, blocks * side), BF16),
        in_specs=[pl.BlockSpec(memory_space=pltpu.SMEM)] + vmem(2),
        out_specs=vmem(1)[0],
        compiler_params=PARAMS,
    )(device_ref, rows, held)
    planes = [[z * plane + i for i in range(plane)] for z in range(depth)]
    trained = lax.all_to_all(
        trained.reshape(plane, pair_slots, blocks * side),
        "dp",
        split_axis=0,
        concat_axis=0,
        tiled=True,
        axis_index_groups=planes,
    )
    decoded = pl.pallas_call(
        combine_kernel,
        out_shape=jax.ShapeDtypeStruct((steps * step_rows, columns), BF16),
        in_specs=vmem(4),
        out_specs=vmem(1)[0],
        compiler_params=PARAMS,
    )(returned, trained, gates, gates_trained)
    return (decoded.reshape(steps, step_rows, columns), new_master)


def solution(mesh):
    return jax.shard_map(
        local,
        mesh=mesh,
        in_specs=(
            P(("groups", "dp"), None),
            P(("groups", "dp"), None),
            P("dp", None, None),
            P("dp", None, None),
            P("dp", None, None),
            P("dp", None),
            P("dp", None),
            P(),
            P(None, ("groups", "dp"), None, None),
            P(None, ("groups", "dp"), None),
            P(None, ("groups", "dp"), None),
        ),
        out_specs=(P(None, ("groups", "dp"), None), P(("groups", "dp"), None, None)),
        check_vma=False,
    )
```

time: 523 us -> 150 us (0.29); the launches traced: 513 us -> 150 us
  waiting for transfers between devices: 270 us -> 53.6 us
  local copies, waits for them, and re-layouts: 90.4 us -> 4.39 us
  matrix products: 48 us -> 8.68 us
  starting transfers between devices: 40.2 us -> 23.6 us
  between operations: 15.2 us -> 1.09 us
  Pallas kernels: 0 us -> 9.41 us
    reduce_scatter x1 -> x0, waiting for transfers between devices: 158 us -> none  [local(): lax.psum_scatter(full_gradient, 'dp', scatter_dimension=0, tiled=True)]
    all_to_all x8 -> x2, waiting for transfers between devices: 112 us -> 3.28 us  [the longest x1 3.27 us: local(): lax.all_to_all(trained.reshape(plane, pair_slots, blocks * side), 'dp', s...]
    ppermute x0 -> x14, waiting for transfers between devices: none -> 50.3 us  [flip(): return lax.ppermute(array, 'dp', [(i, i ^ mask) for i in range(devices)])]
    all_to_all x0 -> x1, blocking collectives: none -> 39.7 us  [local(): lax.all_to_all(expert_out.reshape(experts, pair_slots, columns), 'dp', sp...]
    dot_general x29 -> x2, matrix products: 48 us -> 8.68 us  [the longest x1 4.76 us: local(): jnp.dot(pick(received, 1 - core, 0), weights, preferred_element_type=F32)]
    unnamed x1 -> x0, blocking collectives: 38.7 us -> none
    all_to_all x8 -> x2, starting transfers between devices: 40.1 us -> 7.5 us  [the longest x1 4.08 us: local(): lax.all_to_all(packed.reshape(devices, pair_slots, half), 'dp', split_axi...]
    transpose x3 -> x1, local copies, waits for them, and re-layouts: 24.8 us -> 0.09 us  [local(): rows = gathered.reshape(plane, 2, pair_slots, row_blocks // 2, side).tran...]
  transfers between devices with their start and end apart: 10 -> 16, of which waited for: 9 -> 10; matrix products, arithmetic and copies ran while one was open for 13% -> 14% of each run, Pallas kernels for 0% -> 2%
where the time goes in v1:
time: 150 us
  waiting for transfers between devices  53.6 us (36%)
  blocking collectives  39.7 us (26%)
  starting transfers between devices  23.6 us (16%)
  Pallas kernels  9.41 us (6%)
  other arithmetic  9.38 us (6%)
  matrix products  8.68 us (6%)
  local copies, waits for them, and re-layouts  4.39 us (3%)
    ppermute x14, waiting for transfers between devices, flip(): return lax.ppermute(array, 'dp', [(i, i ^ mask) for i in range(devices)])  50.3 us
    all_to_all x1, blocking collectives, local(): lax.all_to_all(expert_out.reshape(experts, pair_slots, columns), 'dp', sp...  39.7 us
    ppermute x14, starting transfers between devices, flip(): return lax.ppermute(array, 'dp', [(i, i ^ mask) for i in range(devices)])  16.1 us
    pallas_call x1, Pallas kernels, local(): pl.pallas_call(gradient_kernel, out_shape=(part,) * 4, in_specs=[pl.Block...  4.89 us
    dot_general x1, matrix products, local(): jnp.dot(pick(received, 1 - core, 0), weights, preferred_element_type=F32)  4.76 us
    convert_element_type x1, other arithmetic, local(): weights = (resident_weight.reshape(row_blocks // 2, side, columns).astype...  4.47 us
    all_to_all x1, starting transfers between devices, local(): lax.all_to_all(packed.reshape(devices, pair_slots, half), 'dp', split_axi...  4.08 us
    dot_general x1, matrix products, local(): jnp.dot(pick(received, core, 0), weights, preferred_element_type=F32)  3.92 us
  transfers between devices with their start and end apart: 16, of which 10 were waited for; matrix products, arithmetic and copies ran while one was open for 14% of the time, Pallas kernels for 2%

profile of v1, /device:TPU:0, one launch (start us, length us, event | category | flops | bytes accessed | tf_op | source)
XLA Modules:
  0.0 149.8 jit_solution(15767847659330039853)
XLA Ops:
  1.2 2.2 %collective-permute-done.4.hidden_other = bf16[128,1536]{1,0:T(8,128)(2,1)S(1)} collective-permute-done((bf16[128,1536]{1,0:T(8,128)(2,1)}, bf16[128,1536]{1,0:T(8,128)(2,1)S(1)}, u32[]{:S(2)}, u32[]{:S(2)}) %collective-permute-start.4) | collective-permute-done | bytes 393248 | tf_op jit(solution)/shard_map/ppermute | solution.py:226
  5.5 4.9 %shard_map.123 = (bf16[2,2,6,128,128]{4,3,2,1,0:T(8,128)(2,1)S(1)}, bf16[2,2,6,128,128]{4,3,2,1,0:T(8,128)(2,1)S(1)}, bf16[2,2,6,128,128]{4,3,2,1,0:T(8,128)(2,1)}, bf16[2,2,6,128,128]{4,3,2,1,0:T(8,128)(2,1)S(1)}) custom-call(s32[1]{0:T(128)} %bitcast.8.device_ref, bf16[128,1536]{1,0:T(8,128)(2,1)S(1)} %copy-done.3, ...), custom_call_target="tpu_custom_call" | custom-call | tf_op jit(solution)/shard_map/pallas_call | solution.py:264
  10.5 2.9 %collective-permute-start.6 = (bf16[2,2,6,128,128]{4,3,2,0,1:T(8,128)(2,1)S(1)}, bf16[2,2,6,128,128]{4,3,2,0,1:T(8,128)(2,1)}, u32[]{:S(2)}, u32[]{:S(2)}) collective-permute-start(bf16[2,2,6,128,128]{4,3,2,0,1:T(8,128)(2,1)S(1)} %copy.18), channel_id=1, source_target_pairs={{0,2},{1,3},{2,0},{3,1},{4,6},{5,7},{6,4},{7,5},{8,10},{9,11},{10,... | collective-permute-start | bytes 2359304 | tf_op jit(solution)/shard_map/ppermute | solution.py:226
  13.4 1.5 %collective-permute-start.8 = (bf16[2,2,6,128,128]{4,3,2,1,0:T(8,128)(2,1)}, bf16[2,2,6,128,128]{4,3,2,1,0:T(8,128)(2,1)}, u32[]{:S(2)}, u32[]{:S(2)}) collective-permute-start(bf16[2,2,6,128,128]{4,3,2,1,0:T(8,128)(2,1)} %get-tuple-element.13), channel_id=1, source_target_pairs={{0,4},{1,5},{2,6},{3,7},{4,0},{5,1},{6,2},{7,3},{8,12},{9,13},{10,... | collective-permute-start | bytes 2359304 | tf_op jit(solution)/shard_map/ppermute | solution.py:226
  15.2 2.2 %shard_map.122 = (bf16[2,384,768]{2,1,0:T(8,128)(2,1)}, bf16[64,384]{1,0:T(8,128)(2,1)S(1)}, bf16[64,24]{1,0:T(8,128)(2,1)S(1)}) custom-call(s32[16]{0:T(128)S(1)} %copy-done.4, s32[1,256]{1,0:T(1,128)S(1)} %reshape.65.refs_1_, s32[256,1]{1,0:T(8,128)S(1)} %reshape_reshape.4.refs_2_, f32[1,256]{1,0:T(1,128)S(1)} %reshape.66.refs_3_, ...), custom_call_target="tpu_custom_call" | custom-call | tf_op jit(solution)/shard_map/pallas_call | solution.py:235
  17.4 4.1 %all-to-all-start = ((bf16[32,24,768]{2,1,0:T(8,128)(2,1)}), bf16[32,24,768]{2,1,0:T(8,128)(2,1)}, u32[]{:S(2)}, u32[]{:S(2)}) async-start(bf16[32,24,768]{2,1,0:T(8,128)(2,1)} %bitcast.1), calls=%async_computation | async-start | bytes 2359296 | tf_op jit(solution)/shard_map/all_to_all | solution.py:253
  22.7 14.8 %collective-permute-done.6 = bf16[2,2,6,128,128]{4,3,2,0,1:T(8,128)(2,1)} collective-permute-done((bf16[2,2,6,128,128]{4,3,2,0,1:T(8,128)(2,1)S(1)}, bf16[2,2,6,128,128]{4,3,2,0,1:T(8,128)(2,1)}, u32[]{:S(2)}, u32[]{:S(2)}) %collective-permute-start.6) | collective-permute-done | bytes 786464 | tf_op jit(solution)/shard_map/ppermute | solution.py:226
  37.5 1.4 convert_add_fusion.1
  39.0 2.0 %collective-permute-start.7 = (bf16[2,6,128,128]{3,2,1,0:T(8,128)(2,1)S(1)}, bf16[2,6,128,128]{3,2,1,0:T(8,128)(2,1)S(1)}, u32[]{:S(2)}, u32[]{:S(2)}) collective-permute-start(bf16[2,6,128,128]{3,2,1,0:T(8,128)(2,1)S(1)} %fusion.11), channel_id=1, source_target_pairs={{0,4},{1,5},{2,6},{3,7},{4,0},{5,1},{6,2},{7,3},{8,12},{9,13},{10,... | collective-permute-start | bytes 1179656 | tf_op jit(solution)/shard_map/ppermute | solution.py:226
  41.0 2.6 %collective-permute-done.8 = bf16[2,2,6,128,128]{4,3,2,1,0:T(8,128)(2,1)} collective-permute-done((bf16[2,2,6,128,128]{4,3,2,1,0:T(8,128)(2,1)}, bf16[2,2,6,128,128]{4,3,2,1,0:T(8,128)(2,1)}, u32[]{:S(2)}, u32[]{:S(2)}) %collective-permute-start.8) | collective-permute-done | bytes 786464 | tf_op jit(solution)/shard_map/ppermute | solution.py:226
  43.6 1.4 convert_add_fusion
  46.2 2.1 %collective-permute-start.2 = (bf16[2,2,24,768]{3,2,1,0:T(8,128)(2,1)S(1)}, bf16[2,2,24,768]{3,2,1,0:T(8,128)(2,1)S(1)}, u32[]{:S(2)}, u32[]{:S(2)}) collective-permute-start(bf16[2,2,24,768]{3,2,1,0:T(8,128)(2,1)S(1)} %pad_maximum_fusion.5), channel_id=1, source_target_pairs={{0,2},{1,3},{2,0},{3,1},{4,6},{5,7},{6,4},{7,5},{8,10},{9,11},{10,... | collective-permute-start | bytes 442376 | tf_op jit(solution)/shard_map/ppermute | solution.py:226
  48.2 5.8 %collective-permute-done.7 = bf16[2,6,128,128]{3,2,1,0:T(8,128)(2,1)S(1)} collective-permute-done((bf16[2,6,128,128]{3,2,1,0:T(8,128)(2,1)S(1)}, bf16[2,6,128,128]{3,2,1,0:T(8,128)(2,1)S(1)}, u32[]{:S(2)}, u32[]{:S(2)}) %collective-permute-start.7) | collective-permute-done | bytes 393248 | tf_op jit(solution)/shard_map/ppermute | solution.py:226
  54.1 2.2 %collective-permute-done.9 = bf16[2,6,128,128]{3,2,1,0:T(8,128)(2,1)S(1)} collective-permute-done((bf16[2,6,128,128]{3,2,1,0:T(8,128)(2,1)S(1)}, bf16[2,6,128,128]{3,2,1,0:T(8,128)(2,1)S(1)}, u32[]{:S(2)}, u32[]{:S(2)}) %collective-permute-start.9) | collective-permute-done | bytes 393248 | tf_op jit(solution)/shard_map/ppermute | solution.py:226
  56.8 4.5 %fusion = bf16[768,2048]{1,0:T(8,128)(2,1)} fusion(bf16[768,2048]{1,0:T(8,128)(2,1)} %param.16, f32[6,2048]{1,0:T(8,128)S(1)} %bitcast.77), kind=kLoop, calls=%fused_computation.1 | loop fusion | flops 4718592 | bytes 6340608 | tf_op jit(solution)/shard_map/convert_element_type | solution.py:304
  61.3 3.2 %collective-permute-done.10 = bf16[2,6,128,128]{3,2,1,0:T(8,128)(2,1)S(1)} collective-permute-done((bf16[2,6,128,128]{3,2,1,0:T(8,128)(2,1)S(1)}, bf16[2,6,128,128]{3,2,1,0:T(8,128)(2,1)S(1)}, u32[]{:S(2)}, u32[]{:S(2)}) %collective-permute-start.10) | collective-permute-done | bytes 393248 | tf_op jit(solution)/shard_map/ppermute | solution.py:226
  64.6 4.2 %collective-permute-start.11 = (bf16[1,6,128,128]{3,2,1,0:T(8,128)(2,1)S(1)}, bf16[1,6,128,128]{3,2,1,0:T(8,128)(2,1)S(1)}, u32[]{:S(2)}, u32[]{:S(2)}) collective-permute-start(bf16[1,6,128,128]{3,2,1,0:T(8,128)(2,1)S(1)} %dynamic-slice_convert_fusion.2), channel_id=1, source_target_pairs={{0,16},{1,17},{2,18},{3,19},{4,20},{5,21},{6,22},{7,23},{8,24},{9,... | collective-permute-start | bytes 589832 | tf_op jit(solution)/shard_map/ppermute | solution.py:226
  68.8 4.8 %convolution_convert_fusion = bf16[384,2048]{1,0:T(8,128)(2,1)} fusion(bf16[768,2048]{1,0:T(8,128)(2,1)} %fusion, bf16[2,384,768]{2,1,0:T(8,128)(2,1)} %bitcast.2, s32[]{:T(128)S(6)} %select_n.133), kind=kOutput, calls=%fused_computation.3 | convolution fusion | flops 1208745984 | bytes 5308420 | tf_op jit(solution)/shard_map/dot_general | solution.py:308
  77.3 8.6 %collective-permute-done.12 = bf16[1,6,128,128]{3,2,1,0:T(8,128)(2,1)S(1)} collective-permute-done((bf16[1,6,128,128]{3,2,1,0:T(8,128)(2,1)S(1)}, bf16[1,6,128,128]{3,2,1,0:T(8,128)(2,1)S(1)}, u32[]{:S(2)}, u32[]{:S(2)}) %collective-permute-start.12) | collective-permute-done | bytes 196640 | tf_op jit(solution)/shard_map/ppermute | solution.py:226
  86.9 10.1 %collective-permute-done.13 = bf16[2,6,128,128]{3,2,1,0:T(8,128)(2,1)S(1)} collective-permute-done((bf16[2,6,128,128]{3,2,1,0:T(8,128)(2,1)S(1)}, bf16[2,6,128,128]{3,2,1,0:T(8,128)(2,1)S(1)}, u32[]{:S(2)}, u32[]{:S(2)}) %collective-permute-start.13) | collective-permute-done | bytes 393248 | tf_op jit(solution)/shard_map/ppermute | solution.py:226
  98.3 3.4 %all-to-all-start.2 = ((bf16[8,24,768]{2,1,0:T(8,128)(2,1)}), bf16[8,24,768]{2,1,0:T(8,128)(2,1)S(1)}, u32[]{:S(2)}, u32[]{:S(2)}) async-start(bf16[8,24,768]{2,1,0:T(8,128)(2,1)} %bitcast.23), calls=%async_computation.2 | async-start | bytes 589824 | tf_op jit(solution)/shard_map/all_to_all | solution.py:353
  101.7 3.9 %add_convert_fusion = bf16[384,2048]{1,0:T(8,128)(2,1)S(1)} fusion(bf16[384,2048]{1,0:T(8,128)(2,1)} %collective-permute-done, bf16[768,2048]{1,0:T(8,128)(2,1)} %fusion, bf16[2,384,768]{2,1,0:T(8,128)(2,1)} %bitcast.2, s32[]{:T(128)S(6)} %select_n.132), kind=kOutput, calls=%fused_computation.2 | convolution fusion | flops 1211891712 | bytes 6881284 | tf_op jit(solution)/shard_map/dot_general | solution.py:309
  105.7 3.3 %all-to-all-done.2.trained = bf16[8,24,768]{2,1,0:T(8,128)(2,1)S(1)} async-done(((bf16[8,24,768]{2,1,0:T(8,128)(2,1)}), bf16[8,24,768]{2,1,0:T(8,128)(2,1)S(1)}, u32[]{:S(2)}, u32[]{:S(2)}) %all-to-all-start.2) | async-done | bytes 294944 | tf_op jit(solution)/shard_map/all_to_all | solution.py:353
  108.9 39.7 %all_to_all.15 = bf16[16,24,2048]{2,1,0:T(8,128)(2,1)S(1)} all-to-all(bf16[16,24,2048]{2,1,0:T(8,128)(2,1)S(1)} %bitcast.76), channel_id=1, replica_groups={{0,2,4,6,8,10,12,14,16,18,20,22,24,26,28,30},{1,3,5,7,9,11,13,15,17,19,..., dimensions={0} | all-to-all | bytes 3145728 | tf_op jit(solution)/shard_map/all_to_all | solution.py:312
  (68 shorter events, 13.0 us)
Async XLA Ops:
  0.6 56.0 %copy-start = (f32[6,16]{1,0:T(8,128)S(1)}, f32[6,16]{1,0:T(8,128)}, u32[]{:S(2)}) copy-start(f32[6,16]{1,0:T(8,128)} %param.17) | copy-start | bytes 1156
  0.6 2.8 %collective-permute-start.5 = (bf16[128,2048]{1,0:T(8,128)(2,1)}, bf16[128,2048]{1,0:T(8,128)(2,1)S(1)}, u32[]{:S(2)}, u32[]{:S(2)}) collective-permute-start(bf16[128,2048]{1,0:T(8,128)(2,1)} %cotangent_own.1), channel_id=1, source_target_pairs={{0,1},{1,0},{2,3},{3,2},{4,5},{5,4},{6,7},{7,6},{8,9},{9,8},{10,11... | collective-permute-start | bytes 1572872 | tf_op jit(solution)/shard_map/ppermute | solution.py:226
  1.2 2.3 %collective-permute-start.4 = (bf16[128,1536]{1,0:T(8,128)(2,1)}, bf16[128,1536]{1,0:T(8,128)(2,1)S(1)}, u32[]{:S(2)}, u32[]{:S(2)}) collective-permute-start(bf16[128,1536]{1,0:T(8,128)(2,1)} %hidden_own.1), channel_id=1, source_target_pairs={{0,1},{1,0},{2,3},{3,2},{4,5},{5,4},{6,7},{7,6},{8,9},{9,8},{10,11... | collective-permute-start | bytes 1179656 | tf_op jit(solution)/shard_map/ppermute | solution.py:226
  5.5 9.4 %copy-start.9 = (s32[4,8,8]{2,1,0:T(8,128)S(1)}, s32[4,8,8]{2,1,0:T(8,128)}, u32[]{:S(2)}) copy-start(s32[4,8,8]{2,1,0:T(8,128)} %param.20) | copy-start | bytes 3076
  5.5 9.6 %copy-start.10 = (f32[4,8,8]{2,1,0:T(8,128)S(1)}, f32[4,8,8]{2,1,0:T(8,128)}, u32[]{:S(2)}) copy-start(f32[4,8,8]{2,1,0:T(8,128)} %param.21) | copy-start | bytes 3076
  5.5 9.7 %copy-start.1 = (bf16[4,8,8,1536]{3,2,1,0:T(8,128)(2,1)S(1)}, bf16[4,8,8,1536]{3,2,1,0:T(8,128)(2,1)}, u32[]{:S(2)}) copy-start(bf16[4,8,8,1536]{3,2,1,0:T(8,128)(2,1)} %param.19) | copy-start | bytes 2359300
  5.5 9.7 %copy-start.4 = (s32[16]{0:T(128)S(1)}, s32[16]{0:T(128)}, u32[]{:S(2)}) copy-start(s32[16]{0:T(128)} %refs_0_.1) | copy-start | bytes 196
  10.5 27.0 %collective-permute-start.6 = (bf16[2,2,6,128,128]{4,3,2,0,1:T(8,128)(2,1)S(1)}, bf16[2,2,6,128,128]{4,3,2,0,1:T(8,128)(2,1)}, u32[]{:S(2)}, u32[]{:S(2)}) collective-permute-start(bf16[2,2,6,128,128]{4,3,2,0,1:T(8,128)(2,1)S(1)} %copy.18), channel_id=1, source_target_pairs={{0,2},{1,3},{2,0},{3,1},{4,6},{5,7},{6,4},{7,5},{8,10},{9,11},{10,... | collective-permute-start | bytes 2359304 | tf_op jit(solution)/shard_map/ppermute | solution.py:226
  13.4 30.2 %collective-permute-start.8 = (bf16[2,2,6,128,128]{4,3,2,1,0:T(8,128)(2,1)}, bf16[2,2,6,128,128]{4,3,2,1,0:T(8,128)(2,1)}, u32[]{:S(2)}, u32[]{:S(2)}) collective-permute-start(bf16[2,2,6,128,128]{4,3,2,1,0:T(8,128)(2,1)} %get-tuple-element.13), channel_id=1, source_target_pairs={{0,4},{1,5},{2,6},{3,7},{4,0},{5,1},{6,2},{7,3},{8,12},{9,13},{10,... | collective-permute-start | bytes 2359304 | tf_op jit(solution)/shard_map/ppermute | solution.py:226
  17.4 51.4 %all-to-all-start = ((bf16[32,24,768]{2,1,0:T(8,128)(2,1)}), bf16[32,24,768]{2,1,0:T(8,128)(2,1)}, u32[]{:S(2)}, u32[]{:S(2)}) async-start(bf16[32,24,768]{2,1,0:T(8,128)(2,1)} %bitcast.1), calls=%async_computation | async-start | bytes 2359296 | tf_op jit(solution)/shard_map/all_to_all | solution.py:253
  22.5 22.7 %collective-permute-start.1 = (bf16[1,2,24,768]{3,2,1,0:T(8,128)(2,1)S(1)}, bf16[1,2,24,768]{3,2,1,0:T(8,128)(2,1)S(1)}, u32[]{:S(2)}, u32[]{:S(2)}) collective-permute-start(bf16[1,2,24,768]{3,2,1,0:T(8,128)(2,1)S(1)} %dynamic-slice_bitcast_fusion), channel_id=1, source_target_pairs={{0,1},{1,0},{2,3},{3,2},{4,5},{5,4},{6,7},{7,6},{8,9},{9,8},{10,11... | collective-permute-start | bytes 221192 | tf_op jit(solution)/shard_map/ppermute | solution.py:226
  39.0 15.0 %collective-permute-start.7 = (bf16[2,6,128,128]{3,2,1,0:T(8,128)(2,1)S(1)}, bf16[2,6,128,128]{3,2,1,0:T(8,128)(2,1)S(1)}, u32[]{:S(2)}, u32[]{:S(2)}) collective-permute-start(bf16[2,6,128,128]{3,2,1,0:T(8,128)(2,1)S(1)} %fusion.11), channel_id=1, source_target_pairs={{0,4},{1,5},{2,6},{3,7},{4,0},{5,1},{6,2},{7,3},{8,12},{9,13},{10,... | collective-permute-start | bytes 1179656 | tf_op jit(solution)/shard_map/ppermute | solution.py:226
  45.1 11.2 %collective-permute-start.9 = (bf16[2,6,128,128]{3,2,1,0:T(8,128)(2,1)S(1)}, bf16[2,6,128,128]{3,2,1,0:T(8,128)(2,1)S(1)}, u32[]{:S(2)}, u32[]{:S(2)}) collective-permute-start(bf16[2,6,128,128]{3,2,1,0:T(8,128)(2,1)S(1)} %fusion.12), channel_id=1, source_target_pairs={{0,2},{1,3},{2,0},{3,1},{4,6},{5,7},{6,4},{7,5},{8,10},{9,11},{10,... | collective-permute-start | bytes 1179656 | tf_op jit(solution)/shard_map/ppermute | solution.py:226
  46.2 15.1 %collective-permute-start.2 = (bf16[2,2,24,768]{3,2,1,0:T(8,128)(2,1)S(1)}, bf16[2,2,24,768]{3,2,1,0:T(8,128)(2,1)S(1)}, u32[]{:S(2)}, u32[]{:S(2)}) collective-permute-start(bf16[2,2,24,768]{3,2,1,0:T(8,128)(2,1)S(1)} %pad_maximum_fusion.5), channel_id=1, source_target_pairs={{0,2},{1,3},{2,0},{3,1},{4,6},{5,7},{6,4},{7,5},{8,10},{9,11},{10,... | collective-permute-start | bytes 442376 | tf_op jit(solution)/shard_map/ppermute | solution.py:226
  56.5 7.9 %collective-permute-start.10 = (bf16[2,6,128,128]{3,2,1,0:T(8,128)(2,1)S(1)}, bf16[2,6,128,128]{3,2,1,0:T(8,128)(2,1)S(1)}, u32[]{:S(2)}, u32[]{:S(2)}) collective-permute-start(bf16[2,6,128,128]{3,2,1,0:T(8,128)(2,1)S(1)} %fusion.13), channel_id=1, source_target_pairs={{0,8},{1,9},{2,10},{3,11},{4,12},{5,13},{6,14},{7,15},{8,0},{9,1},... | collective-permute-start | bytes 1179656 | tf_op jit(solution)/shard_map/ppermute | solution.py:226
  64.6 9.8 %collective-permute-start.11 = (bf16[1,6,128,128]{3,2,1,0:T(8,128)(2,1)S(1)}, bf16[1,6,128,128]{3,2,1,0:T(8,128)(2,1)S(1)}, u32[]{:S(2)}, u32[]{:S(2)}) collective-permute-start(bf16[1,6,128,128]{3,2,1,0:T(8,128)(2,1)S(1)} %dynamic-slice_convert_fusion.2), channel_id=1, source_target_pairs={{0,16},{1,17},{2,18},{3,19},{4,20},{5,21},{6,22},{7,23},{8,24},{9,... | collective-permute-start | bytes 589832 | tf_op jit(solution)/shard_map/ppermute | solution.py:226
  68.8 5.6 %copy-start.7 = (f32[6,128,128]{2,1,0:T(8,128)S(1)}, f32[6,128,128]{2,1,0:T(8,128)}, u32[]{:S(2)}) copy-start(f32[6,128,128]{2,1,0:T(8,128)} %param.15) | copy-start | bytes 1179652
  68.8 5.6 %copy-start.8 = (f32[6,128,128]{2,1,0:T(8,128)S(1)}, f32[6,128,128]{2,1,0:T(8,128)}, u32[]{:S(2)}) copy-start(f32[6,128,128]{2,1,0:T(8,128)} %param.14) | copy-start | bytes 1179652
  73.5 28.2 %collective-permute-start = (bf16[384,2048]{1,0:T(8,128)(2,1)}, bf16[384,2048]{1,0:T(8,128)(2,1)}, u32[]{:S(2)}, u32[]{:S(2)}) collective-permute-start(bf16[384,2048]{1,0:T(8,128)(2,1)} %convolution_convert_fusion), channel_id=1, source_target_pairs={{0,1},{1,0},{2,3},{3,2},{4,5},{5,4},{6,7},{7,6},{8,9},{9,8},{10,11... | collective-permute-start | bytes 4718600 | tf_op jit(solution)/shard_map/ppermute | solution.py:226
  74.8 11.3 %copy-start.5 = (f32[6,128,128]{2,1,0:T(8,128)}, f32[6,128,128]{2,1,0:T(8,128)S(1)}, u32[]{:S(2)}) copy-start(f32[6,128,128]{2,1,0:T(8,128)S(1)} %get-tuple-element.17) | copy-start | bytes 1179652
  74.9 11.0 %collective-permute-start.12 = (bf16[1,6,128,128]{3,2,1,0:T(8,128)(2,1)S(1)}, bf16[1,6,128,128]{3,2,1,0:T(8,128)(2,1)S(1)}, u32[]{:S(2)}, u32[]{:S(2)}) collective-permute-start(bf16[1,6,128,128]{3,2,1,0:T(8,128)(2,1)S(1)} %fusion.16), channel_id=1, source_target_pairs={{0,16},{1,17},{2,18},{3,19},{4,20},{5,21},{6,22},{7,23},{8,24},{9,... | collective-permute-start | bytes 589832 | tf_op jit(solution)/shard_map/ppermute | solution.py:226
  76.1 9.9 %collective-permute-start.3 = (bf16[4,2,24,768]{3,2,1,0:T(8,128)(2,1)S(1)}, bf16[4,2,24,768]{3,2,1,0:T(8,128)(2,1)S(1)}, u32[]{:S(2)}, u32[]{:S(2)}) collective-permute-start(bf16[4,2,24,768]{3,2,1,0:T(8,128)(2,1)S(1)} %pad_maximum_fusion.4), channel_id=1, source_target_pairs={{0,4},{1,5},{2,6},{3,7},{4,0},{5,1},{6,2},{7,3},{8,12},{9,13},{10,... | collective-permute-start | bytes 884744 | tf_op jit(solution)/shard_map/ppermute | solution.py:226
  85.9 11.1 %collective-permute-start.13 = (bf16[2,6,128,128]{3,2,1,0:T(8,128)(2,1)S(1)}, bf16[2,6,128,128]{3,2,1,0:T(8,128)(2,1)S(1)}, u32[]{:S(2)}, u32[]{:S(2)}) collective-permute-start(bf16[2,6,128,128]{3,2,1,0:T(8,128)(2,1)S(1)} %pad_maximum_fusion.3), channel_id=1, source_target_pairs={{0,8},{1,9},{2,10},{3,11},{4,12},{5,13},{6,14},{7,15},{8,0},{9,1},... | collective-permute-start | bytes 1179656 | tf_op jit(solution)/shard_map/ppermute | solution.py:226
  98.3 10.6 %all-to-all-start.2 = ((bf16[8,24,768]{2,1,0:T(8,128)(2,1)}), bf16[8,24,768]{2,1,0:T(8,128)(2,1)S(1)}, u32[]{:S(2)}, u32[]{:S(2)}) async-start(bf16[8,24,768]{2,1,0:T(8,128)(2,1)} %bitcast.23), calls=%async_computation.2 | async-start | bytes 589824 | tf_op jit(solution)/shard_map/all_to_all | solution.py:353
  (3 other events, 7.6 us)

commit v2 on v1

v2 whole, which is shorter than its diff:
```python
import jax
import jax.numpy as jnp
from jax import lax
from jax.experimental import pallas as pl
from jax.experimental.pallas import tpu as pltpu
from jax.sharding import PartitionSpec as P

learn_rate = 0.05
beta_first = 0.9
beta_second = 0.95
correct_first = 1.0 - 0.9**10
correct_second = 1.0 - 0.95**10
decay_rate = 0.1
adam_epsilon = 1e-08
quant_range = 448.0

F32 = jnp.float32
BF16 = jnp.bfloat16
PARAMS = pltpu.CompilerParams(vmem_limit_bytes=16 * 2**20)


def optimizer(gradient, master, moment_first, moment_second):
    first_moment = beta_first * moment_first + (1.0 - beta_first) * gradient
    second_moment = beta_second * moment_second + (1.0 - beta_second) * gradient * gradient
    update = (
        first_moment / correct_first / (jnp.sqrt(second_moment / correct_second) + adam_epsilon)
    )
    return master - learn_rate * (update + decay_rate * master)


def update_kernel(master, moment_first, moment_second, *rest):
    parts, new_master, fresh = rest[:-2], rest[-2], rest[-1]
    for block in range(master.shape[0]):
        gradient = parts[0][block].astype(F32)
        for part in parts[1:]:
            gradient = gradient + part[block].astype(F32)
        weights = optimizer(gradient, master[block], moment_first[block], moment_second[block])
        new_master[block] = weights
        largest = jnp.max(jnp.abs(weights), axis=(0, 1), keepdims=True)
        scale = (largest + 1e-06) / quant_range
        quantized = (weights / scale).astype(BF16)
        fresh[block] = (quantized.astype(F32) * scale).astype(BF16)


def in_hbm(*arrays):
    return [pltpu.with_memory_space_constraint(array, pltpu.HBM) for array in arrays]


def vmem(count):
    return [pl.BlockSpec(memory_space=pltpu.VMEM)] * count


def pack_kernel(
    steps,
    capacity,
    depth,
    placement,
    routing,
    gate_weight,
    hidden,
    packed,
    gates_trained,
    rows_trained,
):
    rows, topk = routing.shape
    entries = rows * topk
    step_entries = entries // steps
    experts = placement.shape[0]
    chips = experts // depth
    pair_slots = steps * capacity

    def iota(shape, axis):
        return lax.broadcasted_iota(jnp.int32, shape, axis)

    def ones(mask):
        return jnp.where(mask, 1.0, 0.0).astype(BF16)

    spread = ones(iota((topk, entries), 1) % topk == iota((topk, entries), 0))
    mine = iota((rows, entries), 1) // topk == iota((rows, entries), 0)

    def along(values):
        return jnp.where(mine, jnp.dot(values, spread, preferred_element_type=F32), 0.0)

    routed = jnp.sum(along(routing[...].astype(F32).astype(BF16)), axis=0, keepdims=True)
    routed = routed.astype(jnp.int32)
    named = ones(iota((experts, entries), 0) == routed)
    same = lax.dot_general(named, named, (((0,), (0,)), ((), ())), preferred_element_type=F32)
    lane, line = iota((entries, entries), 1), iota((entries, entries), 0)
    earlier = (lane // step_entries == line // step_entries) & (line // topk < lane // topk)
    place = jnp.sum(jnp.where(earlier, same, 0.0), axis=0, keepdims=True).astype(jnp.int32)
    pair = jnp.zeros_like(routed)
    for expert in range(experts):
        pair = jnp.where(routed == expert, placement[expert], pair)
    entry = lax.broadcasted_iota(jnp.int32, (1, entries), 1)
    step_slot = entry // step_entries * capacity + place
    chip = pair % chips * depth
    slot = (chip + pair // chips) * pair_slots + step_slot
    slots = experts * pair_slots
    slot_line = lax.broadcasted_iota(jnp.int32, (slots, entries), 0)
    onehot = jnp.where(slot_line == slot, 1.0, 0.0).astype(BF16)
    width = hidden.shape[1]
    packed[:, :width] = jnp.dot(
        onehot, hidden[...], preferred_element_type=F32
    ).astype(BF16)
    onehot_trained = ones((iota((pair_slots, entries), 0) == step_slot) & (routed == 0))
    rows_trained[...] = jnp.dot(
        onehot_trained, hidden[...], preferred_element_type=F32
    ).astype(BF16)
    weight = gate_weight[...]
    high = weight.astype(BF16)
    rest = (weight - high.astype(F32)).astype(BF16)
    both = jnp.concatenate([along(high), along(rest)], axis=0).astype(BF16)
    over_entries = (((1,), (1,)), ((), ()))
    gates_trained[...] = lax.dot_general(
        both, onehot_trained, over_entries, preferred_element_type=F32
    ).astype(BF16)
    counted = jnp.where(routed == 0, 0.0, both.astype(F32)).astype(BF16)
    unused = jnp.zeros((packed.shape[1] - width - 2 * rows, entries), BF16)
    packed[:, width:] = lax.dot_general(
        onehot,
        jnp.concatenate([counted, unused], axis=0),
        over_entries,
        preferred_element_type=F32,
    ).astype(BF16)


def gradient_kernel(
    device_ref, hidden_own, hidden_other, cotangent_own, cotangent_other, *rest
):
    outs, hidden_across, cotangent = rest[:8], rest[8], rest[9]
    device = device_ref[0]
    tokens = hidden_own.shape[0]
    hidden_across[:, :tokens] = hidden_own[...].T
    hidden_across[:, tokens:] = hidden_other[...].T
    cotangent[:tokens] = cotangent_own[...]
    cotangent[tokens:] = cotangent_other[...]
    highs, blocks, side, _ = outs[0].shape
    column_blocks = cotangent.shape[1] // side
    wide = 2 if blocks % 2 == 0 else 1
    core = device % 2
    bit_x = device // 2 % 2
    bit_y = device // 4 % 2
    for part in range(4):
        for half in range(2):
            first, second = part < 2, part % 2 == 0
            over_x, over_y = (first, second) if half == 0 else (second, first)
            x = 1 - bit_x if over_x else bit_x
            y = 1 - bit_y if over_y else bit_y
            out = outs[4 * half + part]
            for high in range(highs):
                dest = (((high + half * highs) * 2 + y) * 2 + x) * 2 + core
                for at in range(0, blocks, wide):
                    block = dest * blocks + at
                    row = pl.multiple_of(block // column_blocks * side, side)
                    column = pl.multiple_of(block % column_blocks * side, side)
                    product = jnp.dot(
                        hidden_across[pl.ds(row, side), :],
                        cotangent[:, pl.ds(column, wide * side)],
                        preferred_element_type=F32,
                    ).astype(out.dtype)
                    for piece in range(wide):
                        out[high, at + piece] = product[:, piece * side : (piece + 1) * side]


def first_sum_kernel(arrived_a, held_a, arrived_b, held_b, out_a, out_b):
    out_a[...] = (arrived_a[...].astype(F32) + held_a[...].astype(F32)).astype(BF16)
    out_b[...] = (arrived_b[...].astype(F32) + held_b[...].astype(F32)).astype(BF16)


def second_sum_kernel(floor_ref, *rest):
    parts, outs, total = rest[:6], rest[6:10], rest[10]
    highs = parts[0].shape[0]
    for half in range(2):
        one, two, three = parts[3 * half : 3 * half + 3]
        total[half * highs : (half + 1) * highs] = (
            one[...].astype(F32) + two[...].astype(F32) + three[...].astype(F32)
        )
    for flip, out in zip((3, 1, 2, 0), outs, strict=True):
        out[...] = total[floor_ref[0] ^ flip].astype(out.dtype)


def third_sum_kernel(arrived, held, out):
    out[...] = (arrived[...].astype(F32) + held[...].astype(F32)).astype(BF16)


def expert_partial(rows, weights, scales):
    blocks, side = scales.shape[0], weights.shape[0] // scales.shape[0]
    scaled = [
        (weights[at * side : (at + 1) * side].astype(F32) * scales[at]).astype(BF16)
        for at in range(blocks)
    ]
    scaled = jnp.concatenate(scaled, axis=0)
    return jnp.dot(rows, scaled, preferred_element_type=F32).astype(BF16)


def expert_kernel(
    core_ref, rows, rows_trained, weights, weights_other, scales, scales_other, out
):
    half, wide = weights.shape
    step = pl.program_id(0)
    total = 0.0
    for core, kept, scale in (
        (core_ref[0], weights, scales),
        (1 - core_ref[0], weights_other, scales_other),
    ):
        at = pl.ds(pl.multiple_of(core * half, half), half)
        total = total + expert_partial(rows[:, at], kept, scale).astype(F32)
    chips = out.shape[0]
    count = rows.shape[0] // chips
    for chip in range(chips):
        out[chip, :count, pl.ds(pl.multiple_of(step * wide, wide), wide)] = total[
            chip * count : (chip + 1) * count
        ].astype(out.dtype)

    @pl.when(step == 0)
    def _():
        columns = wide * pl.num_programs(0)
        for chip in range(chips):
            out[chip, :count, columns:] = rows[chip * count : (chip + 1) * count, 2 * half :]
            out[chip, count:, : 2 * half] = rows_trained[...]
            out[chip, count:, 2 * half :] = jnp.zeros(
                (out.shape[1] - count, out.shape[2] - 2 * half), out.dtype
            )


def trained_kernel(device_ref, plane, depth, column_blocks, *rest):
    given, weights = rest[:2], rest[2 : 2 + depth]
    out, rows = rest[2 + depth :]
    device = device_ref[0]
    blocks, side, _ = weights[0].shape
    inner = device % plane
    floor = device // plane
    chips, count, _ = given[0].shape
    for row_block in range(rows.shape[0]):
        at = slice(row_block * side, (row_block + 1) * side)
        rows[row_block] = jnp.concatenate(
            [part[chip, :, at] for part in given for chip in range(chips)], axis=0
        )
    for at in range(blocks):
        total = jnp.zeros((rows.shape[1], side), F32)
        for flip in range(depth):
            block = ((floor ^ flip) * plane + inner) * blocks + at
            row_block = block // column_blocks
            total = total + jnp.dot(rows[row_block], weights[flip][at], preferred_element_type=F32)
        for core in range(2):
            for chip in range(chips):
                top = (core * chips + chip) * count
                out[2 * chip + (device % 2 ^ core), :, at * side : (at + 1) * side] = total[
                    top : top + count
                ].astype(BF16)


def mix_kernel(depth, plane_slots, floor_ref, returned, *outs):
    count, columns = outs[0].shape

    def of_chips(at):
        return jnp.concatenate(
            [returned[chip, :plane_slots, at] for chip in range(returned.shape[0])], axis=0
        )

    gates = of_chips(slice(columns, None)).astype(F32)
    slot = lax.broadcasted_iota(jnp.int32, gates.shape, 0)
    plane = slot // (plane_slots // depth) % depth
    mine = [
        jnp.where(plane == (floor_ref[0] ^ flip), gates, 0.0).astype(BF16) for flip in range(depth)
    ]
    wide = 512
    for column in range(0, columns, wide):
        at = slice(column, column + wide)
        rows = of_chips(at)
        for flip, out in enumerate(outs):
            mixed = lax.dot_general(
                mine[flip], rows, (((0,), (0,)), ((), ())), preferred_element_type=F32
            )
            out[:, at] = (mixed[:count] + mixed[count : 2 * count]).astype(out.dtype)


def combine_kernel(depth, side, gates_trained, *rest):
    mixed, trained, out = rest[:depth], rest[depth], rest[depth + 1]
    peers, _, width = trained.shape
    columns = out.shape[1]
    blocks = width // side
    count = out.shape[0]
    wide = 4
    for column in range(0, columns // side, wide):
        fresh = []
        for place in range(column, column + wide):
            total = None
            for number in range(place, peers * blocks, columns // side):
                peer, block = divmod(number, blocks)
                piece = trained[peer, :, block * side : (block + 1) * side].astype(F32)
                total = piece if total is None else total + piece
            fresh.append(total.astype(BF16))
        at = slice(column * side, (column + wide) * side)
        both = jnp.dot(
            gates_trained[...], jnp.concatenate(fresh, axis=1), preferred_element_type=F32
        )
        total = both[:count] + both[count:]
        for part in mixed:
            total = total + part[:, at].astype(F32)
        out[:, at] = total.astype(out.dtype)


def local(
    learn_hidden,
    learn_cotangent,
    master,
    moment_first,
    moment_second,
    resident_weight,
    resident_scale,
    placement,
    decode_hidden,
    routing,
    gate_weight,
):
    devices = lax.axis_size("dp")
    device = lax.axis_index("dp")
    device_ref = device.astype(jnp.int32).reshape(1)
    blocks, side = master.shape[:2]
    hidden_width = learn_hidden.shape[1]
    columns = learn_cotangent.shape[1]
    row_blocks = hidden_width // side
    column_blocks = columns // side
    tokens = learn_hidden.shape[0]
    steps, step_rows, topk = routing.shape
    experts = placement.shape[0]
    capacity = min(step_rows, step_rows * topk // experts + 2)
    entries = steps * step_rows * topk
    pair_slots = steps * capacity
    slots = experts * pair_slots
    half = hidden_width // 2

    def flip(array, mask):
        return lax.ppermute(array, "dp", [(i, i ^ mask) for i in range(devices)])

    def bit(number):
        return device // 2**number % 2

    def after(array, *others):
        return lax.optimization_barrier((array, others))[0]

    def pick(array, index, axis):
        return lax.dynamic_index_in_dim(array, index, axis, keepdims=False)

    plane = 1
    while plane * blocks % column_blocks:
        plane *= 2
    depth = devices // plane
    chips = plane // 2
    floor_ref = (device // plane).astype(jnp.int32).reshape(1)
    row_count = steps * step_rows
    gate_lanes = -(-2 * row_count // 128) * 128
    smem = pl.BlockSpec(memory_space=pltpu.SMEM)

    packed, gates_trained, rows_trained = pl.pallas_call(
        lambda *refs: pack_kernel(steps, capacity, depth, *refs),
        out_shape=(
            pltpu.HBM((slots, hidden_width + gate_lanes), BF16),
            jax.ShapeDtypeStruct((2 * steps * step_rows, pair_slots), BF16),
            jax.ShapeDtypeStruct((pair_slots, hidden_width), BF16),
        ),
        in_specs=[smem] + vmem(3),
        out_specs=tuple(vmem(3)),
        compiler_params=PARAMS,
    )(
        placement,
        *in_hbm(
            routing.reshape(steps * step_rows, topk),
            gate_weight.reshape(steps * step_rows, topk),
            decode_hidden.reshape(entries, hidden_width),
        ),
    )
    hidden_other, cotangent_other = flip(learn_hidden, 1), flip(learn_cotangent, 1)
    same_core = [
        [z * plane + chip * 2 + core for chip in range(chips) for z in range(depth)]
        for core in range(2)
    ]
    received = lax.all_to_all(
        after(packed, hidden_other, cotangent_other).reshape(
            experts, pair_slots, hidden_width + gate_lanes
        ),
        "dp",
        split_axis=0,
        concat_axis=0,
        tiled=True,
        axis_index_groups=same_core,
    ).reshape(slots, hidden_width + gate_lanes)

    highs = devices // 16
    part = jax.ShapeDtypeStruct((highs, blocks, side, side), BF16)
    parts = pl.pallas_call(
        gradient_kernel,
        out_shape=(pltpu.HBM(part.shape, BF16),) * 8,
        in_specs=[smem] + vmem(4),
        out_specs=tuple(vmem(8)),
        scratch_shapes=[
            pltpu.VMEM((hidden_width, 2 * tokens), BF16),
            pltpu.VMEM((2 * tokens, columns), BF16),
        ],
        compiler_params=PARAMS,
    )(
        device_ref,
        *in_hbm(after(learn_hidden, packed), hidden_other, learn_cotangent, cotangent_other),
    )
    both_a, first_a, second_a, stay_a, both_b, first_b, second_b, stay_b = parts
    both_a, both_b = flip(both_a, 2), flip(both_b, 4)
    first_a, first_b = flip(first_a, 2), flip(first_b, 4)
    weights_other = flip(after(resident_weight, hidden_other, cotangent_other), 1)
    scales_other = flip(resident_scale, 1)
    second_a = after(second_a, weights_other)
    second_a, second_b = pl.pallas_call(
        first_sum_kernel,
        out_shape=(pltpu.HBM(part.shape, BF16),) * 2,
        in_specs=vmem(4),
        out_specs=tuple(vmem(2)),
        compiler_params=PARAMS,
    )(both_a, second_a, both_b, second_b)
    sums = second_a, second_b
    second_a, second_b = flip(second_a, 4), flip(second_b, 2)

    plane_slots = depth * pair_slots
    sent_shape = (chips, plane_slots + pair_slots, columns + gate_lanes)

    def expert_sum(rows):
        wide = 512
        weight_spec = pl.BlockSpec((half, wide), lambda i, core: (0, i))
        scale_spec = pl.BlockSpec((row_blocks // 2, 1, wide), lambda i, core: (0, 0, i))
        return pl.pallas_call(
            expert_kernel,
            out_shape=pltpu.HBM(sent_shape, BF16),
            grid_spec=pltpu.PrefetchScalarGridSpec(
                num_scalar_prefetch=1,
                grid=(columns // wide,),
                in_specs=[
                    pl.BlockSpec((slots, hidden_width + gate_lanes), lambda i, core: (0, 0)),
                    pl.BlockSpec((pair_slots, hidden_width), lambda i, core: (0, 0)),
                    weight_spec,
                    weight_spec,
                    scale_spec,
                    scale_spec,
                ],
                out_specs=pl.BlockSpec(sent_shape, lambda i, core: (0, 0, 0)),
            ),
            compiler_params=PARAMS,
        )(
            bit(0).astype(jnp.int32).reshape(1),
            rows,
            rows_trained,
            resident_weight,
            weights_other,
            *(
                jnp.repeat(scales, side, axis=1)[:, None, :]
                for scales in (resident_scale, scales_other)
            ),
        )

    block_shape = (blocks, side, side)
    if highs == 2:
        expert_out = expert_sum(after(received, sums, first_a, first_b))
        expert_out = after(expert_out, second_a, second_b)
        far, near, across, own = pl.pallas_call(
            second_sum_kernel,
            out_shape=(
                pltpu.HBM(block_shape, BF16),
                pltpu.HBM(block_shape, BF16),
                pltpu.HBM(block_shape, F32),
                pltpu.HBM(block_shape, F32),
            ),
            in_specs=[smem] + vmem(6),
            out_specs=tuple(vmem(4)),
            scratch_shapes=[pltpu.VMEM((4,) + block_shape, F32)],
            compiler_params=PARAMS,
        )(
            (device // 8).astype(jnp.int32).reshape(1),
            stay_a,
            first_a,
            second_a,
            stay_b,
            first_b,
            second_b,
        )
        far, near = flip(far, 8), flip(near, 8)
        across = pl.pallas_call(
            third_sum_kernel,
            out_shape=jax.ShapeDtypeStruct(block_shape, BF16),
            in_specs=vmem(2),
            out_specs=vmem(1)[0],
            compiler_params=PARAMS,
        )(far, across)
        gradient = [own, near, flip(across, 16)]
    else:
        expert_out = expert_sum(received)
        sums = [
            sum(piece.astype(F32) for piece in pieces)
            for pieces in ((stay_a, first_a, second_a), (stay_b, first_b, second_b))
        ]
        total = jnp.concatenate(sums, axis=0)
        number = 3
        while total.shape[0] > 1:
            split = total.reshape((-1, 2) + block_shape)
            sent = pick(split, 1 - bit(number), 1).astype(BF16)
            total = pick(split, bit(number), 1) + flip(sent, 2**number).astype(F32)
            number += 1
        gradient = [total[0]]
    new_master, fresh = pl.pallas_call(
        update_kernel,
        out_shape=(
            jax.ShapeDtypeStruct(block_shape, F32),
            jax.ShapeDtypeStruct(block_shape, BF16),
        ),
        in_specs=vmem(3 + len(gradient)),
        out_specs=tuple(vmem(2)),
        compiler_params=PARAMS,
    )(master, moment_first, moment_second, *gradient)

    same_core = [
        [z * plane + chip * 2 + core for chip in range(chips)]
        for z in range(depth)
        for core in range(2)
    ]
    returned = lax.all_to_all(
        expert_out, "dp", split_axis=0, concat_axis=0, tiled=True, axis_index_groups=same_core
    )
    rows_trained = returned[:, plane_slots:, :hidden_width]
    rows_other = flip(rows_trained, 1)
    mixed = pl.pallas_call(
        lambda *refs: mix_kernel(depth, plane_slots, *refs),
        out_shape=(jax.ShapeDtypeStruct((row_count, columns), F32),)
        + (jax.ShapeDtypeStruct((row_count, columns), BF16),) * (depth - 1),
        in_specs=[smem] + vmem(1),
        out_specs=tuple(vmem(depth)),
        compiler_params=PARAMS,
    )(floor_ref, after(returned, fresh))
    mixed = [mixed[0]] + [flip(mixed[z], z * plane) for z in range(1, depth)]

    held = {0: fresh}
    mask = depth // 2
    while mask:
        for key in list(held):
            held[key | mask] = flip(held[key], mask * plane)
        mask //= 2
    trained = pl.pallas_call(
        lambda device_ref, *refs: trained_kernel(device_ref, plane, depth, column_blocks, *refs),
        out_shape=pltpu.HBM((plane, pair_slots, blocks * side), BF16),
        in_specs=[smem] + vmem(2 + depth),
        out_specs=vmem(1)[0],
        scratch_shapes=[pltpu.VMEM((row_blocks, plane * pair_slots, side), BF16)],
        compiler_params=PARAMS,
    )(device_ref, after(rows_trained, mixed[0]), rows_other, *[held[z] for z in range(depth)])
    planes = [[z * plane + i for i in range(plane)] for z in range(depth)]
    trained = lax.all_to_all(
        trained, "dp", split_axis=0, concat_axis=0, tiled=True, axis_index_groups=planes
    )
    decoded = pl.pallas_call(
        lambda *refs: combine_kernel(depth, side, *refs),
        out_shape=jax.ShapeDtypeStruct((row_count, columns), BF16),
        in_specs=vmem(2 + depth),
        out_specs=vmem(1)[0],
        compiler_params=PARAMS,
    )(gates_trained, *mixed, trained)
    return (decoded.reshape(steps, step_rows, columns), new_master)


def solution(mesh):
    return jax.shard_map(
        local,
        mesh=mesh,
        in_specs=(
            P(("groups", "dp"), None),
            P(("groups", "dp"), None),
            P("dp", None, None),
            P("dp", None, None),
            P("dp", None, None),
            P("dp", None),
            P("dp", None),
            P(),
            P(None, ("groups", "dp"), None, None),
            P(None, ("groups", "dp"), None),
            P(None, ("groups", "dp"), None),
        ),
        out_specs=(P(None, ("groups", "dp"), None), P(("groups", "dp"), None, None)),
        check_vma=False,
    )
```

time: 150 us -> 123 us (0.82)
  blocking collectives: 39.7 us -> 0 us
  Pallas kernels: 9.41 us -> 22.3 us
  starting transfers between devices: 23.6 us -> 33.7 us
  other arithmetic: 9.38 us -> 0 us
  matrix products: 8.68 us -> 0 us
  local copies, waits for them, and re-layouts: 4.39 us -> 9.46 us
  waiting for transfers between devices: 53.6 us -> 56.3 us
    all_to_all x1 -> x0, blocking collectives: 39.7 us -> none  [local(): lax.all_to_all(expert_out.reshape(experts, pair_slots, columns), 'dp', sp...]
    pallas_call x3 -> x9, Pallas kernels: 8.23 us -> 21.1 us  [the longest x1 6.34 us: expert_sum(): pl.pallas_call(expert_kernel, out_shape=pltpu.HBM(sent_shape, BF16), grid...]
    dot_general x2 -> x0, matrix products: 8.68 us -> none  [the longest x1 4.76 us: local(): jnp.dot(pick(received, 1 - core, 0), weights, preferred_element_type=F32)]
    all_to_all x2 -> x3, starting transfers between devices: 7.5 us -> 15.8 us  [the longest x1 7.97 us: local(): lax.all_to_all(after(packed, hidden_other, cotangent_other).reshape(exper...]
    unnamed x24 -> x36, local copies, waits for them, and re-layouts: 2.17 us -> 9.3 us
    ppermute x14 -> x20, waiting for transfers between devices: 50.3 us -> 56.3 us  [flip(): return lax.ppermute(array, 'dp', [(i, i ^ mask) for i in range(devices)])]
    convert_element_type x1 -> x0, other arithmetic: 4.47 us -> none  [local(): weights = (resident_weight.reshape(row_blocks // 2, side, columns).astype...]
    all_to_all x2 -> x3, waiting for transfers between devices: 3.28 us -> 0.01 us  [the longest x1 0.01 us: local(): lax.all_to_all(after(packed, hidden_other, cotangent_other).reshape(exper...]
  transfers between devices with their start and end apart: 16 -> 23, of which waited for: 10 -> 11; matrix products, arithmetic and copies ran while one was open for 14% -> 0% of each run, Pallas kernels for 2% -> 16%
where the time goes in v2:
time: 123 us
  waiting for transfers between devices  56.3 us (46%)
  starting transfers between devices  33.7 us (27%)
  Pallas kernels  22.3 us (18%)
  local copies, waits for them, and re-layouts  9.46 us (8%)
    ppermute x20, waiting for transfers between devices, flip(): return lax.ppermute(array, 'dp', [(i, i ^ mask) for i in range(devices)])  56.3 us
    ppermute x20, starting transfers between devices, flip(): return lax.ppermute(array, 'dp', [(i, i ^ mask) for i in range(devices)])  17.9 us
    unnamed x36, local copies, waits for them, and re-layouts  9.3 us
    all_to_all x1, starting transfers between devices, local(): lax.all_to_all(after(packed, hidden_other, cotangent_other).reshape(exper...  7.97 us
    pallas_call x1, Pallas kernels, expert_sum(): pl.pallas_call(expert_kernel, out_shape=pltpu.HBM(sent_shape, BF16), grid...  6.34 us
    pallas_call x1, Pallas kernels, local(): pl.pallas_call(gradient_kernel, out_shape=(pltpu.HBM(part.shape, BF16),)...  4.43 us
    all_to_all x1, starting transfers between devices, local(): lax.all_to_all(trained, 'dp', split_axis=0, concat_axis=0, tiled=True, ax...  4.2 us
    all_to_all x1, starting transfers between devices, local(): lax.all_to_all(expert_out, 'dp', split_axis=0, concat_axis=0, tiled=True,...  3.61 us
  transfers between devices with their start and end apart: 23, of which 11 were waited for; matrix products, arithmetic and copies ran while one was open for 0% of the time, Pallas kernels for 16%

profile of v2, /device:TPU:0, one launch (start us, length us, event | category | flops | bytes accessed | tf_op | source)
XLA Modules:
  0.0 122.6 jit_solution(2937658831629430524)
XLA Ops:
  1.2 2.2 %collective-permute-done.hidden_other = bf16[128,1536]{1,0:T(8,128)(2,1)S(1)} collective-permute-done((bf16[128,1536]{1,0:T(8,128)(2,1)}, bf16[128,1536]{1,0:T(8,128)(2,1)S(1)}, u32[]{:S(2)}, u32[]{:S(2)}) %collective-permute-start) | collective-permute-done | bytes 393248 | tf_op jit(solution)/shard_map/ppermute | solution.py:335
  4.6 3.3 %shard_map.122 = (bf16[384,1664]{1,0:T(8,128)(2,1)}, bf16[64,24]{1,0:T(8,128)(2,1)S(1)}, bf16[24,1536]{1,0:T(8,128)(2,1)S(1)}) custom-call(s32[16]{0:T(128)S(1)} %copy-done.14, s32[32,8]{1,0:T(8,128)} %bitcast.17, f32[32,8]{1,0:T(8,128)} %bitcast.18, bf16[256,1536]{1,0:T(8,128)(2,1)} %bitcast.15), custom_call_target="tpu_custom_call" | custom-call | tf_op jit(solution)/shard_map/pallas_call | solution.py:356
  7.9 8.0 %all-to-all-start = ((bf16[16,24,1664]{2,1,0:T(8,128)(2,1)}), bf16[16,24,1664]{2,1,0:T(8,128)(2,1)S(1)}, u32[]{:S(2)}, u32[]{:S(2)}) async-start(bf16[16,24,1664]{2,1,0:T(8,128)(2,1)} %bitcast.14), calls=%async_computation | async-start | bytes 2555904 | tf_op jit(solution)/shard_map/all_to_all | solution.py:379
  15.9 4.4 %shard_map.123 = (bf16[2,6,128,128]{3,2,1,0:T(8,128)(2,1)}, bf16[2,6,128,128]{3,2,1,0:T(8,128)(2,1)}, bf16[2,6,128,128]{3,2,1,0:T(8,128)(2,1)}, bf16[2,6,128,128...) custom-call(s32[1]{0:T(128)} %bitcast.7.device_ref, ...), custom_call_target="tpu_custom_call" | custom-call | tf_op jit(solution)/shard_map/pallas_call | solution.py:392
  20.3 1.9 %collective-permute-start.2 = (bf16[2,6,128,128]{3,2,1,0:T(8,128)(2,1)}, bf16[2,6,128,128]{3,2,1,0:T(8,128)(2,1)S(1)}, u32[]{:S(2)}, u32[]{:S(2)}) collective-permute-start(bf16[2,6,128,128]{3,2,1,0:T(8,128)(2,1)} %get-tuple-element.37), channel_id=1, source_target_pairs={{0,2},{1,3},{2,0},{3,1},{4,6},{5,7},{6,4},{7,5},{8,10},{9,11},{10,... | collective-permute-start | bytes 1179656 | tf_op jit(solution)/shard_map/ppermute | solution.py:335
  24.4 16.3 %collective-permute-done.2.arrived_a = bf16[2,6,128,128]{3,2,1,0:T(8,128)(2,1)S(1)} collective-permute-done((bf16[2,6,128,128]{3,2,1,0:T(8,128)(2,1)}, bf16[2,6,128,128]{3,2,1,0:T(8,128)(2,1)S(1)}, u32[]{:S(2)}, u32[]{:S(2)}) %collective-permute-start.2) | collective-permute-done | bytes 393248 | tf_op jit(solution)/shard_map/ppermute | solution.py:335
  46.1 4.7 %collective-permute-done.5.rest_1_ = bf16[2,6,128,128]{3,2,1,0:T(8,128)(2,1)S(1)} collective-permute-done((bf16[2,6,128,128]{3,2,1,0:T(8,128)(2,1)}, bf16[2,6,128,128]{3,2,1,0:T(8,128)(2,1)S(1)}, u32[]{:S(2)}, u32[]{:S(2)}) %collective-permute-start.5) | collective-permute-done | bytes 393248 | tf_op jit(solution)/shard_map/ppermute | solution.py:335
  51.0 1.9 %copy-done = bf16[768,2048]{1,0:T(8,128)(2,1)S(1)} copy-done((bf16[768,2048]{1,0:T(8,128)(2,1)S(1)}, bf16[768,2048]{1,0:T(8,128)(2,1)}, u32[]{:S(2)}) %copy-start) | copy-done | bytes 3145752
  52.9 6.3 %shard_map.125 = bf16[4,120,2176]{2,1,0:T(8,128)(2,1)} custom-call(s32[1]{0:T(128)} %bitcast.4.core_ref, bf16[384,1664]{1,0:T(8,128)(2,1)S(1)} %bitcast.11, bf16[24,1536]{1,0:T(8,128)(2,1)S(1)} %get-tuple-element.48.rows_trained, bf16[768,2048]{1,0:T(8,128)(2,1)S(1)} %copy-done, bf16[768,2048]{1,0:T(8,128)(2,1)} %collective-permute-done.3.weights_other, ...), custom_call_target="tpu_custom_call" | custom-call | tf_op jit(solution)/shard_map/pallas_call | solution.py:429
  60.0 3.6 %all-to-all-start.1 = ((bf16[4,120,2176]{2,1,0:T(8,128)(2,1)}), bf16[4,120,2176]{2,1,0:T(8,128)(2,1)S(1)}, u32[]{:S(2)}, u32[]{:S(2)}) async-start(bf16[4,120,2176]{2,1,0:T(8,128)(2,1)} %shard_map.125), calls=%async_computation.1 | async-start | bytes 4177920 | tf_op jit(solution)/shard_map/all_to_all | solution.py:522
  65.7 2.6 %shard_map.126 = (bf16[6,128,128]{2,1,0:T(8,128)(2,1)}, bf16[6,128,128]{2,1,0:T(8,128)(2,1)}, f32[6,128,128]{2,1,0:T(8,128)}, f32[6,128,128]{2,1,0:T(8,128)}) custom-call(s32[1]{0:T(128)} %bitcast.3.floor_ref.refs_0_, bf16[2,6,128,128]{3,2,1,0:T(8,128)(2,1)S(1)} %copy-done.1, bf16[2,6,128,128]{3,2,1,0:T(8,128)(2,1)S(1)} %collective-permute-done.5.rest_1_, ...), custom_call_target="tpu_custom_call" | custom-call | tf_op jit(solution)/shard_map/pallas_call | solution.py:462
  68.2 2.1 %collective-permute-start.11 = (bf16[6,128,128]{2,1,0:T(8,128)(2,1)}, bf16[6,128,128]{2,1,0:T(8,128)(2,1)S(1)}, u32[]{:S(2)}, u32[]{:S(2)}) collective-permute-start(bf16[6,128,128]{2,1,0:T(8,128)(2,1)} %get-tuple-element.54), channel_id=1, source_target_pairs={{0,8},{1,9},{2,10},{3,11},{4,12},{5,13},{6,14},{7,15},{8,0},{9,1},... | collective-permute-start | bytes 589832 | tf_op jit(solution)/shard_map/ppermute | solution.py:335
  70.4 5.5 %collective-permute-done.11.arrived = bf16[6,128,128]{2,1,0:T(8,128)(2,1)S(1)} collective-permute-done((bf16[6,128,128]{2,1,0:T(8,128)(2,1)}, bf16[6,128,128]{2,1,0:T(8,128)(2,1)S(1)}, u32[]{:S(2)}, u32[]{:S(2)}) %collective-permute-start.11) | collective-permute-done | bytes 196640 | tf_op jit(solution)/shard_map/ppermute | solution.py:335
  76.9 2.1 %collective-permute-start.12 = (bf16[6,128,128]{2,1,0:T(8,128)(2,1)S(1)}, bf16[6,128,128]{2,1,0:T(8,128)(2,1)S(1)}, u32[]{:S(2)}, u32[]{:S(2)}) collective-permute-start(bf16[6,128,128]{2,1,0:T(8,128)(2,1)S(1)} %shard_map.127), channel_id=1, source_target_pairs={{0,16},{1,17},{2,18},{3,19},{4,20},{5,21},{6,22},{7,23},{8,24},{9,... | collective-permute-start | bytes 589832 | tf_op jit(solution)/shard_map/ppermute | solution.py:335
  79.7 7.7 %collective-permute-done.12.rest_2_ = bf16[6,128,128]{2,1,0:T(8,128)(2,1)S(1)} collective-permute-done((bf16[6,128,128]{2,1,0:T(8,128)(2,1)S(1)}, bf16[6,128,128]{2,1,0:T(8,128)(2,1)S(1)}, u32[]{:S(2)}, u32[]{:S(2)}) %collective-permute-start.12) | collective-permute-done | bytes 196640 | tf_op jit(solution)/shard_map/ppermute | solution.py:335
  89.7 1.8 %collective-permute-start.17 = (bf16[6,128,128]{2,1,0:T(8,128)(2,1)S(1)}, bf16[6,128,128]{2,1,0:T(8,128)(2,1)S(1)}, u32[]{:S(2)}, u32[]{:S(2)}) collective-permute-start(bf16[6,128,128]{2,1,0:T(8,128)(2,1)S(1)} %get-tuple-element.56.refs_2_), channel_id=1, source_target_pairs={{0,8},{1,9},{2,10},{3,11},{4,12},{5,13},{6,14},{7,15},{8,0},{9,1},... | collective-permute-start | bytes 589832 | tf_op jit(solution)/shard_map/ppermute | solution.py:335
  91.4 5.1 %collective-permute-done.18.refs_4_ = bf16[6,128,128]{2,1,0:T(8,128)(2,1)S(1)} collective-permute-done((bf16[6,128,128]{2,1,0:T(8,128)(2,1)S(1)}, bf16[6,128,128]{2,1,0:T(8,128)(2,1)S(1)}, u32[]{:S(2)}, u32[]{:S(2)}) %collective-permute-start.18) | collective-permute-done | bytes 196640 | tf_op jit(solution)/shard_map/ppermute | solution.py:335
  97.9 1.6 %collective-permute-done.17.refs_3_ = bf16[6,128,128]{2,1,0:T(8,128)(2,1)S(1)} collective-permute-done((bf16[6,128,128]{2,1,0:T(8,128)(2,1)S(1)}, bf16[6,128,128]{2,1,0:T(8,128)(2,1)S(1)}, u32[]{:S(2)}, u32[]{:S(2)}) %collective-permute-start.17) | collective-permute-done | bytes 196640 | tf_op jit(solution)/shard_map/ppermute | solution.py:335
  99.5 3.8 %collective-permute-done.19.refs_5_ = bf16[6,128,128]{2,1,0:T(8,128)(2,1)S(1)} collective-permute-done((bf16[6,128,128]{2,1,0:T(8,128)(2,1)S(1)}, bf16[6,128,128]{2,1,0:T(8,128)(2,1)S(1)}, u32[]{:S(2)}, u32[]{:S(2)}) %collective-permute-start.19) | collective-permute-done | bytes 196640 | tf_op jit(solution)/shard_map/ppermute | solution.py:335
  104.6 4.2 %all-to-all-start.2 = ((bf16[8,24,768]{2,1,0:T(8,128)(2,1)}), bf16[8,24,768]{2,1,0:T(8,128)(2,1)S(1)}, u32[]{:S(2)}, u32[]{:S(2)}) async-start(bf16[8,24,768]{2,1,0:T(8,128)(2,1)} %shard_map.130), calls=%async_computation.2 | async-start | bytes 589824 | tf_op jit(solution)/shard_map/all_to_all | solution.py:552
  108.8 2.6 %collective-permute-start.14 = (bf16[32,2048]{1,0:T(8,128)(2,1)S(1)}, bf16[32,2048]{1,0:T(8,128)(2,1)S(1)}, u32[]{:S(2)}, u32[]{:S(2)}) collective-permute-start(bf16[32,2048]{1,0:T(8,128)(2,1)S(1)} %get-tuple-element.60), channel_id=1, source_target_pairs={{0,16},{1,17},{2,18},{3,19},{4,20},{5,21},{6,22},{7,23},{8,24},{9,... | collective-permute-start | bytes 393224 | tf_op jit(solution)/shard_map/ppermute | solution.py:335
  111.3 1.8 %collective-permute-start.15 = (bf16[32,2048]{1,0:T(8,128)(2,1)S(1)}, bf16[32,2048]{1,0:T(8,128)(2,1)S(1)}, u32[]{:S(2)}, u32[]{:S(2)}) collective-permute-start(bf16[32,2048]{1,0:T(8,128)(2,1)S(1)} %get-tuple-element.61), channel_id=1, source_target_pairs={{0,24},{1,25},{2,26},{3,27},{4,28},{5,29},{6,30},{7,31},{8,16},{9,... | collective-permute-start | bytes 393224 | tf_op jit(solution)/shard_map/ppermute | solution.py:335
  113.2 3.7 %collective-permute-done.13.refs_2_ = bf16[32,2048]{1,0:T(8,128)(2,1)S(1)} collective-permute-done((bf16[32,2048]{1,0:T(8,128)(2,1)S(1)}, bf16[32,2048]{1,0:T(8,128)(2,1)S(1)}, u32[]{:S(2)}, u32[]{:S(2)}) %collective-permute-start.13) | collective-permute-done | bytes 131104 | tf_op jit(solution)/shard_map/ppermute | solution.py:335
  116.9 4.8 %collective-permute-done.14.refs_3_ = bf16[32,2048]{1,0:T(8,128)(2,1)S(1)} collective-permute-done((bf16[32,2048]{1,0:T(8,128)(2,1)S(1)}, bf16[32,2048]{1,0:T(8,128)(2,1)S(1)}, u32[]{:S(2)}, u32[]{:S(2)}) %collective-permute-start.14) | collective-permute-done | bytes 131104 | tf_op jit(solution)/shard_map/ppermute | solution.py:335
  (71 shorter events, 19.6 us)
Async XLA Ops:
  0.6 2.8 %collective-permute-start.1 = (bf16[128,2048]{1,0:T(8,128)(2,1)}, bf16[128,2048]{1,0:T(8,128)(2,1)S(1)}, u32[]{:S(2)}, u32[]{:S(2)}) collective-permute-start(bf16[128,2048]{1,0:T(8,128)(2,1)} %cotangent_own.1), channel_id=1, source_target_pairs={{0,1},{1,0},{2,3},{3,2},{4,5},{5,4},{6,7},{7,6},{8,9},{9,8},{10,11... | collective-permute-start | bytes 1572872 | tf_op jit(solution)/shard_map/ppermute | solution.py:335
  1.1 2.3 %collective-permute-start = (bf16[128,1536]{1,0:T(8,128)(2,1)}, bf16[128,1536]{1,0:T(8,128)(2,1)S(1)}, u32[]{:S(2)}, u32[]{:S(2)}) collective-permute-start(bf16[128,1536]{1,0:T(8,128)(2,1)} %hidden_own), channel_id=1, source_target_pairs={{0,1},{1,0},{2,3},{3,2},{4,5},{5,4},{6,7},{7,6},{8,9},{9,8},{10,11... | collective-permute-start | bytes 1179656 | tf_op jit(solution)/shard_map/ppermute | solution.py:335
  3.5 20.9 %collective-permute-start.3 = (bf16[768,2048]{1,0:T(8,128)(2,1)}, bf16[768,2048]{1,0:T(8,128)(2,1)}, u32[]{:S(2)}, u32[]{:S(2)}) collective-permute-start(bf16[768,2048]{1,0:T(8,128)(2,1)} %weights.1), channel_id=1, source_target_pairs={{0,1},{1,0},{2,3},{3,2},{4,5},{5,4},{6,7},{7,6},{8,9},{9,8},{10,11... | collective-permute-start | bytes 9437192 | tf_op jit(solution)/shard_map/ppermute | solution.py:335
  7.9 43.0 %all-to-all-start = ((bf16[16,24,1664]{2,1,0:T(8,128)(2,1)}), bf16[16,24,1664]{2,1,0:T(8,128)(2,1)S(1)}, u32[]{:S(2)}, u32[]{:S(2)}) async-start(bf16[16,24,1664]{2,1,0:T(8,128)(2,1)} %bitcast.14), calls=%async_computation | async-start | bytes 2555904 | tf_op jit(solution)/shard_map/all_to_all | solution.py:379
  15.9 30.2 %copy-start.17 = (f32[6,16]{1,0:T(8,128)S(1)}, f32[6,16]{1,0:T(8,128)}, u32[]{:S(2)}) copy-start(f32[6,16]{1,0:T(8,128)} %param.17) | copy-start | bytes 1156
  20.3 20.4 %collective-permute-start.2 = (bf16[2,6,128,128]{3,2,1,0:T(8,128)(2,1)}, bf16[2,6,128,128]{3,2,1,0:T(8,128)(2,1)S(1)}, u32[]{:S(2)}, u32[]{:S(2)}) collective-permute-start(bf16[2,6,128,128]{3,2,1,0:T(8,128)(2,1)} %get-tuple-element.37), channel_id=1, source_target_pairs={{0,2},{1,3},{2,0},{3,1},{4,6},{5,7},{6,4},{7,5},{8,10},{9,11},{10,... | collective-permute-start | bytes 1179656 | tf_op jit(solution)/shard_map/ppermute | solution.py:335
  22.3 18.4 %collective-permute-start.4 = (bf16[2,6,128,128]{3,2,1,0:T(8,128)(2,1)}, bf16[2,6,128,128]{3,2,1,0:T(8,128)(2,1)S(1)}, u32[]{:S(2)}, u32[]{:S(2)}) collective-permute-start(bf16[2,6,128,128]{3,2,1,0:T(8,128)(2,1)} %get-tuple-element.41), channel_id=1, source_target_pairs={{0,4},{1,5},{2,6},{3,7},{4,0},{5,1},{6,2},{7,3},{8,12},{9,13},{10,... | collective-permute-start | bytes 1179656 | tf_op jit(solution)/shard_map/ppermute | solution.py:335
  23.7 27.1 %collective-permute-start.5 = (bf16[2,6,128,128]{3,2,1,0:T(8,128)(2,1)}, bf16[2,6,128,128]{3,2,1,0:T(8,128)(2,1)S(1)}, u32[]{:S(2)}, u32[]{:S(2)}) collective-permute-start(bf16[2,6,128,128]{3,2,1,0:T(8,128)(2,1)} %get-tuple-element.45), channel_id=1, source_target_pairs={{0,2},{1,3},{2,0},{3,1},{4,6},{5,7},{6,4},{7,5},{8,10},{9,11},{10,... | collective-permute-start | bytes 1179656 | tf_op jit(solution)/shard_map/ppermute | solution.py:335
  24.3 26.5 %collective-permute-start.6 = (bf16[2,6,128,128]{3,2,1,0:T(8,128)(2,1)}, bf16[2,6,128,128]{3,2,1,0:T(8,128)(2,1)S(1)}, u32[]{:S(2)}, u32[]{:S(2)}) collective-permute-start(bf16[2,6,128,128]{3,2,1,0:T(8,128)(2,1)} %get-tuple-element.46), channel_id=1, source_target_pairs={{0,4},{1,5},{2,6},{3,7},{4,0},{5,1},{6,2},{7,3},{8,12},{9,13},{10,... | collective-permute-start | bytes 1179656 | tf_op jit(solution)/shard_map/ppermute | solution.py:335
  43.7 15.6 %collective-permute-start.8 = (bf16[2,6,128,128]{3,2,1,0:T(8,128)(2,1)}, bf16[2,6,128,128]{3,2,1,0:T(8,128)(2,1)S(1)}, u32[]{:S(2)}, u32[]{:S(2)}) collective-permute-start(bf16[2,6,128,128]{3,2,1,0:T(8,128)(2,1)} %get-tuple-element.43), channel_id=1, source_target_pairs={{0,4},{1,5},{2,6},{3,7},{4,0},{5,1},{6,2},{7,3},{8,12},{9,13},{10,... | collective-permute-start | bytes 1179656 | tf_op jit(solution)/shard_map/ppermute | solution.py:335
  45.2 14.8 %collective-permute-start.9 = (bf16[2,6,128,128]{3,2,1,0:T(8,128)(2,1)}, bf16[2,6,128,128]{3,2,1,0:T(8,128)(2,1)}, u32[]{:S(2)}, u32[]{:S(2)}) collective-permute-start(bf16[2,6,128,128]{3,2,1,0:T(8,128)(2,1)} %get-tuple-element.44), channel_id=1, source_target_pairs={{0,2},{1,3},{2,0},{3,1},{4,6},{5,7},{6,4},{7,5},{8,10},{9,11},{10,... | collective-permute-start | bytes 1179656 | tf_op jit(solution)/shard_map/ppermute | solution.py:335
  46.1 4.8 %collective-permute-start.7 = (f32[6,16]{1,0:T(8,128)S(1)}, f32[6,16]{1,0:T(8,128)S(1)}, u32[]{:S(2)}, u32[]{:S(2)}) collective-permute-start(f32[6,16]{1,0:T(8,128)S(1)} %copy-done.17), channel_id=1, source_target_pairs={{0,1},{1,0},{2,3},{3,2},{4,5},{5,4},{6,7},{7,6},{8,9},{9,8},{10,11... | collective-permute-start | bytes 1160 | tf_op jit(solution)/shard_map/ppermute | solution.py:335
  60.0 29.6 %all-to-all-start.1 = ((bf16[4,120,2176]{2,1,0:T(8,128)(2,1)}), bf16[4,120,2176]{2,1,0:T(8,128)(2,1)S(1)}, u32[]{:S(2)}, u32[]{:S(2)}) async-start(bf16[4,120,2176]{2,1,0:T(8,128)(2,1)} %shard_map.125), calls=%async_computation.1 | async-start | bytes 4177920 | tf_op jit(solution)/shard_map/all_to_all | solution.py:522
  68.2 7.7 %collective-permute-start.11 = (bf16[6,128,128]{2,1,0:T(8,128)(2,1)}, bf16[6,128,128]{2,1,0:T(8,128)(2,1)S(1)}, u32[]{:S(2)}, u32[]{:S(2)}) collective-permute-start(bf16[6,128,128]{2,1,0:T(8,128)(2,1)} %get-tuple-element.54), channel_id=1, source_target_pairs={{0,8},{1,9},{2,10},{3,11},{4,12},{5,13},{6,14},{7,15},{8,0},{9,1},... | collective-permute-start | bytes 589832 | tf_op jit(solution)/shard_map/ppermute | solution.py:335
  70.3 9.4 %collective-permute-start.10 = (bf16[6,128,128]{2,1,0:T(8,128)(2,1)}, bf16[6,128,128]{2,1,0:T(8,128)(2,1)S(1)}, u32[]{:S(2)}, u32[]{:S(2)}) collective-permute-start(bf16[6,128,128]{2,1,0:T(8,128)(2,1)} %get-tuple-element.53), channel_id=1, source_target_pairs={{0,8},{1,9},{2,10},{3,11},{4,12},{5,13},{6,14},{7,15},{8,0},{9,1},... | collective-permute-start | bytes 589832 | tf_op jit(solution)/shard_map/ppermute | solution.py:335
  76.9 10.5 %collective-permute-start.12 = (bf16[6,128,128]{2,1,0:T(8,128)(2,1)S(1)}, bf16[6,128,128]{2,1,0:T(8,128)(2,1)S(1)}, u32[]{:S(2)}, u32[]{:S(2)}) collective-permute-start(bf16[6,128,128]{2,1,0:T(8,128)(2,1)S(1)} %shard_map.127), channel_id=1, source_target_pairs={{0,16},{1,17},{2,18},{3,19},{4,20},{5,21},{6,22},{7,23},{8,24},{9,... | collective-permute-start | bytes 589832 | tf_op jit(solution)/shard_map/ppermute | solution.py:335
  89.6 7.0 %collective-permute-start.18 = (bf16[6,128,128]{2,1,0:T(8,128)(2,1)S(1)}, bf16[6,128,128]{2,1,0:T(8,128)(2,1)S(1)}, u32[]{:S(2)}, u32[]{:S(2)}) collective-permute-start(bf16[6,128,128]{2,1,0:T(8,128)(2,1)S(1)} %get-tuple-element.56.refs_2_), channel_id=1, source_target_pairs={{0,16},{1,17},{2,18},{3,19},{4,20},{5,21},{6,22},{7,23},{8,24},{9,... | collective-permute-start | bytes 589832 | tf_op jit(solution)/shard_map/ppermute | solution.py:335
  89.6 13.7 %collective-permute-start.16 = (bf16[4,24,1536]{2,1,0:T(8,128)(2,1)S(1)}, bf16[4,24,1536]{2,1,0:T(8,128)(2,1)S(1)}, u32[]{:S(2)}, u32[]{:S(2)}) collective-permute-start(bf16[4,24,1536]{2,1,0:T(8,128)(2,1)S(1)} %slice.4.refs_0_), channel_id=1, source_target_pairs={{0,1},{1,0},{2,3},{3,2},{4,5},{5,4},{6,7},{7,6},{8,9},{9,8},{10,11... | collective-permute-start | bytes 884744 | tf_op jit(solution)/shard_map/ppermute | solution.py:335
  89.7 9.9 %collective-permute-start.17 = (bf16[6,128,128]{2,1,0:T(8,128)(2,1)S(1)}, bf16[6,128,128]{2,1,0:T(8,128)(2,1)S(1)}, u32[]{:S(2)}, u32[]{:S(2)}) collective-permute-start(bf16[6,128,128]{2,1,0:T(8,128)(2,1)S(1)} %get-tuple-element.56.refs_2_), channel_id=1, source_target_pairs={{0,8},{1,9},{2,10},{3,11},{4,12},{5,13},{6,14},{7,15},{8,0},{9,1},... | collective-permute-start | bytes 589832 | tf_op jit(solution)/shard_map/ppermute | solution.py:335
  96.6 6.7 %collective-permute-start.19 = (bf16[6,128,128]{2,1,0:T(8,128)(2,1)S(1)}, bf16[6,128,128]{2,1,0:T(8,128)(2,1)S(1)}, u32[]{:S(2)}, u32[]{:S(2)}) collective-permute-start(bf16[6,128,128]{2,1,0:T(8,128)(2,1)S(1)} %collective-permute-done.18.refs_4_), channel_id=1, source_target_pairs={{0,8},{1,9},{2,10},{3,11},{4,12},{5,13},{6,14},{7,15},{8,0},{9,1},... | collective-permute-start | bytes 589832 | tf_op jit(solution)/shard_map/ppermute | solution.py:335
  104.6 17.1 %all-to-all-start.2 = ((bf16[8,24,768]{2,1,0:T(8,128)(2,1)}), bf16[8,24,768]{2,1,0:T(8,128)(2,1)S(1)}, u32[]{:S(2)}, u32[]{:S(2)}) async-start(bf16[8,24,768]{2,1,0:T(8,128)(2,1)} %shard_map.130), calls=%async_computation.2 | async-start | bytes 589824 | tf_op jit(solution)/shard_map/all_to_all | solution.py:552
  108.8 8.1 %collective-permute-start.13 = (bf16[32,2048]{1,0:T(8,128)(2,1)S(1)}, bf16[32,2048]{1,0:T(8,128)(2,1)S(1)}, u32[]{:S(2)}, u32[]{:S(2)}) collective-permute-start(bf16[32,2048]{1,0:T(8,128)(2,1)S(1)} %get-tuple-element.59), channel_id=1, source_target_pairs={{0,8},{1,9},{2,10},{3,11},{4,12},{5,13},{6,14},{7,15},{8,0},{9,1},... | collective-permute-start | bytes 393224 | tf_op jit(solution)/shard_map/ppermute | solution.py:335
  108.8 12.9 %collective-permute-start.14 = (bf16[32,2048]{1,0:T(8,128)(2,1)S(1)}, bf16[32,2048]{1,0:T(8,128)(2,1)S(1)}, u32[]{:S(2)}, u32[]{:S(2)}) collective-permute-start(bf16[32,2048]{1,0:T(8,128)(2,1)S(1)} %get-tuple-element.60), channel_id=1, source_target_pairs={{0,16},{1,17},{2,18},{3,19},{4,20},{5,21},{6,22},{7,23},{8,24},{9,... | collective-permute-start | bytes 393224 | tf_op jit(solution)/shard_map/ppermute | solution.py:335
  111.3 10.4 %collective-permute-start.15 = (bf16[32,2048]{1,0:T(8,128)(2,1)S(1)}, bf16[32,2048]{1,0:T(8,128)(2,1)S(1)}, u32[]{:S(2)}, u32[]{:S(2)}) collective-permute-start(bf16[32,2048]{1,0:T(8,128)(2,1)S(1)} %get-tuple-element.61), channel_id=1, source_target_pairs={{0,24},{1,25},{2,26},{3,27},{4,28},{5,29},{6,30},{7,31},{8,16},{9,... | collective-permute-start | bytes 393224 | tf_op jit(solution)/shard_map/ppermute | solution.py:335
  (17 other events, 116.7 us)

commit v3 on v2

--- a/solution.py
+++ b/solution.py
@@ -250,8 +250,9 @@
                 ].astype(BF16)
 
 
-def mix_kernel(depth, plane_slots, floor_ref, returned, *outs):
-    count, columns = outs[0].shape
+def mix_kernel(depth, plane_slots, floor_ref, returned, own, across, sent):
+    count, columns = own.shape
+    outs = own, sent.at[0], across, sent.at[1]
 
     def of_chips(at):
         return jnp.concatenate(
@@ -275,8 +276,12 @@
             out[:, at] = (mixed[:count] + mixed[count : 2 * count]).astype(out.dtype)
 
 
-def combine_kernel(depth, side, gates_trained, *rest):
-    mixed, trained, out = rest[:depth], rest[depth], rest[depth + 1]
+def mix_sum_kernel(arrived, across, own, out_across, out_own):
+    out_across[...] = (arrived[1].astype(F32) + across[...]).astype(BF16)
+    out_own[...] = arrived[0].astype(F32) + own[...]
+
+
+def combine_kernel(side, gates_trained, near, across, trained, out):
     peers, _, width = trained.shape
     columns = out.shape[1]
     blocks = width // side
@@ -296,8 +301,7 @@
             gates_trained[...], jnp.concatenate(fresh, axis=1), preferred_element_type=F32
         )
         total = both[:count] + both[count:]
-        for part in mixed:
-            total = total + part[:, at].astype(F32)
+        total = total + near[:, at] + across[:, at].astype(F32)
         out[:, at] = total.astype(out.dtype)
 
 
@@ -406,7 +410,7 @@
     both_a, first_a, second_a, stay_a, both_b, first_b, second_b, stay_b = parts
     both_a, both_b = flip(both_a, 2), flip(both_b, 4)
     first_a, first_b = flip(first_a, 2), flip(first_b, 4)
-    weights_other = flip(after(resident_weight, hidden_other, cotangent_other), 1)
+    weights_other = flip(after(resident_weight, packed, hidden_other, cotangent_other), 1)
     scales_other = flip(resident_scale, 1)
     second_a = after(second_a, weights_other)
     second_a, second_b = pl.pallas_call(
@@ -415,7 +419,7 @@
         in_specs=vmem(4),
         out_specs=tuple(vmem(2)),
         compiler_params=PARAMS,
-    )(both_a, second_a, both_b, second_b)
+    )(both_a, *in_hbm(second_a), both_b, *in_hbm(second_b))
     sums = second_a, second_b
     second_a, second_b = flip(second_a, 4), flip(second_b, 2)
 
@@ -458,7 +462,6 @@
     block_shape = (blocks, side, side)
     if highs == 2:
         expert_out = expert_sum(after(received, sums, first_a, first_b))
-        expert_out = after(expert_out, second_a, second_b)
         far, near, across, own = pl.pallas_call(
             second_sum_kernel,
             out_shape=(
@@ -473,13 +476,14 @@
             compiler_params=PARAMS,
         )(
             (device // 8).astype(jnp.int32).reshape(1),
-            stay_a,
+            *in_hbm(stay_a),
             first_a,
             second_a,
-            stay_b,
+            *in_hbm(stay_b),
             first_b,
             second_b,
         )
+        expert_out = after(expert_out, own)
         far, near = flip(far, 8), flip(near, 8)
         across = pl.pallas_call(
             third_sum_kernel,
@@ -487,7 +491,7 @@
             in_specs=vmem(2),
             out_specs=vmem(1)[0],
             compiler_params=PARAMS,
-        )(far, across)
+        )(far, *in_hbm(across))
         gradient = [own, near, flip(across, 16)]
     else:
         expert_out = expert_sum(received)
@@ -524,15 +528,30 @@
     )
     rows_trained = returned[:, plane_slots:, :hidden_width]
     rows_other = flip(rows_trained, 1)
-    mixed = pl.pallas_call(
+    row_shape = (row_count, columns)
+    mixed, across_rows, sent_rows = pl.pallas_call(
         lambda *refs: mix_kernel(depth, plane_slots, *refs),
-        out_shape=(jax.ShapeDtypeStruct((row_count, columns), F32),)
-        + (jax.ShapeDtypeStruct((row_count, columns), BF16),) * (depth - 1),
+        out_shape=(
+            jax.ShapeDtypeStruct(row_shape, F32),
+            jax.ShapeDtypeStruct(row_shape, F32),
+            jax.ShapeDtypeStruct((2,) + row_shape, BF16),
+        ),
         in_specs=[smem] + vmem(1),
-        out_specs=tuple(vmem(depth)),
+        out_specs=tuple(vmem(3)),
         compiler_params=PARAMS,
     )(floor_ref, after(returned, fresh))
-    mixed = [mixed[0]] + [flip(mixed[z], z * plane) for z in range(1, depth)]
+    sent_rows = flip(sent_rows, plane)
+    across_rows, mixed_near = pl.pallas_call(
+        mix_sum_kernel,
+        out_shape=(
+            jax.ShapeDtypeStruct(row_shape, BF16),
+            jax.ShapeDtypeStruct(row_shape, F32),
+        ),
+        in_specs=vmem(3),
+        out_specs=tuple(vmem(2)),
+        compiler_params=PARAMS,
+    )(sent_rows, across_rows, mixed)
+    across_rows = flip(across_rows, 2 * plane)
 
     held = {0: fresh}
     mask = depth // 2
@@ -547,18 +566,18 @@
         out_specs=vmem(1)[0],
         scratch_shapes=[pltpu.VMEM((row_blocks, plane * pair_slots, side), BF16)],
         compiler_params=PARAMS,
-    )(device_ref, after(rows_trained, mixed[0]), rows_other, *[held[z] for z in range(depth)])
+    )(device_ref, after(rows_trained, mixed), rows_other, *[held[z] for z in range(depth)])
     planes = [[z * plane + i for i in range(plane)] for z in range(depth)]
     trained = lax.all_to_all(
         trained, "dp", split_axis=0, concat_axis=0, tiled=True, axis_index_groups=planes
     )
     decoded = pl.pallas_call(
-        lambda *refs: combine_kernel(depth, side, *refs),
+        lambda *refs: combine_kernel(side, *refs),
         out_shape=jax.ShapeDtypeStruct((row_count, columns), BF16),
-        in_specs=vmem(2 + depth),
+        in_specs=vmem(4),
         out_specs=vmem(1)[0],
         compiler_params=PARAMS,
-    )(gates_trained, *mixed, trained)
+    )(gates_trained, mixed_near, across_rows, trained)
     return (decoded.reshape(steps, step_rows, columns), new_master)
 
 

time: 123 us -> 117 us (0.951)
  local copies, waits for them, and re-layouts: 9.46 us -> 3.74 us
  Pallas kernels: 22.3 us -> 24.5 us
  waiting for transfers between devices: 56.3 us -> 54.1 us
    unnamed x36 -> x18, local copies, waits for them, and re-layouts: 9.3 us -> 3.57 us
    ppermute x20 -> x19, waiting for transfers between devices: 56.3 us -> 51.4 us  [flip(): return lax.ppermute(array, 'dp', [(i, i ^ mask) for i in range(devices)])]
    all_to_all x1, waiting for transfers between devices: 0.01 us -> 2.67 us  [local(): lax.all_to_all(expert_out, 'dp', split_axis=0, concat_axis=0, tiled=True,...]
    ppermute x20 -> x19, starting transfers between devices: 17.9 us -> 17.3 us  [flip(): return lax.ppermute(array, 'dp', [(i, i ^ mask) for i in range(devices)])]
  transfers between devices with their start and end apart: 23 -> 22, of which waited for: 11 -> 11; matrix products, arithmetic and copies ran while one was open for 0% -> 0% of each run, Pallas kernels for 16% -> 18%
where the time goes in v3:
time: 117 us; the launch traced here: 116 us
  waiting for transfers between devices  54.1 us (46%)
  starting transfers between devices  32.9 us (28%)
  Pallas kernels  24.5 us (21%)
  local copies, waits for them, and re-layouts  3.74 us (3%)
    ppermute x19, waiting for transfers between devices, flip(): return lax.ppermute(array, 'dp', [(i, i ^ mask) for i in range(devices)])  51.4 us
    ppermute x19, starting transfers between devices, flip(): return lax.ppermute(array, 'dp', [(i, i ^ mask) for i in range(devices)])  17.3 us
    all_to_all x1, starting transfers between devices, local(): lax.all_to_all(after(packed, hidden_other, cotangent_other).reshape(exper...  7.94 us
    pallas_call x1, Pallas kernels, expert_sum(): pl.pallas_call(expert_kernel, out_shape=pltpu.HBM(sent_shape, BF16), grid...  6.32 us
    pallas_call x1, Pallas kernels, local(): pl.pallas_call(gradient_kernel, out_shape=(pltpu.HBM(part.shape, BF16),)...  4.38 us
    all_to_all x1, starting transfers between devices, local(): lax.all_to_all(trained, 'dp', split_axis=0, concat_axis=0, tiled=True, ax...  3.91 us
    all_to_all x1, starting transfers between devices, local(): lax.all_to_all(expert_out, 'dp', split_axis=0, concat_axis=0, tiled=True,...  3.75 us
    unnamed x18, local copies, waits for them, and re-layouts  3.57 us
  transfers between devices with their start and end apart: 22, of which 11 were waited for; matrix products, arithmetic and copies ran while one was open for 0% of the time, Pallas kernels for 18%

profile of v3, /device:TPU:0, one launch (start us, length us, event | category | flops | bytes accessed | tf_op | source)
XLA Modules:
  0.0 115.9 jit_solution(15650318869675747190)
XLA Ops:
  1.9 3.3 %shard_map.122 = (bf16[384,1664]{1,0:T(8,128)(2,1)}, bf16[64,24]{1,0:T(8,128)(2,1)S(1)}, bf16[24,1536]{1,0:T(8,128)(2,1)S(1)}) custom-call(s32[16]{0:T(128)S(1)} %copy-done.5, s32[32,8]{1,0:T(8,128)} %bitcast.17, f32[32,8]{1,0:T(8,128)} %bitcast.18, bf16[256,1536]{1,0:T(8,128)(2,1)} %bitcast.15), custom_call_target="tpu_custom_call" | custom-call | tf_op jit(solution)/shard_map/pallas_call | solution.py:360
  5.7 7.9 %all-to-all-start = ((bf16[16,24,1664]{2,1,0:T(8,128)(2,1)}), bf16[16,24,1664]{2,1,0:T(8,128)(2,1)S(1)}, u32[]{:S(2)}, u32[]{:S(2)}) async-start(bf16[16,24,1664]{2,1,0:T(8,128)(2,1)} %bitcast.14), calls=%async_computation | async-start | bytes 2555904 | tf_op jit(solution)/shard_map/all_to_all | solution.py:383
  13.7 4.4 %shard_map.123 = (bf16[2,6,128,128]{3,2,1,0:T(8,128)(2,1)}, bf16[2,6,128,128]{3,2,1,0:T(8,128)(2,1)}, bf16[2,6,128,128]{3,2,1,0:T(8,128)(2,1)}, bf16[2,6,128,128...) custom-call(s32[1]{0:T(128)} %bitcast.7.device_ref, ...), custom_call_target="tpu_custom_call" | custom-call | tf_op jit(solution)/shard_map/pallas_call | solution.py:396
  18.1 1.9 %collective-permute-start.2 = (bf16[2,6,128,128]{3,2,1,0:T(8,128)(2,1)}, bf16[2,6,128,128]{3,2,1,0:T(8,128)(2,1)S(1)}, u32[]{:S(2)}, u32[]{:S(2)}) collective-permute-start(bf16[2,6,128,128]{3,2,1,0:T(8,128)(2,1)} %get-tuple-element.38), channel_id=1, source_target_pairs={{0,2},{1,3},{2,0},{3,1},{4,6},{5,7},{6,4},{7,5},{8,10},{9,11},{10,... | collective-permute-start | bytes 1179656 | tf_op jit(solution)/shard_map/ppermute | solution.py:339
  20.0 1.5 %collective-permute-start.4 = (bf16[2,6,128,128]{3,2,1,0:T(8,128)(2,1)}, bf16[2,6,128,128]{3,2,1,0:T(8,128)(2,1)S(1)}, u32[]{:S(2)}, u32[]{:S(2)}) collective-permute-start(bf16[2,6,128,128]{3,2,1,0:T(8,128)(2,1)} %get-tuple-element.42), channel_id=1, source_target_pairs={{0,4},{1,5},{2,6},{3,7},{4,0},{5,1},{6,2},{7,3},{8,12},{9,13},{10,... | collective-permute-start | bytes 1179656 | tf_op jit(solution)/shard_map/ppermute | solution.py:339
  22.1 16.4 %collective-permute-done.2.arrived_a = bf16[2,6,128,128]{3,2,1,0:T(8,128)(2,1)S(1)} collective-permute-done((bf16[2,6,128,128]{3,2,1,0:T(8,128)(2,1)}, bf16[2,6,128,128]{3,2,1,0:T(8,128)(2,1)S(1)}, u32[]{:S(2)}, u32[]{:S(2)}) %collective-permute-start.2) | collective-permute-done | bytes 393248 | tf_op jit(solution)/shard_map/ppermute | solution.py:339
  38.5 2.1 %shard_map.124 = (bf16[2,6,128,128]{3,2,1,0:T(8,128)(2,1)}, bf16[2,6,128,128]{3,2,1,0:T(8,128)(2,1)}) custom-call(bf16[2,6,128,128]{3,2,1,0:T(8,128)(2,1)S(1)} %collective-permute-done.2.arrived_a, bf16[2,6,128,128]{3,2,1,0:T(8,128)(2,1)} %get-tuple-element.41.held_a, bf16[2,6,128,128]{3,2,1,0:T(8,128)(2,1)S(1)} %collective-permute-done.4.arrived_b, ...), custom_call_target="tpu_custom_call" | custom-call | tf_op jit(solution)/shard_map/pallas_call | solution.py:416
  43.0 5.6 %collective-permute-done.5.rest_1_ = bf16[2,6,128,128]{3,2,1,0:T(8,128)(2,1)S(1)} collective-permute-done((bf16[2,6,128,128]{3,2,1,0:T(8,128)(2,1)}, bf16[2,6,128,128]{3,2,1,0:T(8,128)(2,1)S(1)}, u32[]{:S(2)}, u32[]{:S(2)}) %collective-permute-start.5) | collective-permute-done | bytes 393248 | tf_op jit(solution)/shard_map/ppermute | solution.py:339
  48.8 1.9 %copy-done = bf16[768,2048]{1,0:T(8,128)(2,1)S(1)} copy-done((bf16[768,2048]{1,0:T(8,128)(2,1)S(1)}, bf16[768,2048]{1,0:T(8,128)(2,1)}, u32[]{:S(2)}) %copy-start) | copy-done | bytes 3145752
  50.7 6.3 %shard_map.125 = bf16[4,120,2176]{2,1,0:T(8,128)(2,1)} custom-call(s32[1]{0:T(128)} %bitcast.4.core_ref, bf16[384,1664]{1,0:T(8,128)(2,1)S(1)} %bitcast.11, bf16[24,1536]{1,0:T(8,128)(2,1)S(1)} %get-tuple-element.49.rows_trained, bf16[768,2048]{1,0:T(8,128)(2,1)S(1)} %copy-done, bf16[768,2048]{1,0:T(8,128)(2,1)} %collective-permute-done.3.weights_other, ...), custom_call_target="tpu_custom_call" | custom-call | tf_op jit(solution)/shard_map/pallas_call | solution.py:433
  57.0 2.6 %shard_map.126 = (bf16[6,128,128]{2,1,0:T(8,128)(2,1)}, bf16[6,128,128]{2,1,0:T(8,128)(2,1)}, f32[6,128,128]{2,1,0:T(8,128)}, f32[6,128,128]{2,1,0:T(8,128)}) custom-call(s32[1]{0:T(128)} %bitcast.3.floor_ref.refs_0_, bf16[2,6,128,128]{3,2,1,0:T(8,128)(2,1)} %get-tuple-element.50.rest_0_, bf16[2,6,128,128]{3,2,1,0:T(8,128)(2,1)S(1)} %collective-permute-done.5.rest_1_, ...), custom_call_target="tpu_custom_call" | custom-call | tf_op jit(solution)/shard_map/pallas_call | solution.py:465
  59.6 3.8 %all-to-all-start.1 = ((bf16[4,120,2176]{2,1,0:T(8,128)(2,1)}), bf16[4,120,2176]{2,1,0:T(8,128)(2,1)S(1)}, u32[]{:S(2)}, u32[]{:S(2)}) async-start(bf16[4,120,2176]{2,1,0:T(8,128)(2,1)} %shard_map.125), calls=%async_computation.1 | async-start | bytes 4177920 | tf_op jit(solution)/shard_map/all_to_all | solution.py:526
  63.4 2.1 %collective-permute-start.11 = (bf16[6,128,128]{2,1,0:T(8,128)(2,1)}, bf16[6,128,128]{2,1,0:T(8,128)(2,1)S(1)}, u32[]{:S(2)}, u32[]{:S(2)}) collective-permute-start(bf16[6,128,128]{2,1,0:T(8,128)(2,1)} %get-tuple-element.55), channel_id=1, source_target_pairs={{0,8},{1,9},{2,10},{3,11},{4,12},{5,13},{6,14},{7,15},{8,0},{9,1},... | collective-permute-start | bytes 589832 | tf_op jit(solution)/shard_map/ppermute | solution.py:339
  65.6 5.6 %collective-permute-done.11.arrived = bf16[6,128,128]{2,1,0:T(8,128)(2,1)S(1)} collective-permute-done((bf16[6,128,128]{2,1,0:T(8,128)(2,1)}, bf16[6,128,128]{2,1,0:T(8,128)(2,1)S(1)}, u32[]{:S(2)}, u32[]{:S(2)}) %collective-permute-start.11) | collective-permute-done | bytes 196640 | tf_op jit(solution)/shard_map/ppermute | solution.py:339
  72.2 1.9 %collective-permute-start.12 = (bf16[6,128,128]{2,1,0:T(8,128)(2,1)S(1)}, bf16[6,128,128]{2,1,0:T(8,128)(2,1)S(1)}, u32[]{:S(2)}, u32[]{:S(2)}) collective-permute-start(bf16[6,128,128]{2,1,0:T(8,128)(2,1)S(1)} %shard_map.127), channel_id=1, source_target_pairs={{0,16},{1,17},{2,18},{3,19},{4,20},{5,21},{6,22},{7,23},{8,24},{9,... | collective-permute-start | bytes 589832 | tf_op jit(solution)/shard_map/ppermute | solution.py:339
  74.9 7.5 %collective-permute-done.12.rest_2_ = bf16[6,128,128]{2,1,0:T(8,128)(2,1)S(1)} collective-permute-done((bf16[6,128,128]{2,1,0:T(8,128)(2,1)S(1)}, bf16[6,128,128]{2,1,0:T(8,128)(2,1)S(1)}, u32[]{:S(2)}, u32[]{:S(2)}) %collective-permute-start.12) | collective-permute-done | bytes 196640 | tf_op jit(solution)/shard_map/ppermute | solution.py:339
  84.5 2.7 %all-to-all-done.1.refs_1_ = bf16[4,120,2176]{2,1,0:T(8,128)(2,1)S(1)} async-done(((bf16[4,120,2176]{2,1,0:T(8,128)(2,1)}), bf16[4,120,2176]{2,1,0:T(8,128)(2,1)S(1)}, u32[]{:S(2)}, u32[]{:S(2)}) %all-to-all-start.1) | async-done | bytes 2088992 | tf_op jit(solution)/shard_map/all_to_all | solution.py:526
  87.3 1.6 %collective-permute-start.16 = (bf16[6,128,128]{2,1,0:T(8,128)(2,1)S(1)}, bf16[6,128,128]{2,1,0:T(8,128)(2,1)S(1)}, u32[]{:S(2)}, u32[]{:S(2)}) collective-permute-start(bf16[6,128,128]{2,1,0:T(8,128)(2,1)S(1)} %get-tuple-element.57.refs_2_), channel_id=1, source_target_pairs={{0,8},{1,9},{2,10},{3,11},{4,12},{5,13},{6,14},{7,15},{8,0},{9,1},... | collective-permute-start | bytes 589832 | tf_op jit(solution)/shard_map/ppermute | solution.py:339
  88.9 2.9 %collective-permute-done.17.refs_4_ = bf16[6,128,128]{2,1,0:T(8,128)(2,1)S(1)} collective-permute-done((bf16[6,128,128]{2,1,0:T(8,128)(2,1)S(1)}, bf16[6,128,128]{2,1,0:T(8,128)(2,1)S(1)}, u32[]{:S(2)}, u32[]{:S(2)}) %collective-permute-start.17) | collective-permute-done | bytes 196640 | tf_op jit(solution)/shard_map/ppermute | solution.py:339
  93.1 2.1 %collective-permute-start.13 = (bf16[2,32,2048]{2,1,0:T(8,128)(2,1)S(1)}, bf16[2,32,2048]{2,1,0:T(8,128)(2,1)S(1)}, u32[]{:S(2)}, u32[]{:S(2)}) collective-permute-start(bf16[2,32,2048]{2,1,0:T(8,128)(2,1)S(1)} %get-tuple-element.59), channel_id=1, source_target_pairs={{0,8},{1,9},{2,10},{3,11},{4,12},{5,13},{6,14},{7,15},{8,0},{9,1},... | collective-permute-start | bytes 786440 | tf_op jit(solution)/shard_map/ppermute | solution.py:339
  95.9 4.2 %collective-permute-done.18.refs_5_ = bf16[6,128,128]{2,1,0:T(8,128)(2,1)S(1)} collective-permute-done((bf16[6,128,128]{2,1,0:T(8,128)(2,1)S(1)}, bf16[6,128,128]{2,1,0:T(8,128)(2,1)S(1)}, u32[]{:S(2)}, u32[]{:S(2)}) %collective-permute-start.18) | collective-permute-done | bytes 196640 | tf_op jit(solution)/shard_map/ppermute | solution.py:339
  101.4 3.9 %all-to-all-start.2 = ((bf16[8,24,768]{2,1,0:T(8,128)(2,1)}), bf16[8,24,768]{2,1,0:T(8,128)(2,1)S(1)}, u32[]{:S(2)}, u32[]{:S(2)}) async-start(bf16[8,24,768]{2,1,0:T(8,128)(2,1)} %shard_map.131), calls=%async_computation.2 | async-start | bytes 589824 | tf_op jit(solution)/shard_map/all_to_all | solution.py:571
  105.8 1.8 %collective-permute-start.14 = (bf16[32,2048]{1,0:T(8,128)(2,1)S(1)}, bf16[32,2048]{1,0:T(8,128)(2,1)S(1)}, u32[]{:S(2)}, u32[]{:S(2)}) collective-permute-start(bf16[32,2048]{1,0:T(8,128)(2,1)S(1)} %get-tuple-element.63), channel_id=1, source_target_pairs={{0,16},{1,17},{2,18},{3,19},{4,20},{5,21},{6,22},{7,23},{8,24},{9,... | collective-permute-start | bytes 393224 | tf_op jit(solution)/shard_map/ppermute | solution.py:339
  107.6 7.5 %collective-permute-done.14.refs_2_ = bf16[32,2048]{1,0:T(8,128)(2,1)S(1)} collective-permute-done((bf16[32,2048]{1,0:T(8,128)(2,1)S(1)}, bf16[32,2048]{1,0:T(8,128)(2,1)S(1)}, u32[]{:S(2)}, u32[]{:S(2)}) %collective-permute-start.14) | collective-permute-done | bytes 131104 | tf_op jit(solution)/shard_map/ppermute | solution.py:339
  (52 shorter events, 13.7 us)
Async XLA Ops:
  0.6 4.6 %collective-permute-start.1 = (bf16[128,2048]{1,0:T(8,128)(2,1)}, bf16[128,2048]{1,0:T(8,128)(2,1)S(1)}, u32[]{:S(2)}, u32[]{:S(2)}) collective-permute-start(bf16[128,2048]{1,0:T(8,128)(2,1)} %cotangent_own.1), channel_id=1, source_target_pairs={{0,1},{1,0},{2,3},{3,2},{4,5},{5,4},{6,7},{7,6},{8,9},{9,8},{10,11... | collective-permute-start | bytes 1572872 | tf_op jit(solution)/shard_map/ppermute | solution.py:339
  1.1 4.0 %collective-permute-start = (bf16[128,1536]{1,0:T(8,128)(2,1)}, bf16[128,1536]{1,0:T(8,128)(2,1)S(1)}, u32[]{:S(2)}, u32[]{:S(2)}) collective-permute-start(bf16[128,1536]{1,0:T(8,128)(2,1)} %hidden_own), channel_id=1, source_target_pairs={{0,1},{1,0},{2,3},{3,2},{4,5},{5,4},{6,7},{7,6},{8,9},{9,8},{10,11... | collective-permute-start | bytes 1179656 | tf_op jit(solution)/shard_map/ppermute | solution.py:339
  5.2 16.9 %collective-permute-start.3 = (bf16[768,2048]{1,0:T(8,128)(2,1)}, bf16[768,2048]{1,0:T(8,128)(2,1)}, u32[]{:S(2)}, u32[]{:S(2)}) collective-permute-start(bf16[768,2048]{1,0:T(8,128)(2,1)} %weights.1), channel_id=1, source_target_pairs={{0,1},{1,0},{2,3},{3,2},{4,5},{5,4},{6,7},{7,6},{8,9},{9,8},{10,11... | collective-permute-start | bytes 9437192 | tf_op jit(solution)/shard_map/ppermute | solution.py:339
  5.7 42.9 %all-to-all-start = ((bf16[16,24,1664]{2,1,0:T(8,128)(2,1)}), bf16[16,24,1664]{2,1,0:T(8,128)(2,1)S(1)}, u32[]{:S(2)}, u32[]{:S(2)}) async-start(bf16[16,24,1664]{2,1,0:T(8,128)(2,1)} %bitcast.14), calls=%async_computation | async-start | bytes 2555904 | tf_op jit(solution)/shard_map/all_to_all | solution.py:383
  13.7 29.3 %copy-start.8 = (f32[6,16]{1,0:T(8,128)S(1)}, f32[6,16]{1,0:T(8,128)}, u32[]{:S(2)}) copy-start(f32[6,16]{1,0:T(8,128)} %param.17) | copy-start | bytes 1156
  18.1 20.4 %collective-permute-start.2 = (bf16[2,6,128,128]{3,2,1,0:T(8,128)(2,1)}, bf16[2,6,128,128]{3,2,1,0:T(8,128)(2,1)S(1)}, u32[]{:S(2)}, u32[]{:S(2)}) collective-permute-start(bf16[2,6,128,128]{3,2,1,0:T(8,128)(2,1)} %get-tuple-element.38), channel_id=1, source_target_pairs={{0,2},{1,3},{2,0},{3,1},{4,6},{5,7},{6,4},{7,5},{8,10},{9,11},{10,... | collective-permute-start | bytes 1179656 | tf_op jit(solution)/shard_map/ppermute | solution.py:339
  20.0 18.5 %collective-permute-start.4 = (bf16[2,6,128,128]{3,2,1,0:T(8,128)(2,1)}, bf16[2,6,128,128]{3,2,1,0:T(8,128)(2,1)S(1)}, u32[]{:S(2)}, u32[]{:S(2)}) collective-permute-start(bf16[2,6,128,128]{3,2,1,0:T(8,128)(2,1)} %get-tuple-element.42), channel_id=1, source_target_pairs={{0,4},{1,5},{2,6},{3,7},{4,0},{5,1},{6,2},{7,3},{8,12},{9,13},{10,... | collective-permute-start | bytes 1179656 | tf_op jit(solution)/shard_map/ppermute | solution.py:339
  21.5 27.2 %collective-permute-start.5 = (bf16[2,6,128,128]{3,2,1,0:T(8,128)(2,1)}, bf16[2,6,128,128]{3,2,1,0:T(8,128)(2,1)S(1)}, u32[]{:S(2)}, u32[]{:S(2)}) collective-permute-start(bf16[2,6,128,128]{3,2,1,0:T(8,128)(2,1)} %get-tuple-element.46), channel_id=1, source_target_pairs={{0,2},{1,3},{2,0},{3,1},{4,6},{5,7},{6,4},{7,5},{8,10},{9,11},{10,... | collective-permute-start | bytes 1179656 | tf_op jit(solution)/shard_map/ppermute | solution.py:339
  22.0 26.6 %collective-permute-start.6 = (bf16[2,6,128,128]{3,2,1,0:T(8,128)(2,1)}, bf16[2,6,128,128]{3,2,1,0:T(8,128)(2,1)S(1)}, u32[]{:S(2)}, u32[]{:S(2)}) collective-permute-start(bf16[2,6,128,128]{3,2,1,0:T(8,128)(2,1)} %get-tuple-element.47), channel_id=1, source_target_pairs={{0,4},{1,5},{2,6},{3,7},{4,0},{5,1},{6,2},{7,3},{8,12},{9,13},{10,... | collective-permute-start | bytes 1179656 | tf_op jit(solution)/shard_map/ppermute | solution.py:339
  40.6 16.4 %collective-permute-start.8 = (bf16[2,6,128,128]{3,2,1,0:T(8,128)(2,1)}, bf16[2,6,128,128]{3,2,1,0:T(8,128)(2,1)S(1)}, u32[]{:S(2)}, u32[]{:S(2)}) collective-permute-start(bf16[2,6,128,128]{3,2,1,0:T(8,128)(2,1)} %get-tuple-element.44), channel_id=1, source_target_pairs={{0,4},{1,5},{2,6},{3,7},{4,0},{5,1},{6,2},{7,3},{8,12},{9,13},{10,... | collective-permute-start | bytes 1179656 | tf_op jit(solution)/shard_map/ppermute | solution.py:339
  42.1 15.0 %collective-permute-start.9 = (bf16[2,6,128,128]{3,2,1,0:T(8,128)(2,1)}, bf16[2,6,128,128]{3,2,1,0:T(8,128)(2,1)S(1)}, u32[]{:S(2)}, u32[]{:S(2)}) collective-permute-start(bf16[2,6,128,128]{3,2,1,0:T(8,128)(2,1)} %get-tuple-element.45), channel_id=1, source_target_pairs={{0,2},{1,3},{2,0},{3,1},{4,6},{5,7},{6,4},{7,5},{8,10},{9,11},{10,... | collective-permute-start | bytes 1179656 | tf_op jit(solution)/shard_map/ppermute | solution.py:339
  43.0 5.6 %collective-permute-start.7 = (f32[6,16]{1,0:T(8,128)S(1)}, f32[6,16]{1,0:T(8,128)S(1)}, u32[]{:S(2)}, u32[]{:S(2)}) collective-permute-start(f32[6,16]{1,0:T(8,128)S(1)} %copy-done.8), channel_id=1, source_target_pairs={{0,1},{1,0},{2,3},{3,2},{4,5},{5,4},{6,7},{7,6},{8,9},{9,8},{10,11... | collective-permute-start | bytes 1160 | tf_op jit(solution)/shard_map/ppermute | solution.py:339
  59.6 22.8 %copy-start.3 = (f32[6,128,128]{2,1,0:T(8,128)S(1)}, f32[6,128,128]{2,1,0:T(8,128)}, u32[]{:S(2)}) copy-start(f32[6,128,128]{2,1,0:T(8,128)} %moment_second.1) | copy-start | bytes 1179652
  59.6 27.5 %all-to-all-start.1 = ((bf16[4,120,2176]{2,1,0:T(8,128)(2,1)}), bf16[4,120,2176]{2,1,0:T(8,128)(2,1)S(1)}, u32[]{:S(2)}, u32[]{:S(2)}) async-start(bf16[4,120,2176]{2,1,0:T(8,128)(2,1)} %shard_map.125), calls=%async_computation.1 | async-start | bytes 4177920 | tf_op jit(solution)/shard_map/all_to_all | solution.py:526
  63.4 7.8 %collective-permute-start.11 = (bf16[6,128,128]{2,1,0:T(8,128)(2,1)}, bf16[6,128,128]{2,1,0:T(8,128)(2,1)S(1)}, u32[]{:S(2)}, u32[]{:S(2)}) collective-permute-start(bf16[6,128,128]{2,1,0:T(8,128)(2,1)} %get-tuple-element.55), channel_id=1, source_target_pairs={{0,8},{1,9},{2,10},{3,11},{4,12},{5,13},{6,14},{7,15},{8,0},{9,1},... | collective-permute-start | bytes 589832 | tf_op jit(solution)/shard_map/ppermute | solution.py:339
  65.5 9.4 %collective-permute-start.10 = (bf16[6,128,128]{2,1,0:T(8,128)(2,1)}, bf16[6,128,128]{2,1,0:T(8,128)(2,1)S(1)}, u32[]{:S(2)}, u32[]{:S(2)}) collective-permute-start(bf16[6,128,128]{2,1,0:T(8,128)(2,1)} %get-tuple-element.54), channel_id=1, source_target_pairs={{0,8},{1,9},{2,10},{3,11},{4,12},{5,13},{6,14},{7,15},{8,0},{9,1},... | collective-permute-start | bytes 589832 | tf_op jit(solution)/shard_map/ppermute | solution.py:339
  72.2 10.1 %collective-permute-start.12 = (bf16[6,128,128]{2,1,0:T(8,128)(2,1)S(1)}, bf16[6,128,128]{2,1,0:T(8,128)(2,1)S(1)}, u32[]{:S(2)}, u32[]{:S(2)}) collective-permute-start(bf16[6,128,128]{2,1,0:T(8,128)(2,1)S(1)} %shard_map.127), channel_id=1, source_target_pairs={{0,16},{1,17},{2,18},{3,19},{4,20},{5,21},{6,22},{7,23},{8,24},{9,... | collective-permute-start | bytes 589832 | tf_op jit(solution)/shard_map/ppermute | solution.py:339
  84.5 7.2 %collective-permute-start.17 = (bf16[6,128,128]{2,1,0:T(8,128)(2,1)S(1)}, bf16[6,128,128]{2,1,0:T(8,128)(2,1)S(1)}, u32[]{:S(2)}, u32[]{:S(2)}) collective-permute-start(bf16[6,128,128]{2,1,0:T(8,128)(2,1)S(1)} %get-tuple-element.57.refs_2_), channel_id=1, source_target_pairs={{0,16},{1,17},{2,18},{3,19},{4,20},{5,21},{6,22},{7,23},{8,24},{9,... | collective-permute-start | bytes 589832 | tf_op jit(solution)/shard_map/ppermute | solution.py:339
  87.2 12.9 %collective-permute-start.15 = (bf16[4,24,1536]{2,1,0:T(8,128)(2,1)S(1)}, bf16[4,24,1536]{2,1,0:T(8,128)(2,1)S(1)}, u32[]{:S(2)}, u32[]{:S(2)}) collective-permute-start(bf16[4,24,1536]{2,1,0:T(8,128)(2,1)S(1)} %slice.4.refs_0_), channel_id=1, source_target_pairs={{0,1},{1,0},{2,3},{3,2},{4,5},{5,4},{6,7},{7,6},{8,9},{9,8},{10,11... | collective-permute-start | bytes 884744 | tf_op jit(solution)/shard_map/ppermute | solution.py:339
  87.3 8.6 %collective-permute-start.16 = (bf16[6,128,128]{2,1,0:T(8,128)(2,1)S(1)}, bf16[6,128,128]{2,1,0:T(8,128)(2,1)S(1)}, u32[]{:S(2)}, u32[]{:S(2)}) collective-permute-start(bf16[6,128,128]{2,1,0:T(8,128)(2,1)S(1)} %get-tuple-element.57.refs_2_), channel_id=1, source_target_pairs={{0,8},{1,9},{2,10},{3,11},{4,12},{5,13},{6,14},{7,15},{8,0},{9,1},... | collective-permute-start | bytes 589832 | tf_op jit(solution)/shard_map/ppermute | solution.py:339
  91.8 8.4 %collective-permute-start.18 = (bf16[6,128,128]{2,1,0:T(8,128)(2,1)S(1)}, bf16[6,128,128]{2,1,0:T(8,128)(2,1)S(1)}, u32[]{:S(2)}, u32[]{:S(2)}) collective-permute-start(bf16[6,128,128]{2,1,0:T(8,128)(2,1)S(1)} %collective-permute-done.17.refs_4_), channel_id=1, source_target_pairs={{0,8},{1,9},{2,10},{3,11},{4,12},{5,13},{6,14},{7,15},{8,0},{9,1},... | collective-permute-start | bytes 589832 | tf_op jit(solution)/shard_map/ppermute | solution.py:339
  93.1 12.6 %collective-permute-start.13 = (bf16[2,32,2048]{2,1,0:T(8,128)(2,1)S(1)}, bf16[2,32,2048]{2,1,0:T(8,128)(2,1)S(1)}, u32[]{:S(2)}, u32[]{:S(2)}) collective-permute-start(bf16[2,32,2048]{2,1,0:T(8,128)(2,1)S(1)} %get-tuple-element.59), channel_id=1, source_target_pairs={{0,8},{1,9},{2,10},{3,11},{4,12},{5,13},{6,14},{7,15},{8,0},{9,1},... | collective-permute-start | bytes 786440 | tf_op jit(solution)/shard_map/ppermute | solution.py:339
  101.4 13.7 %all-to-all-start.2 = ((bf16[8,24,768]{2,1,0:T(8,128)(2,1)}), bf16[8,24,768]{2,1,0:T(8,128)(2,1)S(1)}, u32[]{:S(2)}, u32[]{:S(2)}) async-start(bf16[8,24,768]{2,1,0:T(8,128)(2,1)} %shard_map.131), calls=%async_computation.2 | async-start | bytes 589824 | tf_op jit(solution)/shard_map/all_to_all | solution.py:571
  105.8 9.3 %collective-permute-start.14 = (bf16[32,2048]{1,0:T(8,128)(2,1)S(1)}, bf16[32,2048]{1,0:T(8,128)(2,1)S(1)}, u32[]{:S(2)}, u32[]{:S(2)}) collective-permute-start(bf16[32,2048]{1,0:T(8,128)(2,1)S(1)} %get-tuple-element.63), channel_id=1, source_target_pairs={{0,16},{1,17},{2,18},{3,19},{4,20},{5,21},{6,22},{7,23},{8,24},{9,... | collective-permute-start | bytes 393224 | tf_op jit(solution)/shard_map/ppermute | solution.py:339
  (7 other events, 66.0 us)

commit v4 on v3

--- a/solution.py
+++ b/solution.py
@@ -167,15 +167,25 @@
     out_b[...] = (arrived_b[...].astype(F32) + held_b[...].astype(F32)).astype(BF16)
 
 
+def far_sum_kernel(far_ref, *rest):
+    parts, out = rest[:6], rest[6]
+    for half in range(2):
+
+        @pl.when(far_ref[0] // 2 == half)
+        def _(pieces=parts[3 * half : 3 * half + 3]):
+            one, two, three = (piece[0].astype(F32) for piece in pieces)
+            out[...] = (one + two + three).astype(out.dtype)
+
+
 def second_sum_kernel(floor_ref, *rest):
-    parts, outs, total = rest[:6], rest[6:10], rest[10]
+    parts, outs, total = rest[:6], rest[6:9], rest[9]
     highs = parts[0].shape[0]
     for half in range(2):
         one, two, three = parts[3 * half : 3 * half + 3]
         total[half * highs : (half + 1) * highs] = (
             one[...].astype(F32) + two[...].astype(F32) + three[...].astype(F32)
         )
-    for flip, out in zip((3, 1, 2, 0), outs, strict=True):
+    for flip, out in zip((1, 2, 0), outs, strict=True):
         out[...] = total[floor_ref[0] ^ flip].astype(out.dtype)
 
 
@@ -223,31 +233,29 @@
             )
 
 
-def trained_kernel(device_ref, plane, depth, column_blocks, *rest):
-    given, weights = rest[:2], rest[2 : 2 + depth]
-    out, rows = rest[2 + depth :]
+def trained_kernel(device_ref, plane, depth, column_blocks, rows, *rest):
+    weights, outs = rest[: 2 * depth], rest[2 * depth :]
     device = device_ref[0]
     blocks, side, _ = weights[0].shape
-    inner = device % plane
     floor = device // plane
-    chips, count, _ = given[0].shape
-    for row_block in range(rows.shape[0]):
-        at = slice(row_block * side, (row_block + 1) * side)
-        rows[row_block] = jnp.concatenate(
-            [part[chip, :, at] for part in given for chip in range(chips)], axis=0
-        )
-    for at in range(blocks):
-        total = jnp.zeros((rows.shape[1], side), F32)
-        for flip in range(depth):
-            block = ((floor ^ flip) * plane + inner) * blocks + at
-            row_block = block // column_blocks
-            total = total + jnp.dot(rows[row_block], weights[flip][at], preferred_element_type=F32)
-        for core in range(2):
-            for chip in range(chips):
-                top = (core * chips + chip) * count
-                out[2 * chip + (device % 2 ^ core), :, at * side : (at + 1) * side] = total[
-                    top : top + count
-                ].astype(BF16)
+    chip = device % plane // 2
+    chips, count, _ = rows.shape
+    for core in range(2):
+        number = device % 2 ^ core
+        for at in range(blocks):
+            total = jnp.zeros((chips * count, side), F32)
+            for flip in range(depth):
+                block = (floor ^ flip) * plane * blocks + (chip * 2 + number) * blocks + at
+                start = pl.multiple_of(block // column_blocks * side, side)
+                part = jnp.concatenate(
+                    [rows[chip ^ turn, :, pl.ds(start, side)] for turn in range(chips)], axis=0
+                )
+                total = total + jnp.dot(
+                    part, weights[core * depth + flip][at], preferred_element_type=F32
+                )
+            column = pl.ds(pl.multiple_of((number * blocks + at) * side, side), side)
+            for turn in range(chips):
+                outs[turn][:, column] = total[turn * count : (turn + 1) * count].astype(BF16)
 
 
 def mix_kernel(depth, plane_slots, floor_ref, returned, own, across, sent):
@@ -281,27 +289,22 @@
     out_own[...] = arrived[0].astype(F32) + own[...]
 
 
-def combine_kernel(side, gates_trained, near, across, trained, out):
-    peers, _, width = trained.shape
+def combine_kernel(chip_ref, chips, side, gates_trained, near, across, *rest):
+    trained, out, fresh = rest[:chips], rest[chips], rest[chips + 1]
     columns = out.shape[1]
-    blocks = width // side
+    blocks = trained[0].shape[1] // side
     count = out.shape[0]
-    wide = 4
-    for column in range(0, columns // side, wide):
-        fresh = []
-        for place in range(column, column + wide):
-            total = None
-            for number in range(place, peers * blocks, columns // side):
-                peer, block = divmod(number, blocks)
-                piece = trained[peer, :, block * side : (block + 1) * side].astype(F32)
-                total = piece if total is None else total + piece
-            fresh.append(total.astype(BF16))
-        at = slice(column * side, (column + wide) * side)
-        both = jnp.dot(
-            gates_trained[...], jnp.concatenate(fresh, axis=1), preferred_element_type=F32
-        )
-        total = both[:count] + both[count:]
-        total = total + near[:, at] + across[:, at].astype(F32)
+    fresh[...] = jnp.zeros_like(fresh)
+    for turn in range(chips):
+        for at in range(blocks):
+            number = ((chip_ref[0] ^ turn) * blocks + at) % (columns // side)
+            column = pl.ds(pl.multiple_of(number * side, side), side)
+            fresh[:, column] += trained[turn][:, at * side : (at + 1) * side].astype(F32)
+    wide = 512
+    for column in range(0, columns, wide):
+        at = slice(column, column + wide)
+        both = jnp.dot(gates_trained[...], fresh[:, at].astype(BF16), preferred_element_type=F32)
+        total = both[:count] + both[count:] + near[:, at] + across[:, at].astype(F32)
         out[:, at] = total.astype(out.dtype)
 
 
@@ -462,28 +465,33 @@
     block_shape = (blocks, side, side)
     if highs == 2:
         expert_out = expert_sum(after(received, sums, first_a, first_b))
-        far, near, across, own = pl.pallas_call(
+        parts = stay_a, first_a, second_a, stay_b, first_b, second_b
+        high = (device // 8).astype(jnp.int32).reshape(1)
+        piece = pl.BlockSpec((1,) + block_shape, lambda i, far: (far[0] % 2, 0, 0, 0))
+        far = pl.pallas_call(
+            far_sum_kernel,
+            out_shape=jax.ShapeDtypeStruct(block_shape, BF16),
+            grid_spec=pltpu.PrefetchScalarGridSpec(
+                num_scalar_prefetch=1,
+                grid=(1,),
+                in_specs=[piece] * 6,
+                out_specs=pl.BlockSpec(block_shape, lambda i, far: (0, 0, 0)),
+            ),
+            compiler_params=PARAMS,
+        )(high ^ 3, *parts)
+        expert_out = after(expert_out, far)
+        near, across, own = pl.pallas_call(
             second_sum_kernel,
             out_shape=(
-                pltpu.HBM(block_shape, BF16),
-                pltpu.HBM(block_shape, BF16),
-                pltpu.HBM(block_shape, F32),
-                pltpu.HBM(block_shape, F32),
+                jax.ShapeDtypeStruct(block_shape, BF16),
+                jax.ShapeDtypeStruct(block_shape, F32),
+                jax.ShapeDtypeStruct(block_shape, F32),
             ),
             in_specs=[smem] + vmem(6),
-            out_specs=tuple(vmem(4)),
+            out_specs=tuple(vmem(3)),
             scratch_shapes=[pltpu.VMEM((4,) + block_shape, F32)],
             compiler_params=PARAMS,
-        )(
-            (device // 8).astype(jnp.int32).reshape(1),
-            *in_hbm(stay_a),
-            first_a,
-            second_a,
-            *in_hbm(stay_b),
-            first_b,
-            second_b,
-        )
-        expert_out = after(expert_out, own)
+        )(after(high, far), *parts)
         far, near = flip(far, 8), flip(near, 8)
         across = pl.pallas_call(
             third_sum_kernel,
@@ -491,7 +499,7 @@
             in_specs=vmem(2),
             out_specs=vmem(1)[0],
             compiler_params=PARAMS,
-        )(far, *in_hbm(across))
+        )(far, across)
         gradient = [own, near, flip(across, 16)]
     else:
         expert_out = expert_sum(received)
@@ -527,7 +535,6 @@
         expert_out, "dp", split_axis=0, concat_axis=0, tiled=True, axis_index_groups=same_core
     )
     rows_trained = returned[:, plane_slots:, :hidden_width]
-    rows_other = flip(rows_trained, 1)
     row_shape = (row_count, columns)
     mixed, across_rows, sent_rows = pl.pallas_call(
         lambda *refs: mix_kernel(depth, plane_slots, *refs),
@@ -559,25 +566,25 @@
         for key in list(held):
             held[key | mask] = flip(held[key], mask * plane)
         mask //= 2
+    blocks_held = [held[z] for z in range(depth)]
+    blocks_held += [flip(block, 1) for block in blocks_held]
+    chip_ref = (device % plane // 2).astype(jnp.int32).reshape(1)
     trained = pl.pallas_call(
         lambda device_ref, *refs: trained_kernel(device_ref, plane, depth, column_blocks, *refs),
-        out_shape=pltpu.HBM((plane, pair_slots, blocks * side), BF16),
-        in_specs=[smem] + vmem(2 + depth),
+        out_shape=(jax.ShapeDtypeStruct((pair_slots, 2 * blocks * side), BF16),) * chips,
+        in_specs=[smem] + vmem(1 + 2 * depth),
+        out_specs=tuple(vmem(chips)),
+        compiler_params=PARAMS,
+    )(device_ref, after(rows_trained, mixed), *blocks_held)
+    trained = [trained[0]] + [flip(trained[turn], 2 * turn) for turn in range(1, chips)]
+    decoded = pl.pallas_call(
+        lambda chip_ref, *refs: combine_kernel(chip_ref, chips, side, *refs),
+        out_shape=jax.ShapeDtypeStruct((row_count, columns), BF16),
+        in_specs=[smem] + vmem(3 + chips),
         out_specs=vmem(1)[0],
-        scratch_shapes=[pltpu.VMEM((row_blocks, plane * pair_slots, side), BF16)],
-        compiler_params=PARAMS,
-    )(device_ref, after(rows_trained, mixed), rows_other, *[held[z] for z in range(depth)])
-    planes = [[z * plane + i for i in range(plane)] for z in range(depth)]
-    trained = lax.all_to_all(
-        trained, "dp", split_axis=0, concat_axis=0, tiled=True, axis_index_groups=planes
-    )
-    decoded = pl.pallas_call(
-        lambda *refs: combine_kernel(side, *refs),
-        out_shape=jax.ShapeDtypeStruct((row_count, columns), BF16),
-        in_specs=vmem(4),
-        out_specs=vmem(1)[0],
-        compiler_params=PARAMS,
-    )(gates_trained, mixed_near, across_rows, trained)
+        scratch_shapes=[pltpu.VMEM((pair_slots, columns), F32)],
+        compiler_params=PARAMS,
+    )(chip_ref, gates_trained, mixed_near, across_rows, *trained)
     return (decoded.reshape(steps, step_rows, columns), new_master)
 
 

time: 117 us -> 111 us (0.949)
  waiting for transfers between devices: 54.1 us -> 46.9 us
    ppermute x19 -> x25, starting transfers between devices: 17.3 us -> 22.5 us  [flip(): return lax.ppermute(array, 'dp', [(i, i ^ mask) for i in range(devices)])]
    ppermute x19 -> x25, waiting for transfers between devices: 51.4 us -> 46.9 us  [flip(): return lax.ppermute(array, 'dp', [(i, i ^ mask) for i in range(devices)])]
    all_to_all x1 -> x0, starting transfers between devices: 3.91 us -> none  [local(): lax.all_to_all(trained, 'dp', split_axis=0, concat_axis=0, tiled=True, ax...]
    all_to_all x1, waiting for transfers between devices: 2.67 us -> 0.01 us  [local(): lax.all_to_all(expert_out, 'dp', split_axis=0, concat_axis=0, tiled=True,...]
    unnamed x18 -> x28, local copies, waits for them, and re-layouts: 3.57 us -> 4.59 us
    pallas_call x2 -> x3, Pallas kernels: 3.48 us -> 3.89 us  [the longest x1 1.61 us: local(): pl.pallas_call(second_sum_kernel, out_shape=(jax.ShapeDtypeStruct(block_s...]
  transfers between devices with their start and end apart: 22 -> 27, of which waited for: 11 -> 11; matrix products, arithmetic and copies ran while one was open for 0% -> 0% of each run, Pallas kernels for 18% -> 19%
where the time goes in v4:
time: 111 us; the launch traced here: 110 us
  waiting for transfers between devices  46.9 us (42%)
  starting transfers between devices  34 us (31%)
  Pallas kernels  23.4 us (21%)
  local copies, waits for them, and re-layouts  4.75 us (4%)
    ppermute x25, waiting for transfers between devices, flip(): return lax.ppermute(array, 'dp', [(i, i ^ mask) for i in range(devices)])  46.9 us
    ppermute x25, starting transfers between devices, flip(): return lax.ppermute(array, 'dp', [(i, i ^ mask) for i in range(devices)])  22.5 us
    all_to_all x1, starting transfers between devices, local(): lax.all_to_all(after(packed, hidden_other, cotangent_other).reshape(exper...  7.94 us
    pallas_call x1, Pallas kernels, expert_sum(): pl.pallas_call(expert_kernel, out_shape=pltpu.HBM(sent_shape, BF16), grid...  6.48 us
    unnamed x28, local copies, waits for them, and re-layouts  4.59 us
    pallas_call x1, Pallas kernels, local(): pl.pallas_call(gradient_kernel, out_shape=(pltpu.HBM(part.shape, BF16),)...  4.4 us
    all_to_all x1, starting transfers between devices, local(): lax.all_to_all(expert_out, 'dp', split_axis=0, concat_axis=0, tiled=True,...  3.62 us
    pallas_call x1, Pallas kernels, local(): pl.pallas_call(lambda *refs: pack_kernel(steps, capacity, depth, *refs),...  3.32 us
  transfers between devices with their start and end apart: 27, of which 11 were waited for; matrix products, arithmetic and copies ran while one was open for 0% of the time, Pallas kernels for 19%

profile of v4, /device:TPU:0, one launch (start us, length us, event | category | flops | bytes accessed | tf_op | source)
XLA Modules:
  0.0 109.9 jit_solution(9061895556003717077)
XLA Ops:
  1.9 3.3 %shard_map.122 = (bf16[384,1664]{1,0:T(8,128)(2,1)}, bf16[64,24]{1,0:T(8,128)(2,1)S(1)}, bf16[24,1536]{1,0:T(8,128)(2,1)S(1)}) custom-call(s32[16]{0:T(128)S(1)} %copy-done.10, s32[32,8]{1,0:T(8,128)} %bitcast.18, f32[32,8]{1,0:T(8,128)} %bitcast.19, bf16[256,1536]{1,0:T(8,128)(2,1)} %bitcast.16), custom_call_target="tpu_custom_call" | custom-call | tf_op jit(solution)/shard_map/pallas_call | solution.py:363
  5.7 7.9 %all-to-all-start = ((bf16[16,24,1664]{2,1,0:T(8,128)(2,1)}), bf16[16,24,1664]{2,1,0:T(8,128)(2,1)S(1)}, u32[]{:S(2)}, u32[]{:S(2)}) async-start(bf16[16,24,1664]{2,1,0:T(8,128)(2,1)} %bitcast.15), calls=%async_computation | async-start | bytes 2555904 | tf_op jit(solution)/shard_map/all_to_all | solution.py:386
  13.7 4.4 %shard_map.123 = (bf16[2,6,128,128]{3,2,1,0:T(8,128)(2,1)}, bf16[2,6,128,128]{3,2,1,0:T(8,128)(2,1)}, bf16[2,6,128,128]{3,2,1,0:T(8,128)(2,1)}, bf16[2,6,128,128...) custom-call(s32[1]{0:T(128)} %bitcast.8.device_ref, ...), custom_call_target="tpu_custom_call" | custom-call | tf_op jit(solution)/shard_map/pallas_call | solution.py:399
  18.1 1.9 %collective-permute-start.2 = (bf16[2,6,128,128]{3,2,1,0:T(8,128)(2,1)}, bf16[2,6,128,128]{3,2,1,0:T(8,128)(2,1)S(1)}, u32[]{:S(2)}, u32[]{:S(2)}) collective-permute-start(bf16[2,6,128,128]{3,2,1,0:T(8,128)(2,1)} %get-tuple-element.42), channel_id=1, source_target_pairs={{0,2},{1,3},{2,0},{3,1},{4,6},{5,7},{6,4},{7,5},{8,10},{9,11},{10,... | collective-permute-start | bytes 1179656 | tf_op jit(solution)/shard_map/ppermute | solution.py:342
  22.2 16.3 %collective-permute-done.2.arrived_a = bf16[2,6,128,128]{3,2,1,0:T(8,128)(2,1)S(1)} collective-permute-done((bf16[2,6,128,128]{3,2,1,0:T(8,128)(2,1)}, bf16[2,6,128,128]{3,2,1,0:T(8,128)(2,1)S(1)}, u32[]{:S(2)}, u32[]{:S(2)}) %collective-permute-start.2) | collective-permute-done | bytes 393248 | tf_op jit(solution)/shard_map/ppermute | solution.py:342
  38.5 2.1 %shard_map.124 = (bf16[2,6,128,128]{3,2,1,0:T(8,128)(2,1)}, bf16[2,6,128,128]{3,2,1,0:T(8,128)(2,1)}) custom-call(bf16[2,6,128,128]{3,2,1,0:T(8,128)(2,1)S(1)} %collective-permute-done.2.arrived_a, bf16[2,6,128,128]{3,2,1,0:T(8,128)(2,1)} %get-tuple-element.45.held_a, bf16[2,6,128,128]{3,2,1,0:T(8,128)(2,1)S(1)} %collective-permute-done.4.arrived_b, ...), custom_call_target="tpu_custom_call" | custom-call | tf_op jit(solution)/shard_map/pallas_call | solution.py:419
  40.6 1.5 %collective-permute-start.8 = (bf16[2,6,128,128]{3,2,1,0:T(8,128)(2,1)}, bf16[2,6,128,128]{3,2,1,0:T(8,128)(2,1)S(1)}, u32[]{:S(2)}, u32[]{:S(2)}) collective-permute-start(bf16[2,6,128,128]{3,2,1,0:T(8,128)(2,1)} %get-tuple-element.48), channel_id=1, source_target_pairs={{0,4},{1,5},{2,6},{3,7},{4,0},{5,1},{6,2},{7,3},{8,12},{9,13},{10,... | collective-permute-start | bytes 1179656 | tf_op jit(solution)/shard_map/ppermute | solution.py:342
  43.0 5.6 %collective-permute-done.5.rest_1_ = bf16[2,6,128,128]{3,2,1,0:T(8,128)(2,1)S(1)} collective-permute-done((bf16[2,6,128,128]{3,2,1,0:T(8,128)(2,1)}, bf16[2,6,128,128]{3,2,1,0:T(8,128)(2,1)S(1)}, u32[]{:S(2)}, u32[]{:S(2)}) %collective-permute-start.5) | collective-permute-done | bytes 393248 | tf_op jit(solution)/shard_map/ppermute | solution.py:342
  48.8 1.9 %copy-done = bf16[768,2048]{1,0:T(8,128)(2,1)S(1)} copy-done((bf16[768,2048]{1,0:T(8,128)(2,1)S(1)}, bf16[768,2048]{1,0:T(8,128)(2,1)}, u32[]{:S(2)}) %copy-start) | copy-done | bytes 3145752
  50.7 6.5 %shard_map.125 = bf16[4,120,2176]{2,1,0:T(8,128)(2,1)} custom-call(s32[1]{0:T(128)} %bitcast.5.core_ref, bf16[384,1664]{1,0:T(8,128)(2,1)S(1)} %bitcast.12, bf16[24,1536]{1,0:T(8,128)(2,1)S(1)} %get-tuple-element.53.rows_trained, bf16[768,2048]{1,0:T(8,128)(2,1)S(1)} %copy-done, bf16[768,2048]{1,0:T(8,128)(2,1)} %collective-permute-done.3.weights_other, ...), custom_call_target="tpu_custom_call" | custom-call | tf_op jit(solution)/shard_map/pallas_call | solution.py:436
  58.4 3.6 %all-to-all-start.1 = ((bf16[4,120,2176]{2,1,0:T(8,128)(2,1)}), bf16[4,120,2176]{2,1,0:T(8,128)(2,1)S(1)}, u32[]{:S(2)}, u32[]{:S(2)}) async-start(bf16[4,120,2176]{2,1,0:T(8,128)(2,1)} %shard_map.125), calls=%async_computation.1 | async-start | bytes 4177920 | tf_op jit(solution)/shard_map/all_to_all | solution.py:534
  62.0 2.1 %collective-permute-start.11 = (bf16[6,128,128]{2,1,0:T(8,128)(2,1)S(1)}, bf16[6,128,128]{2,1,0:T(8,128)(2,1)S(1)}, u32[]{:S(2)}, u32[]{:S(2)}) collective-permute-start(bf16[6,128,128]{2,1,0:T(8,128)(2,1)S(1)} %shard_map.126), channel_id=1, source_target_pairs={{0,8},{1,9},{2,10},{3,11},{4,12},{5,13},{6,14},{7,15},{8,0},{9,1},... | collective-permute-start | bytes 589832 | tf_op jit(solution)/shard_map/ppermute | solution.py:342
  66.1 1.6 %shard_map.127 = (bf16[6,128,128]{2,1,0:T(8,128)(2,1)S(1)}, f32[6,128,128]{2,1,0:T(8,128)S(1)}, f32[6,128,128]{2,1,0:T(8,128)S(1)}) custom-call(s32[1]{0:T(128)} %bitcast.4.floor_ref.refs_0_, bf16[2,6,128,128]{3,2,1,0:T(8,128)(2,1)S(1)} %copy-done.1, bf16[2,6,128,128]{3,2,1,0:T(8,128)(2,1)S(1)} %collective-permute-done.5.rest_1_, ...), custom_call_target="tpu_custom_call" | custom-call | tf_op jit(solution)/shard_map/pallas_call | solution.py:483
  68.5 2.4 %collective-permute-start.12 = (bf16[6,128,128]{2,1,0:T(8,128)(2,1)S(1)}, bf16[6,128,128]{2,1,0:T(8,128)(2,1)S(1)}, u32[]{:S(2)}, u32[]{:S(2)}) collective-permute-start(bf16[6,128,128]{2,1,0:T(8,128)(2,1)S(1)} %shard_map.128), channel_id=1, source_target_pairs={{0,16},{1,17},{2,18},{3,19},{4,20},{5,21},{6,22},{7,23},{8,24},{9,... | collective-permute-start | bytes 589832 | tf_op jit(solution)/shard_map/ppermute | solution.py:342
  70.9 4.9 %collective-permute-done.10.rest_1_ = bf16[6,128,128]{2,1,0:T(8,128)(2,1)S(1)} collective-permute-done((bf16[6,128,128]{2,1,0:T(8,128)(2,1)S(1)}, bf16[6,128,128]{2,1,0:T(8,128)(2,1)S(1)}, u32[]{:S(2)}, u32[]{:S(2)}) %collective-permute-start.10) | collective-permute-done | bytes 196640 | tf_op jit(solution)/shard_map/ppermute | solution.py:342
  75.8 3.2 %collective-permute-done.12.rest_2_ = bf16[6,128,128]{2,1,0:T(8,128)(2,1)S(1)} collective-permute-done((bf16[6,128,128]{2,1,0:T(8,128)(2,1)S(1)}, bf16[6,128,128]{2,1,0:T(8,128)(2,1)S(1)}, u32[]{:S(2)}, u32[]{:S(2)}) %collective-permute-start.12) | collective-permute-done | bytes 196640 | tf_op jit(solution)/shard_map/ppermute | solution.py:342
  80.4 2.5 %collective-permute-start.15 = (bf16[6,128,128]{2,1,0:T(8,128)(2,1)S(1)}, bf16[6,128,128]{2,1,0:T(8,128)(2,1)S(1)}, u32[]{:S(2)}, u32[]{:S(2)}) collective-permute-start(bf16[6,128,128]{2,1,0:T(8,128)(2,1)S(1)} %get-tuple-element.61.refs_1_), channel_id=1, source_target_pairs={{0,8},{1,9},{2,10},{3,11},{4,12},{5,13},{6,14},{7,15},{8,0},{9,1},... | collective-permute-start | bytes 589832 | tf_op jit(solution)/shard_map/ppermute | solution.py:342
  82.8 5.8 %collective-permute-done.16.refs_3_ = bf16[6,128,128]{2,1,0:T(8,128)(2,1)S(1)} collective-permute-done((bf16[6,128,128]{2,1,0:T(8,128)(2,1)S(1)}, bf16[6,128,128]{2,1,0:T(8,128)(2,1)S(1)}, u32[]{:S(2)}, u32[]{:S(2)}) %collective-permute-start.16) | collective-permute-done | bytes 196640 | tf_op jit(solution)/shard_map/ppermute | solution.py:342
  90.0 2.1 %collective-permute-start.13 = (bf16[2,32,2048]{2,1,0:T(8,128)(2,1)S(1)}, bf16[2,32,2048]{2,1,0:T(8,128)(2,1)S(1)}, u32[]{:S(2)}, u32[]{:S(2)}) collective-permute-start(bf16[2,32,2048]{2,1,0:T(8,128)(2,1)S(1)} %get-tuple-element.63), channel_id=1, source_target_pairs={{0,8},{1,9},{2,10},{3,11},{4,12},{5,13},{6,14},{7,15},{8,0},{9,1},... | collective-permute-start | bytes 786440 | tf_op jit(solution)/shard_map/ppermute | solution.py:342
  92.7 3.0 %collective-permute-done.17.refs_4_ = bf16[6,128,128]{2,1,0:T(8,128)(2,1)S(1)} collective-permute-done((bf16[6,128,128]{2,1,0:T(8,128)(2,1)S(1)}, bf16[6,128,128]{2,1,0:T(8,128)(2,1)S(1)}, u32[]{:S(2)}, u32[]{:S(2)}) %collective-permute-start.17) | collective-permute-done | bytes 196640 | tf_op jit(solution)/shard_map/ppermute | solution.py:342
  95.6 2.8 %collective-permute-done.13.arrived = bf16[2,32,2048]{2,1,0:T(8,128)(2,1)S(1)} collective-permute-done((bf16[2,32,2048]{2,1,0:T(8,128)(2,1)S(1)}, bf16[2,32,2048]{2,1,0:T(8,128)(2,1)S(1)}, u32[]{:S(2)}, u32[]{:S(2)}) %collective-permute-start.13) | collective-permute-done | bytes 262176 | tf_op jit(solution)/shard_map/ppermute | solution.py:342
  100.6 2.1 %collective-permute-start.22 = (bf16[24,1536]{1,0:T(8,128)(2,1)S(1)}, bf16[24,1536]{1,0:T(8,128)(2,1)S(1)}, u32[]{:S(2)}, u32[]{:S(2)}) collective-permute-start(bf16[24,1536]{1,0:T(8,128)(2,1)S(1)} %get-tuple-element.70), channel_id=1, source_target_pairs={{0,2},{1,3},{2,0},{3,1},{4,6},{5,7},{6,4},{7,5},{8,10},{9,11},{10,... | collective-permute-start | bytes 221192 | tf_op jit(solution)/shard_map/ppermute | solution.py:342
  105.4 1.6 %collective-permute-done.23.refs_5_ = bf16[24,1536]{1,0:T(8,128)(2,1)S(1)} collective-permute-done((bf16[24,1536]{1,0:T(8,128)(2,1)S(1)}, bf16[24,1536]{1,0:T(8,128)(2,1)S(1)}, u32[]{:S(2)}, u32[]{:S(2)}) %collective-permute-start.23) | collective-permute-done | bytes 73760 | tf_op jit(solution)/shard_map/ppermute | solution.py:342
  107.0 1.8 %collective-permute-done.24.refs_6_ = bf16[24,1536]{1,0:T(8,128)(2,1)S(1)} collective-permute-done((bf16[24,1536]{1,0:T(8,128)(2,1)S(1)}, bf16[24,1536]{1,0:T(8,128)(2,1)S(1)}, u32[]{:S(2)}, u32[]{:S(2)}) %collective-permute-start.24) | collective-permute-done | bytes 73760 | tf_op jit(solution)/shard_map/ppermute | solution.py:342
  (73 shorter events, 18.1 us)
Async XLA Ops:
  0.6 4.6 %collective-permute-start.1 = (bf16[128,2048]{1,0:T(8,128)(2,1)}, bf16[128,2048]{1,0:T(8,128)(2,1)S(1)}, u32[]{:S(2)}, u32[]{:S(2)}) collective-permute-start(bf16[128,2048]{1,0:T(8,128)(2,1)} %cotangent_own.1), channel_id=1, source_target_pairs={{0,1},{1,0},{2,3},{3,2},{4,5},{5,4},{6,7},{7,6},{8,9},{9,8},{10,11... | collective-permute-start | bytes 1572872 | tf_op jit(solution)/shard_map/ppermute | solution.py:342
  5.2 16.9 %collective-permute-start.3 = (bf16[768,2048]{1,0:T(8,128)(2,1)}, bf16[768,2048]{1,0:T(8,128)(2,1)}, u32[]{:S(2)}, u32[]{:S(2)}) collective-permute-start(bf16[768,2048]{1,0:T(8,128)(2,1)} %weights.1), channel_id=1, source_target_pairs={{0,1},{1,0},{2,3},{3,2},{4,5},{5,4},{6,7},{7,6},{8,9},{9,8},{10,11... | collective-permute-start | bytes 9437192 | tf_op jit(solution)/shard_map/ppermute | solution.py:342
  5.7 42.9 %all-to-all-start = ((bf16[16,24,1664]{2,1,0:T(8,128)(2,1)}), bf16[16,24,1664]{2,1,0:T(8,128)(2,1)S(1)}, u32[]{:S(2)}, u32[]{:S(2)}) async-start(bf16[16,24,1664]{2,1,0:T(8,128)(2,1)} %bitcast.15), calls=%async_computation | async-start | bytes 2555904 | tf_op jit(solution)/shard_map/all_to_all | solution.py:386
  18.1 20.4 %collective-permute-start.2 = (bf16[2,6,128,128]{3,2,1,0:T(8,128)(2,1)}, bf16[2,6,128,128]{3,2,1,0:T(8,128)(2,1)S(1)}, u32[]{:S(2)}, u32[]{:S(2)}) collective-permute-start(bf16[2,6,128,128]{3,2,1,0:T(8,128)(2,1)} %get-tuple-element.42), channel_id=1, source_target_pairs={{0,2},{1,3},{2,0},{3,1},{4,6},{5,7},{6,4},{7,5},{8,10},{9,11},{10,... | collective-permute-start | bytes 1179656 | tf_op jit(solution)/shard_map/ppermute | solution.py:342
  20.0 18.5 %collective-permute-start.4 = (bf16[2,6,128,128]{3,2,1,0:T(8,128)(2,1)}, bf16[2,6,128,128]{3,2,1,0:T(8,128)(2,1)S(1)}, u32[]{:S(2)}, u32[]{:S(2)}) collective-permute-start(bf16[2,6,128,128]{3,2,1,0:T(8,128)(2,1)} %get-tuple-element.46), channel_id=1, source_target_pairs={{0,4},{1,5},{2,6},{3,7},{4,0},{5,1},{6,2},{7,3},{8,12},{9,13},{10,... | collective-permute-start | bytes 1179656 | tf_op jit(solution)/shard_map/ppermute | solution.py:342
  21.5 27.1 %collective-permute-start.5 = (bf16[2,6,128,128]{3,2,1,0:T(8,128)(2,1)}, bf16[2,6,128,128]{3,2,1,0:T(8,128)(2,1)S(1)}, u32[]{:S(2)}, u32[]{:S(2)}) collective-permute-start(bf16[2,6,128,128]{3,2,1,0:T(8,128)(2,1)} %get-tuple-element.50), channel_id=1, source_target_pairs={{0,2},{1,3},{2,0},{3,1},{4,6},{5,7},{6,4},{7,5},{8,10},{9,11},{10,... | collective-permute-start | bytes 1179656 | tf_op jit(solution)/shard_map/ppermute | solution.py:342
  22.1 26.6 %collective-permute-start.6 = (bf16[2,6,128,128]{3,2,1,0:T(8,128)(2,1)}, bf16[2,6,128,128]{3,2,1,0:T(8,128)(2,1)S(1)}, u32[]{:S(2)}, u32[]{:S(2)}) collective-permute-start(bf16[2,6,128,128]{3,2,1,0:T(8,128)(2,1)} %get-tuple-element.51), channel_id=1, source_target_pairs={{0,4},{1,5},{2,6},{3,7},{4,0},{5,1},{6,2},{7,3},{8,12},{9,13},{10,... | collective-permute-start | bytes 1179656 | tf_op jit(solution)/shard_map/ppermute | solution.py:342
  40.6 16.6 %collective-permute-start.8 = (bf16[2,6,128,128]{3,2,1,0:T(8,128)(2,1)}, bf16[2,6,128,128]{3,2,1,0:T(8,128)(2,1)S(1)}, u32[]{:S(2)}, u32[]{:S(2)}) collective-permute-start(bf16[2,6,128,128]{3,2,1,0:T(8,128)(2,1)} %get-tuple-element.48), channel_id=1, source_target_pairs={{0,4},{1,5},{2,6},{3,7},{4,0},{5,1},{6,2},{7,3},{8,12},{9,13},{10,... | collective-permute-start | bytes 1179656 | tf_op jit(solution)/shard_map/ppermute | solution.py:342
  42.1 15.1 %collective-permute-start.9 = (bf16[2,6,128,128]{3,2,1,0:T(8,128)(2,1)}, bf16[2,6,128,128]{3,2,1,0:T(8,128)(2,1)}, u32[]{:S(2)}, u32[]{:S(2)}) collective-permute-start(bf16[2,6,128,128]{3,2,1,0:T(8,128)(2,1)} %get-tuple-element.49), channel_id=1, source_target_pairs={{0,2},{1,3},{2,0},{3,1},{4,6},{5,7},{6,4},{7,5},{8,10},{9,11},{10,... | collective-permute-start | bytes 1179656 | tf_op jit(solution)/shard_map/ppermute | solution.py:342
  43.0 5.6 %collective-permute-start.7 = (f32[6,16]{1,0:T(8,128)S(1)}, f32[6,16]{1,0:T(8,128)S(1)}, u32[]{:S(2)}, u32[]{:S(2)}) collective-permute-start(f32[6,16]{1,0:T(8,128)S(1)} %copy-done.13), channel_id=1, source_target_pairs={{0,1},{1,0},{2,3},{3,2},{4,5},{5,4},{6,7},{7,6},{8,9},{9,8},{10,11... | collective-permute-start | bytes 1160 | tf_op jit(solution)/shard_map/ppermute | solution.py:342
  58.4 30.3 %all-to-all-start.1 = ((bf16[4,120,2176]{2,1,0:T(8,128)(2,1)}), bf16[4,120,2176]{2,1,0:T(8,128)(2,1)S(1)}, u32[]{:S(2)}, u32[]{:S(2)}) async-start(bf16[4,120,2176]{2,1,0:T(8,128)(2,1)} %shard_map.125), calls=%async_computation.1 | async-start | bytes 4177920 | tf_op jit(solution)/shard_map/all_to_all | solution.py:534
  62.0 6.4 %collective-permute-start.11 = (bf16[6,128,128]{2,1,0:T(8,128)(2,1)S(1)}, bf16[6,128,128]{2,1,0:T(8,128)(2,1)S(1)}, u32[]{:S(2)}, u32[]{:S(2)}) collective-permute-start(bf16[6,128,128]{2,1,0:T(8,128)(2,1)S(1)} %shard_map.126), channel_id=1, source_target_pairs={{0,8},{1,9},{2,10},{3,11},{4,12},{5,13},{6,14},{7,15},{8,0},{9,1},... | collective-permute-start | bytes 589832 | tf_op jit(solution)/shard_map/ppermute | solution.py:342
  67.8 8.0 %collective-permute-start.10 = (bf16[6,128,128]{2,1,0:T(8,128)(2,1)S(1)}, bf16[6,128,128]{2,1,0:T(8,128)(2,1)S(1)}, u32[]{:S(2)}, u32[]{:S(2)}) collective-permute-start(bf16[6,128,128]{2,1,0:T(8,128)(2,1)S(1)} %get-tuple-element.59), channel_id=1, source_target_pairs={{0,8},{1,9},{2,10},{3,11},{4,12},{5,13},{6,14},{7,15},{8,0},{9,1},... | collective-permute-start | bytes 589832 | tf_op jit(solution)/shard_map/ppermute | solution.py:342
  68.5 10.5 %collective-permute-start.12 = (bf16[6,128,128]{2,1,0:T(8,128)(2,1)S(1)}, bf16[6,128,128]{2,1,0:T(8,128)(2,1)S(1)}, u32[]{:S(2)}, u32[]{:S(2)}) collective-permute-start(bf16[6,128,128]{2,1,0:T(8,128)(2,1)S(1)} %shard_map.128), channel_id=1, source_target_pairs={{0,16},{1,17},{2,18},{3,19},{4,20},{5,21},{6,22},{7,23},{8,24},{9,... | collective-permute-start | bytes 589832 | tf_op jit(solution)/shard_map/ppermute | solution.py:342
  80.1 8.6 %collective-permute-start.16 = (bf16[6,128,128]{2,1,0:T(8,128)(2,1)S(1)}, bf16[6,128,128]{2,1,0:T(8,128)(2,1)S(1)}, u32[]{:S(2)}, u32[]{:S(2)}) collective-permute-start(bf16[6,128,128]{2,1,0:T(8,128)(2,1)S(1)} %get-tuple-element.61.refs_1_), channel_id=1, source_target_pairs={{0,16},{1,17},{2,18},{3,19},{4,20},{5,21},{6,22},{7,23},{8,24},{9,... | collective-permute-start | bytes 589832 | tf_op jit(solution)/shard_map/ppermute | solution.py:342
  80.4 12.3 %collective-permute-start.15 = (bf16[6,128,128]{2,1,0:T(8,128)(2,1)S(1)}, bf16[6,128,128]{2,1,0:T(8,128)(2,1)S(1)}, u32[]{:S(2)}, u32[]{:S(2)}) collective-permute-start(bf16[6,128,128]{2,1,0:T(8,128)(2,1)S(1)} %get-tuple-element.61.refs_1_), channel_id=1, source_target_pairs={{0,8},{1,9},{2,10},{3,11},{4,12},{5,13},{6,14},{7,15},{8,0},{9,1},... | collective-permute-start | bytes 589832 | tf_op jit(solution)/shard_map/ppermute | solution.py:342
  88.7 6.9 %collective-permute-start.17 = (bf16[6,128,128]{2,1,0:T(8,128)(2,1)S(1)}, bf16[6,128,128]{2,1,0:T(8,128)(2,1)S(1)}, u32[]{:S(2)}, u32[]{:S(2)}) collective-permute-start(bf16[6,128,128]{2,1,0:T(8,128)(2,1)S(1)} %collective-permute-done.16.refs_3_), channel_id=1, source_target_pairs={{0,8},{1,9},{2,10},{3,11},{4,12},{5,13},{6,14},{7,15},{8,0},{9,1},... | collective-permute-start | bytes 589832 | tf_op jit(solution)/shard_map/ppermute | solution.py:342
  90.0 8.4 %collective-permute-start.13 = (bf16[2,32,2048]{2,1,0:T(8,128)(2,1)S(1)}, bf16[2,32,2048]{2,1,0:T(8,128)(2,1)S(1)}, u32[]{:S(2)}, u32[]{:S(2)}) collective-permute-start(bf16[2,32,2048]{2,1,0:T(8,128)(2,1)S(1)} %get-tuple-element.63), channel_id=1, source_target_pairs={{0,8},{1,9},{2,10},{3,11},{4,12},{5,13},{6,14},{7,15},{8,0},{9,1},... | collective-permute-start | bytes 786440 | tf_op jit(solution)/shard_map/ppermute | solution.py:342
  92.1 7.7 %collective-permute-start.18 = (bf16[6,128,128]{2,1,0:T(8,128)(2,1)S(1)}, bf16[6,128,128]{2,1,0:T(8,128)(2,1)S(1)}, u32[]{:S(2)}, u32[]{:S(2)}) collective-permute-start(bf16[6,128,128]{2,1,0:T(8,128)(2,1)S(1)} %get-tuple-element.61.refs_1_), channel_id=1, source_target_pairs={{0,1},{1,0},{2,3},{3,2},{4,5},{5,4},{6,7},{7,6},{8,9},{9,8},{10,11... | collective-permute-start | bytes 589832 | tf_op jit(solution)/shard_map/ppermute | solution.py:342
  92.1 7.8 %collective-permute-start.20 = (bf16[6,128,128]{2,1,0:T(8,128)(2,1)S(1)}, bf16[6,128,128]{2,1,0:T(8,128)(2,1)S(1)}, u32[]{:S(2)}, u32[]{:S(2)}) collective-permute-start(bf16[6,128,128]{2,1,0:T(8,128)(2,1)S(1)} %collective-permute-done.16.refs_3_), channel_id=1, source_target_pairs={{0,1},{1,0},{2,3},{3,2},{4,5},{5,4},{6,7},{7,6},{8,9},{9,8},{10,11... | collective-permute-start | bytes 589832 | tf_op jit(solution)/shard_map/ppermute | solution.py:342
  92.7 7.2 %collective-permute-start.19 = (bf16[6,128,128]{2,1,0:T(8,128)(2,1)S(1)}, bf16[6,128,128]{2,1,0:T(8,128)(2,1)S(1)}, u32[]{:S(2)}, u32[]{:S(2)}) collective-permute-start(bf16[6,128,128]{2,1,0:T(8,128)(2,1)S(1)} %collective-permute-done.15.refs_2_), channel_id=1, source_target_pairs={{0,1},{1,0},{2,3},{3,2},{4,5},{5,4},{6,7},{7,6},{8,9},{9,8},{10,11... | collective-permute-start | bytes 589832 | tf_op jit(solution)/shard_map/ppermute | solution.py:342
  98.5 10.3 %collective-permute-start.14 = (bf16[32,2048]{1,0:T(8,128)(2,1)S(1)}, bf16[32,2048]{1,0:T(8,128)(2,1)S(1)}, u32[]{:S(2)}, u32[]{:S(2)}) collective-permute-start(bf16[32,2048]{1,0:T(8,128)(2,1)S(1)} %get-tuple-element.67), channel_id=1, source_target_pairs={{0,16},{1,17},{2,18},{3,19},{4,20},{5,21},{6,22},{7,23},{8,24},{9,... | collective-permute-start | bytes 393224 | tf_op jit(solution)/shard_map/ppermute | solution.py:342
  100.6 4.8 %collective-permute-start.22 = (bf16[24,1536]{1,0:T(8,128)(2,1)S(1)}, bf16[24,1536]{1,0:T(8,128)(2,1)S(1)}, u32[]{:S(2)}, u32[]{:S(2)}) collective-permute-start(bf16[24,1536]{1,0:T(8,128)(2,1)S(1)} %get-tuple-element.70), channel_id=1, source_target_pairs={{0,2},{1,3},{2,0},{3,1},{4,6},{5,7},{6,4},{7,5},{8,10},{9,11},{10,... | collective-permute-start | bytes 221192 | tf_op jit(solution)/shard_map/ppermute | solution.py:342
  103.5 5.3 %collective-permute-start.24 = (bf16[24,1536]{1,0:T(8,128)(2,1)S(1)}, bf16[24,1536]{1,0:T(8,128)(2,1)S(1)}, u32[]{:S(2)}, u32[]{:S(2)}) collective-permute-start(bf16[24,1536]{1,0:T(8,128)(2,1)S(1)} %get-tuple-element.72), channel_id=1, source_target_pairs={{0,6},{1,7},{2,4},{3,5},{4,2},{5,3},{6,0},{7,1},{8,14},{9,15},{10,... | collective-permute-start | bytes 221192 | tf_op jit(solution)/shard_map/ppermute | solution.py:342
  (17 other events, 124.9 us)

commit v5 on v4

--- a/solution.py
+++ b/solution.py
@@ -50,6 +50,12 @@
     return [pl.BlockSpec(memory_space=pltpu.VMEM)] * count
 
 
+def part_of(index, size):
+    if size & (size - 1) == 0:
+        return lax.shift_right_logical(index, jnp.full_like(index, size.bit_length() - 1))
+    return index // size
+
+
 def pack_kernel(
     steps,
     capacity,
@@ -57,11 +63,17 @@
     placement,
     routing,
     gate_weight,
+    hidden_hbm,
+    packed_hbm,
+    gates_trained,
+    rows_trained,
     hidden,
     packed,
-    gates_trained,
-    rows_trained,
+    hidden_sem,
+    packed_sems,
 ):
+    arriving = pltpu.make_async_copy(hidden_hbm, hidden, hidden_sem)
+    arriving.start()
     rows, topk = routing.shape
     entries = rows * topk
     step_entries = entries // steps
@@ -75,8 +87,10 @@
     def ones(mask):
         return jnp.where(mask, 1.0, 0.0).astype(BF16)
 
-    spread = ones(iota((topk, entries), 1) % topk == iota((topk, entries), 0))
-    mine = iota((rows, entries), 1) // topk == iota((rows, entries), 0)
+    entry = iota((1, entries), 1)
+    entry_row = part_of(entry, topk)
+    spread = ones(entry - entry_row * topk == iota((topk, entries), 0))
+    mine = entry_row == iota((rows, entries), 0)
 
     def along(values):
         return jnp.where(mine, jnp.dot(values, spread, preferred_element_type=F32), 0.0)
@@ -85,23 +99,36 @@
     routed = routed.astype(jnp.int32)
     named = ones(iota((experts, entries), 0) == routed)
     same = lax.dot_general(named, named, (((0,), (0,)), ((), ())), preferred_element_type=F32)
-    lane, line = iota((entries, entries), 1), iota((entries, entries), 0)
-    earlier = (lane // step_entries == line // step_entries) & (line // topk < lane // topk)
+    lane, line = iota((1, entries), 1), iota((entries, 1), 0)
+    earlier = (part_of(line, topk) < part_of(lane, topk)) & (
+        part_of(line, step_entries) == part_of(lane, step_entries)
+    )
     place = jnp.sum(jnp.where(earlier, same, 0.0), axis=0, keepdims=True).astype(jnp.int32)
     pair = jnp.zeros_like(routed)
     for expert in range(experts):
         pair = jnp.where(routed == expert, placement[expert], pair)
-    entry = lax.broadcasted_iota(jnp.int32, (1, entries), 1)
-    step_slot = entry // step_entries * capacity + place
-    chip = pair % chips * depth
-    slot = (chip + pair // chips) * pair_slots + step_slot
+    step_slot = part_of(entry, step_entries) * capacity + place
+    floor = part_of(pair, chips)
+    slot = ((pair - floor * chips) * depth + floor) * pair_slots + step_slot
     slots = experts * pair_slots
     slot_line = lax.broadcasted_iota(jnp.int32, (slots, entries), 0)
     onehot = jnp.where(slot_line == slot, 1.0, 0.0).astype(BF16)
     width = hidden.shape[1]
-    packed[:, :width] = jnp.dot(
-        onehot, hidden[...], preferred_element_type=F32
-    ).astype(BF16)
+    arriving.wait()
+    leaving = []
+
+    def leave(at):
+        copy = pltpu.make_async_copy(
+            packed.at[:, at], packed_hbm.at[:, at], packed_sems.at[len(leaving)]
+        )
+        copy.start()
+        leaving.append(copy)
+
+    wide = width // 3
+    for column in range(0, width, wide):
+        at = slice(column, column + wide)
+        packed[:, at] = jnp.dot(onehot, hidden[:, at], preferred_element_type=F32).astype(BF16)
+        leave(pl.ds(column, wide))
     onehot_trained = ones((iota((pair_slots, entries), 0) == step_slot) & (routed == 0))
     rows_trained[...] = jnp.dot(
         onehot_trained, hidden[...], preferred_element_type=F32
@@ -122,6 +149,9 @@
         over_entries,
         preferred_element_type=F32,
     ).astype(BF16)
+    leave(pl.ds(width, packed.shape[1] - width))
+    for copy in leaving:
+        copy.wait()
 
 
 def gradient_kernel(
@@ -268,11 +298,13 @@
         )
 
     gates = of_chips(slice(columns, None)).astype(F32)
-    slot = lax.broadcasted_iota(jnp.int32, gates.shape, 0)
-    plane = slot // (plane_slots // depth) % depth
-    mine = [
-        jnp.where(plane == (floor_ref[0] ^ flip), gates, 0.0).astype(BF16) for flip in range(depth)
-    ]
+    share = plane_slots // depth
+    pieces = [gates[top : top + share] for top in range(0, gates.shape[0], share)]
+    mine = []
+    for flip in range(depth):
+        there = floor_ref[0] ^ flip
+        kept = [jnp.where(there == at % depth, piece, 0.0) for at, piece in enumerate(pieces)]
+        mine.append(jnp.concatenate(kept, axis=0).astype(BF16))
     wide = 512
     for column in range(0, columns, wide):
         at = slice(column, column + wide)
@@ -359,6 +391,7 @@
     row_count = steps * step_rows
     gate_lanes = -(-2 * row_count // 128) * 128
     smem = pl.BlockSpec(memory_space=pltpu.SMEM)
+    hbm = pl.BlockSpec(memory_space=pl.ANY)
 
     packed, gates_trained, rows_trained = pl.pallas_call(
         lambda *refs: pack_kernel(steps, capacity, depth, *refs),
@@ -367,12 +400,18 @@
             jax.ShapeDtypeStruct((2 * steps * step_rows, pair_slots), BF16),
             jax.ShapeDtypeStruct((pair_slots, hidden_width), BF16),
         ),
-        in_specs=[smem] + vmem(3),
-        out_specs=tuple(vmem(3)),
+        in_specs=[smem] + vmem(2) + [hbm],
+        out_specs=(hbm, *vmem(2)),
+        scratch_shapes=[
+            pltpu.VMEM((entries, hidden_width), BF16),
+            pltpu.VMEM((slots, hidden_width + gate_lanes), BF16),
+            pltpu.SemaphoreType.DMA,
+            pltpu.SemaphoreType.DMA((4,)),
+        ],
         compiler_params=PARAMS,
     )(
-        placement,
         *in_hbm(
+            placement,
             routing.reshape(steps * step_rows, topk),
             gate_weight.reshape(steps * step_rows, topk),
             decode_hidden.reshape(entries, hidden_width),
@@ -567,7 +606,7 @@
             held[key | mask] = flip(held[key], mask * plane)
         mask //= 2
     blocks_held = [held[z] for z in range(depth)]
-    blocks_held += [flip(block, 1) for block in blocks_held]
+    blocks_held += [flip(after(block, held[depth // 2]), 1) for block in blocks_held]
     chip_ref = (device % plane // 2).astype(jnp.int32).reshape(1)
     trained = pl.pallas_call(
         lambda device_ref, *refs: trained_kernel(device_ref, plane, depth, column_blocks, *refs),

time: 111 us -> 110 us (level)
    unnamed x28 -> x26, local copies, waits for them, and re-layouts: 4.59 us -> 3.94 us
where the time goes in v5:
time: 110 us; the launch traced here: 109 us
  waiting for transfers between devices  47 us (43%)
  starting transfers between devices  34 us (31%)
  Pallas kernels  23.4 us (21%)
  local copies, waits for them, and re-layouts  4.1 us (4%)
    ppermute x25, waiting for transfers between devices, flip(): return lax.ppermute(array, 'dp', [(i, i ^ mask) for i in range(devices)])  47 us
    ppermute x25, starting transfers between devices, flip(): return lax.ppermute(array, 'dp', [(i, i ^ mask) for i in range(devices)])  22.4 us
    all_to_all x1, starting transfers between devices, local(): lax.all_to_all(after(packed, hidden_other, cotangent_other).reshape(exper...  7.95 us
    pallas_call x1, Pallas kernels, expert_sum(): pl.pallas_call(expert_kernel, out_shape=pltpu.HBM(sent_shape, BF16), grid...  6.47 us
    pallas_call x1, Pallas kernels, local(): pl.pallas_call(gradient_kernel, out_shape=(pltpu.HBM(part.shape, BF16),)...  4.41 us
    unnamed x26, local copies, waits for them, and re-layouts  3.94 us
    all_to_all x1, starting transfers between devices, local(): lax.all_to_all(expert_out, 'dp', split_axis=0, concat_axis=0, tiled=True,...  3.62 us
    pallas_call x1, Pallas kernels, local(): pl.pallas_call(lambda *refs: pack_kernel(steps, capacity, depth, *refs),...  3.36 us
  transfers between devices with their start and end apart: 27, of which 11 were waited for; matrix products, arithmetic and copies ran while one was open for 0% of the time, Pallas kernels for 19%

profile of v5, /device:TPU:0, one launch (start us, length us, event | category | flops | bytes accessed | tf_op | source)
XLA Modules:
  0.0 109.3 jit_solution(14742504917005184694)
XLA Ops:
  1.2 3.4 %shard_map.122 = (bf16[384,1664]{1,0:T(8,128)(2,1)}, bf16[64,24]{1,0:T(8,128)(2,1)S(1)}, bf16[24,1536]{1,0:T(8,128)(2,1)S(1)}) custom-call(s32[16]{0:T(128)} %refs_0_.1, s32[32,8]{1,0:T(8,128)} %bitcast.18, f32[32,8]{1,0:T(8,128)} %bitcast.19, bf16[256,1536]{1,0:T(8,128)(2,1)} %bitcast.16), custom_call_target="tpu_custom_call" | custom-call | tf_op jit(solution)/shard_map/pallas_call | solution.py:396
  5.1 7.9 %all-to-all-start = ((bf16[16,24,1664]{2,1,0:T(8,128)(2,1)}), bf16[16,24,1664]{2,1,0:T(8,128)(2,1)S(1)}, u32[]{:S(2)}, u32[]{:S(2)}) async-start(bf16[16,24,1664]{2,1,0:T(8,128)(2,1)} %bitcast.15), calls=%async_computation | async-start | bytes 2555904 | tf_op jit(solution)/shard_map/all_to_all | solution.py:425
  13.1 4.4 %shard_map.123 = (bf16[2,6,128,128]{3,2,1,0:T(8,128)(2,1)}, bf16[2,6,128,128]{3,2,1,0:T(8,128)(2,1)}, bf16[2,6,128,128]{3,2,1,0:T(8,128)(2,1)}, bf16[2,6,128,128...) custom-call(s32[1]{0:T(128)} %bitcast.8.device_ref, ...), custom_call_target="tpu_custom_call" | custom-call | tf_op jit(solution)/shard_map/pallas_call | solution.py:438
  17.5 1.9 %collective-permute-start.2 = (bf16[2,6,128,128]{3,2,1,0:T(8,128)(2,1)}, bf16[2,6,128,128]{3,2,1,0:T(8,128)(2,1)S(1)}, u32[]{:S(2)}, u32[]{:S(2)}) collective-permute-start(bf16[2,6,128,128]{3,2,1,0:T(8,128)(2,1)} %get-tuple-element.46), channel_id=1, source_target_pairs={{0,2},{1,3},{2,0},{3,1},{4,6},{5,7},{6,4},{7,5},{8,10},{9,11},{10,... | collective-permute-start | bytes 1179656 | tf_op jit(solution)/shard_map/ppermute | solution.py:374
  21.6 16.3 %collective-permute-done.2.arrived_a = bf16[2,6,128,128]{3,2,1,0:T(8,128)(2,1)S(1)} collective-permute-done((bf16[2,6,128,128]{3,2,1,0:T(8,128)(2,1)}, bf16[2,6,128,128]{3,2,1,0:T(8,128)(2,1)S(1)}, u32[]{:S(2)}, u32[]{:S(2)}) %collective-permute-start.2) | collective-permute-done | bytes 393248 | tf_op jit(solution)/shard_map/ppermute | solution.py:374
  37.9 2.1 %shard_map.124 = (bf16[2,6,128,128]{3,2,1,0:T(8,128)(2,1)}, bf16[2,6,128,128]{3,2,1,0:T(8,128)(2,1)}) custom-call(bf16[2,6,128,128]{3,2,1,0:T(8,128)(2,1)S(1)} %collective-permute-done.2.arrived_a, bf16[2,6,128,128]{3,2,1,0:T(8,128)(2,1)} %get-tuple-element.49.held_a, bf16[2,6,128,128]{3,2,1,0:T(8,128)(2,1)S(1)} %collective-permute-done.4.arrived_b, ...), custom_call_target="tpu_custom_call" | custom-call | tf_op jit(solution)/shard_map/pallas_call | solution.py:458
  40.0 1.5 %collective-permute-start.8 = (bf16[2,6,128,128]{3,2,1,0:T(8,128)(2,1)}, bf16[2,6,128,128]{3,2,1,0:T(8,128)(2,1)S(1)}, u32[]{:S(2)}, u32[]{:S(2)}) collective-permute-start(bf16[2,6,128,128]{3,2,1,0:T(8,128)(2,1)} %get-tuple-element.52), channel_id=1, source_target_pairs={{0,4},{1,5},{2,6},{3,7},{4,0},{5,1},{6,2},{7,3},{8,12},{9,13},{10,... | collective-permute-start | bytes 1179656 | tf_op jit(solution)/shard_map/ppermute | solution.py:374
  42.4 5.6 %collective-permute-done.5.rest_1_ = bf16[2,6,128,128]{3,2,1,0:T(8,128)(2,1)S(1)} collective-permute-done((bf16[2,6,128,128]{3,2,1,0:T(8,128)(2,1)}, bf16[2,6,128,128]{3,2,1,0:T(8,128)(2,1)S(1)}, u32[]{:S(2)}, u32[]{:S(2)}) %collective-permute-start.5) | collective-permute-done | bytes 393248 | tf_op jit(solution)/shard_map/ppermute | solution.py:374
  48.2 1.9 %copy-done = bf16[768,2048]{1,0:T(8,128)(2,1)S(1)} copy-done((bf16[768,2048]{1,0:T(8,128)(2,1)S(1)}, bf16[768,2048]{1,0:T(8,128)(2,1)}, u32[]{:S(2)}) %copy-start) | copy-done | bytes 3145752
  50.1 6.5 %shard_map.125 = bf16[4,120,2176]{2,1,0:T(8,128)(2,1)} custom-call(s32[1]{0:T(128)} %bitcast.5.core_ref, bf16[384,1664]{1,0:T(8,128)(2,1)S(1)} %bitcast.12, bf16[24,1536]{1,0:T(8,128)(2,1)S(1)} %get-tuple-element.57.rows_trained, bf16[768,2048]{1,0:T(8,128)(2,1)S(1)} %copy-done, bf16[768,2048]{1,0:T(8,128)(2,1)} %collective-permute-done.3.weights_other, ...), custom_call_target="tpu_custom_call" | custom-call | tf_op jit(solution)/shard_map/pallas_call | solution.py:475
  57.8 3.6 %all-to-all-start.1 = ((bf16[4,120,2176]{2,1,0:T(8,128)(2,1)}), bf16[4,120,2176]{2,1,0:T(8,128)(2,1)S(1)}, u32[]{:S(2)}, u32[]{:S(2)}) async-start(bf16[4,120,2176]{2,1,0:T(8,128)(2,1)} %shard_map.125), calls=%async_computation.1 | async-start | bytes 4177920 | tf_op jit(solution)/shard_map/all_to_all | solution.py:573
  61.4 2.1 %collective-permute-start.11 = (bf16[6,128,128]{2,1,0:T(8,128)(2,1)S(1)}, bf16[6,128,128]{2,1,0:T(8,128)(2,1)S(1)}, u32[]{:S(2)}, u32[]{:S(2)}) collective-permute-start(bf16[6,128,128]{2,1,0:T(8,128)(2,1)S(1)} %shard_map.126), channel_id=1, source_target_pairs={{0,8},{1,9},{2,10},{3,11},{4,12},{5,13},{6,14},{7,15},{8,0},{9,1},... | collective-permute-start | bytes 589832 | tf_op jit(solution)/shard_map/ppermute | solution.py:374
  65.5 1.6 %shard_map.127 = (bf16[6,128,128]{2,1,0:T(8,128)(2,1)S(1)}, f32[6,128,128]{2,1,0:T(8,128)S(1)}, f32[6,128,128]{2,1,0:T(8,128)S(1)}) custom-call(s32[1]{0:T(128)} %bitcast.4.floor_ref.refs_0_, bf16[2,6,128,128]{3,2,1,0:T(8,128)(2,1)S(1)} %copy-done.1, bf16[2,6,128,128]{3,2,1,0:T(8,128)(2,1)S(1)} %collective-permute-done.5.rest_1_, ...), custom_call_target="tpu_custom_call" | custom-call | tf_op jit(solution)/shard_map/pallas_call | solution.py:522
  67.9 2.4 %collective-permute-start.12 = (bf16[6,128,128]{2,1,0:T(8,128)(2,1)S(1)}, bf16[6,128,128]{2,1,0:T(8,128)(2,1)S(1)}, u32[]{:S(2)}, u32[]{:S(2)}) collective-permute-start(bf16[6,128,128]{2,1,0:T(8,128)(2,1)S(1)} %shard_map.128), channel_id=1, source_target_pairs={{0,16},{1,17},{2,18},{3,19},{4,20},{5,21},{6,22},{7,23},{8,24},{9,... | collective-permute-start | bytes 589832 | tf_op jit(solution)/shard_map/ppermute | solution.py:374
  70.3 4.9 %collective-permute-done.10.rest_1_ = bf16[6,128,128]{2,1,0:T(8,128)(2,1)S(1)} collective-permute-done((bf16[6,128,128]{2,1,0:T(8,128)(2,1)S(1)}, bf16[6,128,128]{2,1,0:T(8,128)(2,1)S(1)}, u32[]{:S(2)}, u32[]{:S(2)}) %collective-permute-start.10) | collective-permute-done | bytes 196640 | tf_op jit(solution)/shard_map/ppermute | solution.py:374
  75.2 3.2 %collective-permute-done.12.rest_2_ = bf16[6,128,128]{2,1,0:T(8,128)(2,1)S(1)} collective-permute-done((bf16[6,128,128]{2,1,0:T(8,128)(2,1)S(1)}, bf16[6,128,128]{2,1,0:T(8,128)(2,1)S(1)}, u32[]{:S(2)}, u32[]{:S(2)}) %collective-permute-start.12) | collective-permute-done | bytes 196640 | tf_op jit(solution)/shard_map/ppermute | solution.py:374
  79.8 2.5 %collective-permute-start.15 = (bf16[6,128,128]{2,1,0:T(8,128)(2,1)S(1)}, bf16[6,128,128]{2,1,0:T(8,128)(2,1)S(1)}, u32[]{:S(2)}, u32[]{:S(2)}) collective-permute-start(bf16[6,128,128]{2,1,0:T(8,128)(2,1)S(1)} %get-tuple-element.73.refs_1_), channel_id=1, source_target_pairs={{0,8},{1,9},{2,10},{3,11},{4,12},{5,13},{6,14},{7,15},{8,0},{9,1},... | collective-permute-start | bytes 589832 | tf_op jit(solution)/shard_map/ppermute | solution.py:374
  82.2 5.8 %collective-permute-done.16.refs_3_ = bf16[6,128,128]{2,1,0:T(8,128)(2,1)S(1)} collective-permute-done((bf16[6,128,128]{2,1,0:T(8,128)(2,1)S(1)}, bf16[6,128,128]{2,1,0:T(8,128)(2,1)S(1)}, u32[]{:S(2)}, u32[]{:S(2)}) %collective-permute-start.16) | collective-permute-done | bytes 196640 | tf_op jit(solution)/shard_map/ppermute | solution.py:374
  89.4 2.1 %collective-permute-start.13 = (bf16[2,32,2048]{2,1,0:T(8,128)(2,1)S(1)}, bf16[2,32,2048]{2,1,0:T(8,128)(2,1)S(1)}, u32[]{:S(2)}, u32[]{:S(2)}) collective-permute-start(bf16[2,32,2048]{2,1,0:T(8,128)(2,1)S(1)} %get-tuple-element.67), channel_id=1, source_target_pairs={{0,8},{1,9},{2,10},{3,11},{4,12},{5,13},{6,14},{7,15},{8,0},{9,1},... | collective-permute-start | bytes 786440 | tf_op jit(solution)/shard_map/ppermute | solution.py:374
  92.0 3.0 %collective-permute-done.17.refs_4_ = bf16[6,128,128]{2,1,0:T(8,128)(2,1)S(1)} collective-permute-done((bf16[6,128,128]{2,1,0:T(8,128)(2,1)S(1)}, bf16[6,128,128]{2,1,0:T(8,128)(2,1)S(1)}, u32[]{:S(2)}, u32[]{:S(2)}) %collective-permute-start.17) | collective-permute-done | bytes 196640 | tf_op jit(solution)/shard_map/ppermute | solution.py:374
  95.0 2.8 %collective-permute-done.13.arrived = bf16[2,32,2048]{2,1,0:T(8,128)(2,1)S(1)} collective-permute-done((bf16[2,32,2048]{2,1,0:T(8,128)(2,1)S(1)}, bf16[2,32,2048]{2,1,0:T(8,128)(2,1)S(1)}, u32[]{:S(2)}, u32[]{:S(2)}) %collective-permute-start.13) | collective-permute-done | bytes 262176 | tf_op jit(solution)/shard_map/ppermute | solution.py:374
  99.9 2.2 %collective-permute-start.22 = (bf16[24,1536]{1,0:T(8,128)(2,1)S(1)}, bf16[24,1536]{1,0:T(8,128)(2,1)S(1)}, u32[]{:S(2)}, u32[]{:S(2)}) collective-permute-start(bf16[24,1536]{1,0:T(8,128)(2,1)S(1)} %get-tuple-element.78), channel_id=1, source_target_pairs={{0,2},{1,3},{2,0},{3,1},{4,6},{5,7},{6,4},{7,5},{8,10},{9,11},{10,... | collective-permute-start | bytes 221192 | tf_op jit(solution)/shard_map/ppermute | solution.py:374
  104.8 1.6 %collective-permute-done.23.refs_5_ = bf16[24,1536]{1,0:T(8,128)(2,1)S(1)} collective-permute-done((bf16[24,1536]{1,0:T(8,128)(2,1)S(1)}, bf16[24,1536]{1,0:T(8,128)(2,1)S(1)}, u32[]{:S(2)}, u32[]{:S(2)}) %collective-permute-start.23) | collective-permute-done | bytes 73760 | tf_op jit(solution)/shard_map/ppermute | solution.py:374
  106.4 1.8 %collective-permute-done.24.refs_6_ = bf16[24,1536]{1,0:T(8,128)(2,1)S(1)} collective-permute-done((bf16[24,1536]{1,0:T(8,128)(2,1)S(1)}, bf16[24,1536]{1,0:T(8,128)(2,1)S(1)}, u32[]{:S(2)}, u32[]{:S(2)}) %collective-permute-start.24) | collective-permute-done | bytes 73760 | tf_op jit(solution)/shard_map/ppermute | solution.py:374
  (71 shorter events, 17.3 us)
Async XLA Ops:
  4.6 16.9 %collective-permute-start.3 = (bf16[768,2048]{1,0:T(8,128)(2,1)}, bf16[768,2048]{1,0:T(8,128)(2,1)}, u32[]{:S(2)}, u32[]{:S(2)}) collective-permute-start(bf16[768,2048]{1,0:T(8,128)(2,1)} %weights.1), channel_id=1, source_target_pairs={{0,1},{1,0},{2,3},{3,2},{4,5},{5,4},{6,7},{7,6},{8,9},{9,8},{10,11... | collective-permute-start | bytes 9437192 | tf_op jit(solution)/shard_map/ppermute | solution.py:374
  5.1 42.9 %all-to-all-start = ((bf16[16,24,1664]{2,1,0:T(8,128)(2,1)}), bf16[16,24,1664]{2,1,0:T(8,128)(2,1)S(1)}, u32[]{:S(2)}, u32[]{:S(2)}) async-start(bf16[16,24,1664]{2,1,0:T(8,128)(2,1)} %bitcast.15), calls=%async_computation | async-start | bytes 2555904 | tf_op jit(solution)/shard_map/all_to_all | solution.py:425
  17.5 20.4 %collective-permute-start.2 = (bf16[2,6,128,128]{3,2,1,0:T(8,128)(2,1)}, bf16[2,6,128,128]{3,2,1,0:T(8,128)(2,1)S(1)}, u32[]{:S(2)}, u32[]{:S(2)}) collective-permute-start(bf16[2,6,128,128]{3,2,1,0:T(8,128)(2,1)} %get-tuple-element.46), channel_id=1, source_target_pairs={{0,2},{1,3},{2,0},{3,1},{4,6},{5,7},{6,4},{7,5},{8,10},{9,11},{10,... | collective-permute-start | bytes 1179656 | tf_op jit(solution)/shard_map/ppermute | solution.py:374
  19.5 18.5 %collective-permute-start.4 = (bf16[2,6,128,128]{3,2,1,0:T(8,128)(2,1)}, bf16[2,6,128,128]{3,2,1,0:T(8,128)(2,1)S(1)}, u32[]{:S(2)}, u32[]{:S(2)}) collective-permute-start(bf16[2,6,128,128]{3,2,1,0:T(8,128)(2,1)} %get-tuple-element.50), channel_id=1, source_target_pairs={{0,4},{1,5},{2,6},{3,7},{4,0},{5,1},{6,2},{7,3},{8,12},{9,13},{10,... | collective-permute-start | bytes 1179656 | tf_op jit(solution)/shard_map/ppermute | solution.py:374
  20.9 27.1 %collective-permute-start.5 = (bf16[2,6,128,128]{3,2,1,0:T(8,128)(2,1)}, bf16[2,6,128,128]{3,2,1,0:T(8,128)(2,1)S(1)}, u32[]{:S(2)}, u32[]{:S(2)}) collective-permute-start(bf16[2,6,128,128]{3,2,1,0:T(8,128)(2,1)} %get-tuple-element.54), channel_id=1, source_target_pairs={{0,2},{1,3},{2,0},{3,1},{4,6},{5,7},{6,4},{7,5},{8,10},{9,11},{10,... | collective-permute-start | bytes 1179656 | tf_op jit(solution)/shard_map/ppermute | solution.py:374
  21.5 26.6 %collective-permute-start.6 = (bf16[2,6,128,128]{3,2,1,0:T(8,128)(2,1)}, bf16[2,6,128,128]{3,2,1,0:T(8,128)(2,1)S(1)}, u32[]{:S(2)}, u32[]{:S(2)}) collective-permute-start(bf16[2,6,128,128]{3,2,1,0:T(8,128)(2,1)} %get-tuple-element.55), channel_id=1, source_target_pairs={{0,4},{1,5},{2,6},{3,7},{4,0},{5,1},{6,2},{7,3},{8,12},{9,13},{10,... | collective-permute-start | bytes 1179656 | tf_op jit(solution)/shard_map/ppermute | solution.py:374
  40.0 16.6 %collective-permute-start.8 = (bf16[2,6,128,128]{3,2,1,0:T(8,128)(2,1)}, bf16[2,6,128,128]{3,2,1,0:T(8,128)(2,1)S(1)}, u32[]{:S(2)}, u32[]{:S(2)}) collective-permute-start(bf16[2,6,128,128]{3,2,1,0:T(8,128)(2,1)} %get-tuple-element.52), channel_id=1, source_target_pairs={{0,4},{1,5},{2,6},{3,7},{4,0},{5,1},{6,2},{7,3},{8,12},{9,13},{10,... | collective-permute-start | bytes 1179656 | tf_op jit(solution)/shard_map/ppermute | solution.py:374
  41.5 15.1 %collective-permute-start.9 = (bf16[2,6,128,128]{3,2,1,0:T(8,128)(2,1)}, bf16[2,6,128,128]{3,2,1,0:T(8,128)(2,1)}, u32[]{:S(2)}, u32[]{:S(2)}) collective-permute-start(bf16[2,6,128,128]{3,2,1,0:T(8,128)(2,1)} %get-tuple-element.53), channel_id=1, source_target_pairs={{0,2},{1,3},{2,0},{3,1},{4,6},{5,7},{6,4},{7,5},{8,10},{9,11},{10,... | collective-permute-start | bytes 1179656 | tf_op jit(solution)/shard_map/ppermute | solution.py:374
  42.4 5.6 %collective-permute-start.7 = (f32[6,16]{1,0:T(8,128)S(1)}, f32[6,16]{1,0:T(8,128)S(1)}, u32[]{:S(2)}, u32[]{:S(2)}) collective-permute-start(f32[6,16]{1,0:T(8,128)S(1)} %copy-done.12), channel_id=1, source_target_pairs={{0,1},{1,0},{2,3},{3,2},{4,5},{5,4},{6,7},{7,6},{8,9},{9,8},{10,11... | collective-permute-start | bytes 1160 | tf_op jit(solution)/shard_map/ppermute | solution.py:374
  57.8 30.3 %all-to-all-start.1 = ((bf16[4,120,2176]{2,1,0:T(8,128)(2,1)}), bf16[4,120,2176]{2,1,0:T(8,128)(2,1)S(1)}, u32[]{:S(2)}, u32[]{:S(2)}) async-start(bf16[4,120,2176]{2,1,0:T(8,128)(2,1)} %shard_map.125), calls=%async_computation.1 | async-start | bytes 4177920 | tf_op jit(solution)/shard_map/all_to_all | solution.py:573
  61.4 6.5 %collective-permute-start.11 = (bf16[6,128,128]{2,1,0:T(8,128)(2,1)S(1)}, bf16[6,128,128]{2,1,0:T(8,128)(2,1)S(1)}, u32[]{:S(2)}, u32[]{:S(2)}) collective-permute-start(bf16[6,128,128]{2,1,0:T(8,128)(2,1)S(1)} %shard_map.126), channel_id=1, source_target_pairs={{0,8},{1,9},{2,10},{3,11},{4,12},{5,13},{6,14},{7,15},{8,0},{9,1},... | collective-permute-start | bytes 589832 | tf_op jit(solution)/shard_map/ppermute | solution.py:374
  67.2 8.0 %collective-permute-start.10 = (bf16[6,128,128]{2,1,0:T(8,128)(2,1)S(1)}, bf16[6,128,128]{2,1,0:T(8,128)(2,1)S(1)}, u32[]{:S(2)}, u32[]{:S(2)}) collective-permute-start(bf16[6,128,128]{2,1,0:T(8,128)(2,1)S(1)} %get-tuple-element.63), channel_id=1, source_target_pairs={{0,8},{1,9},{2,10},{3,11},{4,12},{5,13},{6,14},{7,15},{8,0},{9,1},... | collective-permute-start | bytes 589832 | tf_op jit(solution)/shard_map/ppermute | solution.py:374
  67.9 10.5 %collective-permute-start.12 = (bf16[6,128,128]{2,1,0:T(8,128)(2,1)S(1)}, bf16[6,128,128]{2,1,0:T(8,128)(2,1)S(1)}, u32[]{:S(2)}, u32[]{:S(2)}) collective-permute-start(bf16[6,128,128]{2,1,0:T(8,128)(2,1)S(1)} %shard_map.128), channel_id=1, source_target_pairs={{0,16},{1,17},{2,18},{3,19},{4,20},{5,21},{6,22},{7,23},{8,24},{9,... | collective-permute-start | bytes 589832 | tf_op jit(solution)/shard_map/ppermute | solution.py:374
  79.5 8.6 %collective-permute-start.16 = (bf16[6,128,128]{2,1,0:T(8,128)(2,1)S(1)}, bf16[6,128,128]{2,1,0:T(8,128)(2,1)S(1)}, u32[]{:S(2)}, u32[]{:S(2)}) collective-permute-start(bf16[6,128,128]{2,1,0:T(8,128)(2,1)S(1)} %get-tuple-element.73.refs_1_), channel_id=1, source_target_pairs={{0,16},{1,17},{2,18},{3,19},{4,20},{5,21},{6,22},{7,23},{8,24},{9,... | collective-permute-start | bytes 589832 | tf_op jit(solution)/shard_map/ppermute | solution.py:374
  79.8 11.7 %collective-permute-start.15 = (bf16[6,128,128]{2,1,0:T(8,128)(2,1)S(1)}, bf16[6,128,128]{2,1,0:T(8,128)(2,1)S(1)}, u32[]{:S(2)}, u32[]{:S(2)}) collective-permute-start(bf16[6,128,128]{2,1,0:T(8,128)(2,1)S(1)} %get-tuple-element.73.refs_1_), channel_id=1, source_target_pairs={{0,8},{1,9},{2,10},{3,11},{4,12},{5,13},{6,14},{7,15},{8,0},{9,1},... | collective-permute-start | bytes 589832 | tf_op jit(solution)/shard_map/ppermute | solution.py:374
  88.1 6.9 %collective-permute-start.17 = (bf16[6,128,128]{2,1,0:T(8,128)(2,1)S(1)}, bf16[6,128,128]{2,1,0:T(8,128)(2,1)S(1)}, u32[]{:S(2)}, u32[]{:S(2)}) collective-permute-start(bf16[6,128,128]{2,1,0:T(8,128)(2,1)S(1)} %collective-permute-done.16.refs_3_), channel_id=1, source_target_pairs={{0,8},{1,9},{2,10},{3,11},{4,12},{5,13},{6,14},{7,15},{8,0},{9,1},... | collective-permute-start | bytes 589832 | tf_op jit(solution)/shard_map/ppermute | solution.py:374
  89.4 8.5 %collective-permute-start.13 = (bf16[2,32,2048]{2,1,0:T(8,128)(2,1)S(1)}, bf16[2,32,2048]{2,1,0:T(8,128)(2,1)S(1)}, u32[]{:S(2)}, u32[]{:S(2)}) collective-permute-start(bf16[2,32,2048]{2,1,0:T(8,128)(2,1)S(1)} %get-tuple-element.67), channel_id=1, source_target_pairs={{0,8},{1,9},{2,10},{3,11},{4,12},{5,13},{6,14},{7,15},{8,0},{9,1},... | collective-permute-start | bytes 786440 | tf_op jit(solution)/shard_map/ppermute | solution.py:374
  91.5 7.7 %collective-permute-start.18 = (bf16[6,128,128]{2,1,0:T(8,128)(2,1)S(1)}, bf16[6,128,128]{2,1,0:T(8,128)(2,1)S(1)}, u32[]{:S(2)}, u32[]{:S(2)}) collective-permute-start(bf16[6,128,128]{2,1,0:T(8,128)(2,1)S(1)} %get-tuple-element.73.refs_1_), channel_id=1, source_target_pairs={{0,1},{1,0},{2,3},{3,2},{4,5},{5,4},{6,7},{7,6},{8,9},{9,8},{10,11... | collective-permute-start | bytes 589832 | tf_op jit(solution)/shard_map/ppermute | solution.py:374
  91.5 7.7 %collective-permute-start.19 = (bf16[6,128,128]{2,1,0:T(8,128)(2,1)S(1)}, bf16[6,128,128]{2,1,0:T(8,128)(2,1)S(1)}, u32[]{:S(2)}, u32[]{:S(2)}) collective-permute-start(bf16[6,128,128]{2,1,0:T(8,128)(2,1)S(1)} %collective-permute-done.15.refs_2_), channel_id=1, source_target_pairs={{0,1},{1,0},{2,3},{3,2},{4,5},{5,4},{6,7},{7,6},{8,9},{9,8},{10,11... | collective-permute-start | bytes 589832 | tf_op jit(solution)/shard_map/ppermute | solution.py:374
  92.0 7.2 %collective-permute-start.20 = (bf16[6,128,128]{2,1,0:T(8,128)(2,1)S(1)}, bf16[6,128,128]{2,1,0:T(8,128)(2,1)S(1)}, u32[]{:S(2)}, u32[]{:S(2)}) collective-permute-start(bf16[6,128,128]{2,1,0:T(8,128)(2,1)S(1)} %collective-permute-done.16.refs_3_), channel_id=1, source_target_pairs={{0,1},{1,0},{2,3},{3,2},{4,5},{5,4},{6,7},{7,6},{8,9},{9,8},{10,11... | collective-permute-start | bytes 589832 | tf_op jit(solution)/shard_map/ppermute | solution.py:374
  97.9 10.3 %collective-permute-start.14 = (bf16[32,2048]{1,0:T(8,128)(2,1)S(1)}, bf16[32,2048]{1,0:T(8,128)(2,1)S(1)}, u32[]{:S(2)}, u32[]{:S(2)}) collective-permute-start(bf16[32,2048]{1,0:T(8,128)(2,1)S(1)} %get-tuple-element.71), channel_id=1, source_target_pairs={{0,16},{1,17},{2,18},{3,19},{4,20},{5,21},{6,22},{7,23},{8,24},{9,... | collective-permute-start | bytes 393224 | tf_op jit(solution)/shard_map/ppermute | solution.py:374
  99.9 4.9 %collective-permute-start.22 = (bf16[24,1536]{1,0:T(8,128)(2,1)S(1)}, bf16[24,1536]{1,0:T(8,128)(2,1)S(1)}, u32[]{:S(2)}, u32[]{:S(2)}) collective-permute-start(bf16[24,1536]{1,0:T(8,128)(2,1)S(1)} %get-tuple-element.78), channel_id=1, source_target_pairs={{0,2},{1,3},{2,0},{3,1},{4,6},{5,7},{6,4},{7,5},{8,10},{9,11},{10,... | collective-permute-start | bytes 221192 | tf_op jit(solution)/shard_map/ppermute | solution.py:374
  102.1 4.4 %collective-permute-start.23 = (bf16[24,1536]{1,0:T(8,128)(2,1)S(1)}, bf16[24,1536]{1,0:T(8,128)(2,1)S(1)}, u32[]{:S(2)}, u32[]{:S(2)}) collective-permute-start(bf16[24,1536]{1,0:T(8,128)(2,1)S(1)} %get-tuple-element.79), channel_id=1, source_target_pairs={{0,4},{1,5},{2,6},{3,7},{4,0},{5,1},{6,2},{7,3},{8,12},{9,13},{10,... | collective-permute-start | bytes 221192 | tf_op jit(solution)/shard_map/ppermute | solution.py:374
  102.9 5.3 %collective-permute-start.24 = (bf16[24,1536]{1,0:T(8,128)(2,1)S(1)}, bf16[24,1536]{1,0:T(8,128)(2,1)S(1)}, u32[]{:S(2)}, u32[]{:S(2)}) collective-permute-start(bf16[24,1536]{1,0:T(8,128)(2,1)S(1)} %get-tuple-element.80), channel_id=1, source_target_pairs={{0,6},{1,7},{2,4},{3,5},{4,2},{5,3},{6,0},{7,1},{8,14},{9,15},{10,... | collective-permute-start | bytes 221192 | tf_op jit(solution)/shard_map/ppermute | solution.py:374
  (16 other events, 123.1 us)

commit v6 on v5

--- a/solution.py
+++ b/solution.py
@@ -587,17 +587,6 @@
         compiler_params=PARAMS,
     )(floor_ref, after(returned, fresh))
     sent_rows = flip(sent_rows, plane)
-    across_rows, mixed_near = pl.pallas_call(
-        mix_sum_kernel,
-        out_shape=(
-            jax.ShapeDtypeStruct(row_shape, BF16),
-            jax.ShapeDtypeStruct(row_shape, F32),
-        ),
-        in_specs=vmem(3),
-        out_specs=tuple(vmem(2)),
-        compiler_params=PARAMS,
-    )(sent_rows, across_rows, mixed)
-    across_rows = flip(across_rows, 2 * plane)
 
     held = {0: fresh}
     mask = depth // 2
@@ -615,6 +604,17 @@
         out_specs=tuple(vmem(chips)),
         compiler_params=PARAMS,
     )(device_ref, after(rows_trained, mixed), *blocks_held)
+    across_rows, mixed_near = pl.pallas_call(
+        mix_sum_kernel,
+        out_shape=(
+            jax.ShapeDtypeStruct(row_shape, BF16),
+            jax.ShapeDtypeStruct(row_shape, F32),
+        ),
+        in_specs=vmem(3),
+        out_specs=tuple(vmem(2)),
+        compiler_params=PARAMS,
+    )(after(sent_rows, trained[0]), across_rows, mixed)
+    across_rows = flip(across_rows, 2 * plane)
     trained = [trained[0]] + [flip(trained[turn], 2 * turn) for turn in range(1, chips)]
     decoded = pl.pallas_call(
         lambda chip_ref, *refs: combine_kernel(chip_ref, chips, side, *refs),

time: 110 us -> 109 us (level)
  transfers between devices with their start and end apart: 27 -> 27, of which waited for: 11 -> 12; matrix products, arithmetic and copies ran while one was open for 0% -> 0% of each run, Pallas kernels for 19% -> 19%
where the time goes in v6:
time: 109 us
  waiting for transfers between devices  46.4 us (43%)
  starting transfers between devices  33.9 us (31%)
  Pallas kernels  23.3 us (21%)
  local copies, waits for them, and re-layouts  4.1 us (4%)
    ppermute x25, waiting for transfers between devices, flip(): return lax.ppermute(array, 'dp', [(i, i ^ mask) for i in range(devices)])  46.4 us
    ppermute x25, starting transfers between devices, flip(): return lax.ppermute(array, 'dp', [(i, i ^ mask) for i in range(devices)])  22.3 us
    all_to_all x1, starting transfers between devices, local(): lax.all_to_all(after(packed, hidden_other, cotangent_other).reshape(exper...  7.95 us
    pallas_call x1, Pallas kernels, expert_sum(): pl.pallas_call(expert_kernel, out_shape=pltpu.HBM(sent_shape, BF16), grid...  6.47 us
    pallas_call x1, Pallas kernels, local(): pl.pallas_call(gradient_kernel, out_shape=(pltpu.HBM(part.shape, BF16),)...  4.41 us
    unnamed x26, local copies, waits for them, and re-layouts  3.94 us
    all_to_all x1, starting transfers between devices, local(): lax.all_to_all(expert_out, 'dp', split_axis=0, concat_axis=0, tiled=True,...  3.62 us
    pallas_call x1, Pallas kernels, local(): pl.pallas_call(lambda *refs: pack_kernel(steps, capacity, depth, *refs),...  3.36 us
  transfers between devices with their start and end apart: 27, of which 12 were waited for; matrix products, arithmetic and copies ran while one was open for 0% of the time, Pallas kernels for 19%

profile of v6, /device:TPU:0, one launch (start us, length us, event | category | flops | bytes accessed | tf_op | source)
XLA Modules:
  0.0 108.6 jit_solution(18066543279676085081)
XLA Ops:
  1.2 3.4 %shard_map.122 = (bf16[384,1664]{1,0:T(8,128)(2,1)}, bf16[64,24]{1,0:T(8,128)(2,1)S(1)}, bf16[24,1536]{1,0:T(8,128)(2,1)S(1)}) custom-call(s32[16]{0:T(128)} %refs_0_.1, s32[32,8]{1,0:T(8,128)} %bitcast.18, f32[32,8]{1,0:T(8,128)} %bitcast.19, bf16[256,1536]{1,0:T(8,128)(2,1)} %bitcast.16), custom_call_target="tpu_custom_call" | custom-call | tf_op jit(solution)/shard_map/pallas_call | solution.py:396
  5.1 7.9 %all-to-all-start = ((bf16[16,24,1664]{2,1,0:T(8,128)(2,1)}), bf16[16,24,1664]{2,1,0:T(8,128)(2,1)S(1)}, u32[]{:S(2)}, u32[]{:S(2)}) async-start(bf16[16,24,1664]{2,1,0:T(8,128)(2,1)} %bitcast.15), calls=%async_computation | async-start | bytes 2555904 | tf_op jit(solution)/shard_map/all_to_all | solution.py:425
  13.1 4.4 %shard_map.123 = (bf16[2,6,128,128]{3,2,1,0:T(8,128)(2,1)}, bf16[2,6,128,128]{3,2,1,0:T(8,128)(2,1)}, bf16[2,6,128,128]{3,2,1,0:T(8,128)(2,1)}, bf16[2,6,128,128...) custom-call(s32[1]{0:T(128)} %bitcast.8.device_ref, ...), custom_call_target="tpu_custom_call" | custom-call | tf_op jit(solution)/shard_map/pallas_call | solution.py:438
  17.5 1.9 %collective-permute-start.2 = (bf16[2,6,128,128]{3,2,1,0:T(8,128)(2,1)}, bf16[2,6,128,128]{3,2,1,0:T(8,128)(2,1)S(1)}, u32[]{:S(2)}, u32[]{:S(2)}) collective-permute-start(bf16[2,6,128,128]{3,2,1,0:T(8,128)(2,1)} %get-tuple-element.47), channel_id=1, source_target_pairs={{0,2},{1,3},{2,0},{3,1},{4,6},{5,7},{6,4},{7,5},{8,10},{9,11},{10,... | collective-permute-start | bytes 1179656 | tf_op jit(solution)/shard_map/ppermute | solution.py:374
  19.5 1.5 %collective-permute-start.4 = (bf16[2,6,128,128]{3,2,1,0:T(8,128)(2,1)}, bf16[2,6,128,128]{3,2,1,0:T(8,128)(2,1)S(1)}, u32[]{:S(2)}, u32[]{:S(2)}) collective-permute-start(bf16[2,6,128,128]{3,2,1,0:T(8,128)(2,1)} %get-tuple-element.51), channel_id=1, source_target_pairs={{0,4},{1,5},{2,6},{3,7},{4,0},{5,1},{6,2},{7,3},{8,12},{9,13},{10,... | collective-permute-start | bytes 1179656 | tf_op jit(solution)/shard_map/ppermute | solution.py:374
  21.6 16.3 %collective-permute-done.2.arrived_a = bf16[2,6,128,128]{3,2,1,0:T(8,128)(2,1)S(1)} collective-permute-done((bf16[2,6,128,128]{3,2,1,0:T(8,128)(2,1)}, bf16[2,6,128,128]{3,2,1,0:T(8,128)(2,1)S(1)}, u32[]{:S(2)}, u32[]{:S(2)}) %collective-permute-start.2) | collective-permute-done | bytes 393248 | tf_op jit(solution)/shard_map/ppermute | solution.py:374
  37.9 2.1 %shard_map.124 = (bf16[2,6,128,128]{3,2,1,0:T(8,128)(2,1)}, bf16[2,6,128,128]{3,2,1,0:T(8,128)(2,1)}) custom-call(bf16[2,6,128,128]{3,2,1,0:T(8,128)(2,1)S(1)} %collective-permute-done.2.arrived_a, bf16[2,6,128,128]{3,2,1,0:T(8,128)(2,1)} %get-tuple-element.50.held_a, bf16[2,6,128,128]{3,2,1,0:T(8,128)(2,1)S(1)} %collective-permute-done.4.arrived_b, ...), custom_call_target="tpu_custom_call" | custom-call | tf_op jit(solution)/shard_map/pallas_call | solution.py:458
  40.0 1.5 %collective-permute-start.8 = (bf16[2,6,128,128]{3,2,1,0:T(8,128)(2,1)}, bf16[2,6,128,128]{3,2,1,0:T(8,128)(2,1)S(1)}, u32[]{:S(2)}, u32[]{:S(2)}) collective-permute-start(bf16[2,6,128,128]{3,2,1,0:T(8,128)(2,1)} %get-tuple-element.53), channel_id=1, source_target_pairs={{0,4},{1,5},{2,6},{3,7},{4,0},{5,1},{6,2},{7,3},{8,12},{9,13},{10,... | collective-permute-start | bytes 1179656 | tf_op jit(solution)/shard_map/ppermute | solution.py:374
  42.4 5.6 %collective-permute-done.5.rest_1_ = bf16[2,6,128,128]{3,2,1,0:T(8,128)(2,1)S(1)} collective-permute-done((bf16[2,6,128,128]{3,2,1,0:T(8,128)(2,1)}, bf16[2,6,128,128]{3,2,1,0:T(8,128)(2,1)S(1)}, u32[]{:S(2)}, u32[]{:S(2)}) %collective-permute-start.5) | collective-permute-done | bytes 393248 | tf_op jit(solution)/shard_map/ppermute | solution.py:374
  48.2 1.9 %copy-done = bf16[768,2048]{1,0:T(8,128)(2,1)S(1)} copy-done((bf16[768,2048]{1,0:T(8,128)(2,1)S(1)}, bf16[768,2048]{1,0:T(8,128)(2,1)}, u32[]{:S(2)}) %copy-start) | copy-done | bytes 3145752
  50.1 6.5 %shard_map.125 = bf16[4,120,2176]{2,1,0:T(8,128)(2,1)} custom-call(s32[1]{0:T(128)} %bitcast.5.core_ref, bf16[384,1664]{1,0:T(8,128)(2,1)S(1)} %bitcast.12, bf16[24,1536]{1,0:T(8,128)(2,1)S(1)} %get-tuple-element.58.rows_trained, bf16[768,2048]{1,0:T(8,128)(2,1)S(1)} %copy-done, bf16[768,2048]{1,0:T(8,128)(2,1)} %collective-permute-done.3.weights_other, ...), custom_call_target="tpu_custom_call" | custom-call | tf_op jit(solution)/shard_map/pallas_call | solution.py:475
  57.8 3.6 %all-to-all-start.1 = ((bf16[4,120,2176]{2,1,0:T(8,128)(2,1)}), bf16[4,120,2176]{2,1,0:T(8,128)(2,1)S(1)}, u32[]{:S(2)}, u32[]{:S(2)}) async-start(bf16[4,120,2176]{2,1,0:T(8,128)(2,1)} %shard_map.125), calls=%async_computation.1 | async-start | bytes 4177920 | tf_op jit(solution)/shard_map/all_to_all | solution.py:573
  61.4 2.1 %collective-permute-start.11 = (bf16[6,128,128]{2,1,0:T(8,128)(2,1)S(1)}, bf16[6,128,128]{2,1,0:T(8,128)(2,1)S(1)}, u32[]{:S(2)}, u32[]{:S(2)}) collective-permute-start(bf16[6,128,128]{2,1,0:T(8,128)(2,1)S(1)} %shard_map.126), channel_id=1, source_target_pairs={{0,8},{1,9},{2,10},{3,11},{4,12},{5,13},{6,14},{7,15},{8,0},{9,1},... | collective-permute-start | bytes 589832 | tf_op jit(solution)/shard_map/ppermute | solution.py:374
  65.5 1.6 %shard_map.127 = (bf16[6,128,128]{2,1,0:T(8,128)(2,1)S(1)}, f32[6,128,128]{2,1,0:T(8,128)S(1)}, f32[6,128,128]{2,1,0:T(8,128)S(1)}) custom-call(s32[1]{0:T(128)} %bitcast.4.floor_ref.refs_0_, bf16[2,6,128,128]{3,2,1,0:T(8,128)(2,1)S(1)} %copy-done.1, bf16[2,6,128,128]{3,2,1,0:T(8,128)(2,1)S(1)} %collective-permute-done.5.rest_1_, ...), custom_call_target="tpu_custom_call" | custom-call | tf_op jit(solution)/shard_map/pallas_call | solution.py:522
  67.9 2.4 %collective-permute-start.12 = (bf16[6,128,128]{2,1,0:T(8,128)(2,1)S(1)}, bf16[6,128,128]{2,1,0:T(8,128)(2,1)S(1)}, u32[]{:S(2)}, u32[]{:S(2)}) collective-permute-start(bf16[6,128,128]{2,1,0:T(8,128)(2,1)S(1)} %shard_map.128), channel_id=1, source_target_pairs={{0,16},{1,17},{2,18},{3,19},{4,20},{5,21},{6,22},{7,23},{8,24},{9,... | collective-permute-start | bytes 589832 | tf_op jit(solution)/shard_map/ppermute | solution.py:374
  70.3 4.9 %collective-permute-done.10.rest_1_ = bf16[6,128,128]{2,1,0:T(8,128)(2,1)S(1)} collective-permute-done((bf16[6,128,128]{2,1,0:T(8,128)(2,1)S(1)}, bf16[6,128,128]{2,1,0:T(8,128)(2,1)S(1)}, u32[]{:S(2)}, u32[]{:S(2)}) %collective-permute-start.10) | collective-permute-done | bytes 196640 | tf_op jit(solution)/shard_map/ppermute | solution.py:374
  75.2 3.2 %collective-permute-done.12.rest_2_ = bf16[6,128,128]{2,1,0:T(8,128)(2,1)S(1)} collective-permute-done((bf16[6,128,128]{2,1,0:T(8,128)(2,1)S(1)}, bf16[6,128,128]{2,1,0:T(8,128)(2,1)S(1)}, u32[]{:S(2)}, u32[]{:S(2)}) %collective-permute-start.12) | collective-permute-done | bytes 196640 | tf_op jit(solution)/shard_map/ppermute | solution.py:374
  79.8 2.5 %collective-permute-start.14 = (bf16[6,128,128]{2,1,0:T(8,128)(2,1)S(1)}, bf16[6,128,128]{2,1,0:T(8,128)(2,1)S(1)}, u32[]{:S(2)}, u32[]{:S(2)}) collective-permute-start(bf16[6,128,128]{2,1,0:T(8,128)(2,1)S(1)} %get-tuple-element.71.refs_1_), channel_id=1, source_target_pairs={{0,8},{1,9},{2,10},{3,11},{4,12},{5,13},{6,14},{7,15},{8,0},{9,1},... | collective-permute-start | bytes 589832 | tf_op jit(solution)/shard_map/ppermute | solution.py:374
  82.2 5.8 %collective-permute-done.15.refs_3_ = bf16[6,128,128]{2,1,0:T(8,128)(2,1)S(1)} collective-permute-done((bf16[6,128,128]{2,1,0:T(8,128)(2,1)S(1)}, bf16[6,128,128]{2,1,0:T(8,128)(2,1)S(1)}, u32[]{:S(2)}, u32[]{:S(2)}) %collective-permute-start.15) | collective-permute-done | bytes 196640 | tf_op jit(solution)/shard_map/ppermute | solution.py:374
  89.4 2.1 %collective-permute-start.13 = (bf16[2,32,2048]{2,1,0:T(8,128)(2,1)S(1)}, bf16[2,32,2048]{2,1,0:T(8,128)(2,1)S(1)}, u32[]{:S(2)}, u32[]{:S(2)}) collective-permute-start(bf16[2,32,2048]{2,1,0:T(8,128)(2,1)S(1)} %get-tuple-element.68), channel_id=1, source_target_pairs={{0,8},{1,9},{2,10},{3,11},{4,12},{5,13},{6,14},{7,15},{8,0},{9,1},... | collective-permute-start | bytes 786440 | tf_op jit(solution)/shard_map/ppermute | solution.py:374
  92.0 3.0 %collective-permute-done.16.refs_4_ = bf16[6,128,128]{2,1,0:T(8,128)(2,1)S(1)} collective-permute-done((bf16[6,128,128]{2,1,0:T(8,128)(2,1)S(1)}, bf16[6,128,128]{2,1,0:T(8,128)(2,1)S(1)}, u32[]{:S(2)}, u32[]{:S(2)}) %collective-permute-start.16) | collective-permute-done | bytes 196640 | tf_op jit(solution)/shard_map/ppermute | solution.py:374
  99.1 2.1 %collective-permute-start.22 = (bf16[24,1536]{1,0:T(8,128)(2,1)S(1)}, bf16[24,1536]{1,0:T(8,128)(2,1)S(1)}, u32[]{:S(2)}, u32[]{:S(2)}) collective-permute-start(bf16[24,1536]{1,0:T(8,128)(2,1)S(1)} %get-tuple-element.80), channel_id=1, source_target_pairs={{0,2},{1,3},{2,0},{3,1},{4,6},{5,7},{6,4},{7,5},{8,10},{9,11},{10,... | collective-permute-start | bytes 221192 | tf_op jit(solution)/shard_map/ppermute | solution.py:374
  103.6 2.4 %collective-permute-done.23.refs_5_ = bf16[24,1536]{1,0:T(8,128)(2,1)S(1)} collective-permute-done((bf16[24,1536]{1,0:T(8,128)(2,1)S(1)}, bf16[24,1536]{1,0:T(8,128)(2,1)S(1)}, u32[]{:S(2)}, u32[]{:S(2)}) %collective-permute-start.23) | collective-permute-done | bytes 73760 | tf_op jit(solution)/shard_map/ppermute | solution.py:374
  106.0 1.5 %collective-permute-done.24.refs_6_ = bf16[24,1536]{1,0:T(8,128)(2,1)S(1)} collective-permute-done((bf16[24,1536]{1,0:T(8,128)(2,1)S(1)}, bf16[24,1536]{1,0:T(8,128)(2,1)S(1)}, u32[]{:S(2)}, u32[]{:S(2)}) %collective-permute-start.24) | collective-permute-done | bytes 73760 | tf_op jit(solution)/shard_map/ppermute | solution.py:374
  (71 shorter events, 17.5 us)
Async XLA Ops:
  0.6 4.0 %collective-permute-start.1 = (bf16[128,2048]{1,0:T(8,128)(2,1)}, bf16[128,2048]{1,0:T(8,128)(2,1)S(1)}, u32[]{:S(2)}, u32[]{:S(2)}) collective-permute-start(bf16[128,2048]{1,0:T(8,128)(2,1)} %cotangent_own.1), channel_id=1, source_target_pairs={{0,1},{1,0},{2,3},{3,2},{4,5},{5,4},{6,7},{7,6},{8,9},{9,8},{10,11... | collective-permute-start | bytes 1572872 | tf_op jit(solution)/shard_map/ppermute | solution.py:374
  4.6 16.9 %collective-permute-start.3 = (bf16[768,2048]{1,0:T(8,128)(2,1)}, bf16[768,2048]{1,0:T(8,128)(2,1)}, u32[]{:S(2)}, u32[]{:S(2)}) collective-permute-start(bf16[768,2048]{1,0:T(8,128)(2,1)} %weights.1), channel_id=1, source_target_pairs={{0,1},{1,0},{2,3},{3,2},{4,5},{5,4},{6,7},{7,6},{8,9},{9,8},{10,11... | collective-permute-start | bytes 9437192 | tf_op jit(solution)/shard_map/ppermute | solution.py:374
  5.1 42.9 %all-to-all-start = ((bf16[16,24,1664]{2,1,0:T(8,128)(2,1)}), bf16[16,24,1664]{2,1,0:T(8,128)(2,1)S(1)}, u32[]{:S(2)}, u32[]{:S(2)}) async-start(bf16[16,24,1664]{2,1,0:T(8,128)(2,1)} %bitcast.15), calls=%async_computation | async-start | bytes 2555904 | tf_op jit(solution)/shard_map/all_to_all | solution.py:425
  17.5 20.4 %collective-permute-start.2 = (bf16[2,6,128,128]{3,2,1,0:T(8,128)(2,1)}, bf16[2,6,128,128]{3,2,1,0:T(8,128)(2,1)S(1)}, u32[]{:S(2)}, u32[]{:S(2)}) collective-permute-start(bf16[2,6,128,128]{3,2,1,0:T(8,128)(2,1)} %get-tuple-element.47), channel_id=1, source_target_pairs={{0,2},{1,3},{2,0},{3,1},{4,6},{5,7},{6,4},{7,5},{8,10},{9,11},{10,... | collective-permute-start | bytes 1179656 | tf_op jit(solution)/shard_map/ppermute | solution.py:374
  19.5 18.5 %collective-permute-start.4 = (bf16[2,6,128,128]{3,2,1,0:T(8,128)(2,1)}, bf16[2,6,128,128]{3,2,1,0:T(8,128)(2,1)S(1)}, u32[]{:S(2)}, u32[]{:S(2)}) collective-permute-start(bf16[2,6,128,128]{3,2,1,0:T(8,128)(2,1)} %get-tuple-element.51), channel_id=1, source_target_pairs={{0,4},{1,5},{2,6},{3,7},{4,0},{5,1},{6,2},{7,3},{8,12},{9,13},{10,... | collective-permute-start | bytes 1179656 | tf_op jit(solution)/shard_map/ppermute | solution.py:374
  20.9 27.1 %collective-permute-start.5 = (bf16[2,6,128,128]{3,2,1,0:T(8,128)(2,1)}, bf16[2,6,128,128]{3,2,1,0:T(8,128)(2,1)S(1)}, u32[]{:S(2)}, u32[]{:S(2)}) collective-permute-start(bf16[2,6,128,128]{3,2,1,0:T(8,128)(2,1)} %get-tuple-element.55), channel_id=1, source_target_pairs={{0,2},{1,3},{2,0},{3,1},{4,6},{5,7},{6,4},{7,5},{8,10},{9,11},{10,... | collective-permute-start | bytes 1179656 | tf_op jit(solution)/shard_map/ppermute | solution.py:374
  21.5 26.6 %collective-permute-start.6 = (bf16[2,6,128,128]{3,2,1,0:T(8,128)(2,1)}, bf16[2,6,128,128]{3,2,1,0:T(8,128)(2,1)S(1)}, u32[]{:S(2)}, u32[]{:S(2)}) collective-permute-start(bf16[2,6,128,128]{3,2,1,0:T(8,128)(2,1)} %get-tuple-element.56), channel_id=1, source_target_pairs={{0,4},{1,5},{2,6},{3,7},{4,0},{5,1},{6,2},{7,3},{8,12},{9,13},{10,... | collective-permute-start | bytes 1179656 | tf_op jit(solution)/shard_map/ppermute | solution.py:374
  40.0 16.6 %collective-permute-start.8 = (bf16[2,6,128,128]{3,2,1,0:T(8,128)(2,1)}, bf16[2,6,128,128]{3,2,1,0:T(8,128)(2,1)S(1)}, u32[]{:S(2)}, u32[]{:S(2)}) collective-permute-start(bf16[2,6,128,128]{3,2,1,0:T(8,128)(2,1)} %get-tuple-element.53), channel_id=1, source_target_pairs={{0,4},{1,5},{2,6},{3,7},{4,0},{5,1},{6,2},{7,3},{8,12},{9,13},{10,... | collective-permute-start | bytes 1179656 | tf_op jit(solution)/shard_map/ppermute | solution.py:374
  41.5 15.1 %collective-permute-start.9 = (bf16[2,6,128,128]{3,2,1,0:T(8,128)(2,1)}, bf16[2,6,128,128]{3,2,1,0:T(8,128)(2,1)}, u32[]{:S(2)}, u32[]{:S(2)}) collective-permute-start(bf16[2,6,128,128]{3,2,1,0:T(8,128)(2,1)} %get-tuple-element.54), channel_id=1, source_target_pairs={{0,2},{1,3},{2,0},{3,1},{4,6},{5,7},{6,4},{7,5},{8,10},{9,11},{10,... | collective-permute-start | bytes 1179656 | tf_op jit(solution)/shard_map/ppermute | solution.py:374
  42.4 5.6 %collective-permute-start.7 = (f32[6,16]{1,0:T(8,128)S(1)}, f32[6,16]{1,0:T(8,128)S(1)}, u32[]{:S(2)}, u32[]{:S(2)}) collective-permute-start(f32[6,16]{1,0:T(8,128)S(1)} %copy-done.12), channel_id=1, source_target_pairs={{0,1},{1,0},{2,3},{3,2},{4,5},{5,4},{6,7},{7,6},{8,9},{9,8},{10,11... | collective-permute-start | bytes 1160 | tf_op jit(solution)/shard_map/ppermute | solution.py:374
  57.8 30.3 %all-to-all-start.1 = ((bf16[4,120,2176]{2,1,0:T(8,128)(2,1)}), bf16[4,120,2176]{2,1,0:T(8,128)(2,1)S(1)}, u32[]{:S(2)}, u32[]{:S(2)}) async-start(bf16[4,120,2176]{2,1,0:T(8,128)(2,1)} %shard_map.125), calls=%async_computation.1 | async-start | bytes 4177920 | tf_op jit(solution)/shard_map/all_to_all | solution.py:573
  61.4 6.5 %collective-permute-start.11 = (bf16[6,128,128]{2,1,0:T(8,128)(2,1)S(1)}, bf16[6,128,128]{2,1,0:T(8,128)(2,1)S(1)}, u32[]{:S(2)}, u32[]{:S(2)}) collective-permute-start(bf16[6,128,128]{2,1,0:T(8,128)(2,1)S(1)} %shard_map.126), channel_id=1, source_target_pairs={{0,8},{1,9},{2,10},{3,11},{4,12},{5,13},{6,14},{7,15},{8,0},{9,1},... | collective-permute-start | bytes 589832 | tf_op jit(solution)/shard_map/ppermute | solution.py:374
  67.2 8.0 %collective-permute-start.10 = (bf16[6,128,128]{2,1,0:T(8,128)(2,1)S(1)}, bf16[6,128,128]{2,1,0:T(8,128)(2,1)S(1)}, u32[]{:S(2)}, u32[]{:S(2)}) collective-permute-start(bf16[6,128,128]{2,1,0:T(8,128)(2,1)S(1)} %get-tuple-element.64), channel_id=1, source_target_pairs={{0,8},{1,9},{2,10},{3,11},{4,12},{5,13},{6,14},{7,15},{8,0},{9,1},... | collective-permute-start | bytes 589832 | tf_op jit(solution)/shard_map/ppermute | solution.py:374
  67.9 10.5 %collective-permute-start.12 = (bf16[6,128,128]{2,1,0:T(8,128)(2,1)S(1)}, bf16[6,128,128]{2,1,0:T(8,128)(2,1)S(1)}, u32[]{:S(2)}, u32[]{:S(2)}) collective-permute-start(bf16[6,128,128]{2,1,0:T(8,128)(2,1)S(1)} %shard_map.128), channel_id=1, source_target_pairs={{0,16},{1,17},{2,18},{3,19},{4,20},{5,21},{6,22},{7,23},{8,24},{9,... | collective-permute-start | bytes 589832 | tf_op jit(solution)/shard_map/ppermute | solution.py:374
  79.5 8.6 %collective-permute-start.15 = (bf16[6,128,128]{2,1,0:T(8,128)(2,1)S(1)}, bf16[6,128,128]{2,1,0:T(8,128)(2,1)S(1)}, u32[]{:S(2)}, u32[]{:S(2)}) collective-permute-start(bf16[6,128,128]{2,1,0:T(8,128)(2,1)S(1)} %get-tuple-element.71.refs_1_), channel_id=1, source_target_pairs={{0,16},{1,17},{2,18},{3,19},{4,20},{5,21},{6,22},{7,23},{8,24},{9,... | collective-permute-start | bytes 589832 | tf_op jit(solution)/shard_map/ppermute | solution.py:374
  79.8 11.7 %collective-permute-start.14 = (bf16[6,128,128]{2,1,0:T(8,128)(2,1)S(1)}, bf16[6,128,128]{2,1,0:T(8,128)(2,1)S(1)}, u32[]{:S(2)}, u32[]{:S(2)}) collective-permute-start(bf16[6,128,128]{2,1,0:T(8,128)(2,1)S(1)} %get-tuple-element.71.refs_1_), channel_id=1, source_target_pairs={{0,8},{1,9},{2,10},{3,11},{4,12},{5,13},{6,14},{7,15},{8,0},{9,1},... | collective-permute-start | bytes 589832 | tf_op jit(solution)/shard_map/ppermute | solution.py:374
  88.1 6.9 %collective-permute-start.16 = (bf16[6,128,128]{2,1,0:T(8,128)(2,1)S(1)}, bf16[6,128,128]{2,1,0:T(8,128)(2,1)S(1)}, u32[]{:S(2)}, u32[]{:S(2)}) collective-permute-start(bf16[6,128,128]{2,1,0:T(8,128)(2,1)S(1)} %collective-permute-done.15.refs_3_), channel_id=1, source_target_pairs={{0,8},{1,9},{2,10},{3,11},{4,12},{5,13},{6,14},{7,15},{8,0},{9,1},... | collective-permute-start | bytes 589832 | tf_op jit(solution)/shard_map/ppermute | solution.py:374
  89.4 8.5 %collective-permute-start.13 = (bf16[2,32,2048]{2,1,0:T(8,128)(2,1)S(1)}, bf16[2,32,2048]{2,1,0:T(8,128)(2,1)S(1)}, u32[]{:S(2)}, u32[]{:S(2)}) collective-permute-start(bf16[2,32,2048]{2,1,0:T(8,128)(2,1)S(1)} %get-tuple-element.68), channel_id=1, source_target_pairs={{0,8},{1,9},{2,10},{3,11},{4,12},{5,13},{6,14},{7,15},{8,0},{9,1},... | collective-permute-start | bytes 786440 | tf_op jit(solution)/shard_map/ppermute | solution.py:374
  91.5 3.6 %collective-permute-start.17 = (bf16[6,128,128]{2,1,0:T(8,128)(2,1)S(1)}, bf16[6,128,128]{2,1,0:T(8,128)(2,1)S(1)}, u32[]{:S(2)}, u32[]{:S(2)}) collective-permute-start(bf16[6,128,128]{2,1,0:T(8,128)(2,1)S(1)} %get-tuple-element.71.refs_1_), channel_id=1, source_target_pairs={{0,1},{1,0},{2,3},{3,2},{4,5},{5,4},{6,7},{7,6},{8,9},{9,8},{10,11... | collective-permute-start | bytes 589832 | tf_op jit(solution)/shard_map/ppermute | solution.py:374
  91.5 3.6 %collective-permute-start.18 = (bf16[6,128,128]{2,1,0:T(8,128)(2,1)S(1)}, bf16[6,128,128]{2,1,0:T(8,128)(2,1)S(1)}, u32[]{:S(2)}, u32[]{:S(2)}) collective-permute-start(bf16[6,128,128]{2,1,0:T(8,128)(2,1)S(1)} %collective-permute-done.14.refs_2_), channel_id=1, source_target_pairs={{0,1},{1,0},{2,3},{3,2},{4,5},{5,4},{6,7},{7,6},{8,9},{9,8},{10,11... | collective-permute-start | bytes 589832 | tf_op jit(solution)/shard_map/ppermute | solution.py:374
  97.9 9.6 %collective-permute-start.21 = (bf16[32,2048]{1,0:T(8,128)(2,1)S(1)}, bf16[32,2048]{1,0:T(8,128)(2,1)S(1)}, u32[]{:S(2)}, u32[]{:S(2)}) collective-permute-start(bf16[32,2048]{1,0:T(8,128)(2,1)S(1)} %get-tuple-element.79), channel_id=1, source_target_pairs={{0,16},{1,17},{2,18},{3,19},{4,20},{5,21},{6,22},{7,23},{8,24},{9,... | collective-permute-start | bytes 393224 | tf_op jit(solution)/shard_map/ppermute | solution.py:374
  99.1 4.4 %collective-permute-start.22 = (bf16[24,1536]{1,0:T(8,128)(2,1)S(1)}, bf16[24,1536]{1,0:T(8,128)(2,1)S(1)}, u32[]{:S(2)}, u32[]{:S(2)}) collective-permute-start(bf16[24,1536]{1,0:T(8,128)(2,1)S(1)} %get-tuple-element.80), channel_id=1, source_target_pairs={{0,2},{1,3},{2,0},{3,1},{4,6},{5,7},{6,4},{7,5},{8,10},{9,11},{10,... | collective-permute-start | bytes 221192 | tf_op jit(solution)/shard_map/ppermute | solution.py:374
  101.3 4.7 %collective-permute-start.23 = (bf16[24,1536]{1,0:T(8,128)(2,1)S(1)}, bf16[24,1536]{1,0:T(8,128)(2,1)S(1)}, u32[]{:S(2)}, u32[]{:S(2)}) collective-permute-start(bf16[24,1536]{1,0:T(8,128)(2,1)S(1)} %get-tuple-element.81), channel_id=1, source_target_pairs={{0,4},{1,5},{2,6},{3,7},{4,0},{5,1},{6,2},{7,3},{8,12},{9,13},{10,... | collective-permute-start | bytes 221192 | tf_op jit(solution)/shard_map/ppermute | solution.py:374
  102.2 5.3 %collective-permute-start.24 = (bf16[24,1536]{1,0:T(8,128)(2,1)S(1)}, bf16[24,1536]{1,0:T(8,128)(2,1)S(1)}, u32[]{:S(2)}, u32[]{:S(2)}) collective-permute-start(bf16[24,1536]{1,0:T(8,128)(2,1)S(1)} %get-tuple-element.82), channel_id=1, source_target_pairs={{0,6},{1,7},{2,4},{3,5},{4,2},{5,3},{6,0},{7,1},{8,14},{9,15},{10,... | collective-permute-start | bytes 221192 | tf_op jit(solution)/shard_map/ppermute | solution.py:374
  (16 other events, 119.4 us)
